TPU v7x, 32 devices: a whole 2x2x4 slice. The times are simulated.
32 devices in a mesh: dp: 4 (over x, core), seq: 8 (over z, y).
Axes of the slice: x: 2, y: 2, z: 4, core: 2. Of those that a mesh axis runs over, the one named last changes fastest.
Arguments:
- x_long: bfloat16 [4, 4, 4096, 768], P('dp', None, 'seq')
- x_short: bfloat16 [4, 8, 1, 512, 768], P('dp', 'seq')
- item_start: int32 [4, 4], P('dp'), may hold values from 0 to 7
- short_lengths: int32 [4, 8, 1], P('dp', 'seq'), may hold values from 128 to 512, as said below
- w_query: bfloat16 [768, 768], replicated, may hold values from -0.375 to 0.375
- w_key: bfloat16 [768, 768], replicated, may hold values from -0.375 to 0.375
- w_value: bfloat16 [768, 768], replicated, may hold values from -0.21875 to 0.21875
- w_out: bfloat16 [768, 768], replicated, may hold values from -0.4375 to 0.4375
- conv_taps: float32 [33, 12], replicated, may hold values from -2 to 2
- ln1_gain: float32 [768], replicated, may hold values from 0.25 to 1.75
- ln1_bias: float32 [768], replicated, may hold values from -3 to 3
- w_up: bfloat16 [768, 3072], replicated, may hold values from -0.21875 to 0.21875
- up_bias: float32 [3072], replicated, may hold values from -3 to 3
- w_down: bfloat16 [3072, 768], replicated, may hold values from -0.109375 to 0.109375
- down_bias: float32 [768], replicated, may hold values from -3 to 3
- ln2_gain: float32 [768], replicated, may hold values from 0.25 to 1.75
- ln2_bias: float32 [768], replicated, may hold values from -3 to 3
- cot_long: bfloat16 [4, 4, 4096, 768], P('dp', None, 'seq'), may hold values from -6 to 6
- cot_short: bfloat16 [4, 8, 1, 512, 768], P('dp', 'seq'), may hold values from -6 to 6
Outputs:
- out_long: bfloat16 [4, 4, 4096, 768], P('dp', None, 'seq')
- out_short: bfloat16 [4, 8, 1, 512, 768], P('dp', 'seq')
- grad_long: bfloat16 [4, 4, 4096, 768], P('dp', None, 'seq')
- grad_short: bfloat16 [4, 8, 1, 512, 768], P('dp', 'seq')
- grad_w_query: float32 [768, 768], P('seq')
- grad_w_key: float32 [768, 768], P('seq')
- grad_w_value: float32 [768, 768], P('seq')
- grad_w_out: float32 [768, 768], P('seq')
- grad_conv: float32 [33, 12], replicated
- grad_ln1_gain: float32 [768], replicated
- grad_ln1_bias: float32 [768], replicated
- grad_w_up: float32 [768, 3072], P('seq')
- grad_up_bias: float32 [3072], replicated
- grad_w_down: float32 [3072, 768], P('seq')
- grad_down_bias: float32 [768], replicated
- grad_ln2_gain: float32 [768], replicated
- grad_ln2_bias: float32 [768], replicated
Inputs may be any that keep to these rules, and one draw needn't show every extreme that they name: `short_lengths`: each short item's length is a multiple of 64, and some short item has length 512 in every draw.
All inputs are finite; a program needn't handle non-finite values.
Results may differ from a plain program's by a relative error of at most 0.02.
The roundings to bfloat16 on the way count: a program that leaves them out, or rounds other values in their place, can miss the bound.
Values may be sent and summed in bfloat16 or wider, within the bound.
No kernel may reach another device: no remote copies, remote signals or barrier semaphores. Data moves between devices by JAX's collectives and lax.ppermute only.
A program may use at most 448 MiB of HBM per device.

v0:
```python
import jax
import jax.numpy as jnp
from jax import lax
from jax.sharding import PartitionSpec as P

D = 768
H = 12
HD = 64
LM = 64
NS_STEPS = 6
HALF = 16
LONG = 4096


PRECISE = lax.Precision.HIGHEST
EPSILON = 1e-05
MASKED_SCORE = -1e30


def extended(cells, sides, width):
    for axis, dim in sides:
        count = lax.axis_size(axis)
        head = lax.slice_in_dim(cells, 0, width, axis=dim)
        tail = lax.slice_in_dim(cells, cells.shape[dim] - width, cells.shape[dim], axis=dim)
        cells = jnp.concatenate(
            [
                lax.ppermute(tail, axis, [(i, (i + 1) % count) for i in range(count)]),
                cells,
                lax.ppermute(head, axis, [((i + 1) % count, i) for i in range(count)]),
            ],
            axis=dim,
        )
    return cells


def merged(shard, axis, combine):
    everything = jax.tree.map(lambda part: lax.all_gather(part, axis), shard)
    initial = jax.tree.map(lambda part: part[0], everything)

    def turn(k, so_far):
        return combine(so_far, jax.tree.map(lambda part: part[k], everything))

    return lax.fori_loop(1, lax.axis_size(axis), turn, initial)


def layer_norm(values, gain, bias):
    center = values - jnp.mean(values, axis=-1, keepdims=True)
    spread = jnp.mean(center * center, axis=-1, keepdims=True)
    return center * lax.rsqrt(spread + EPSILON) * gain + bias


def newton_inverse(matrix):
    eye_mat = jnp.eye(matrix.shape[-1], dtype=matrix.dtype)
    col_most = jnp.max(jnp.sum(matrix, axis=-2), axis=-1)[..., None, None]
    row_most = jnp.max(jnp.sum(matrix, axis=-1), axis=-1)[..., None, None]
    approx = jnp.swapaxes(matrix, -1, -2) / (col_most * row_most)
    for rounds in range(NS_STEPS):
        product = jnp.einsum("...ij,...jk->...ik", matrix, approx, precision=PRECISE)
        nested = 7.0 * eye_mat - product
        nested = 15.0 * eye_mat - jnp.einsum(
            "...ij,...jk->...ik", product, nested, precision=PRECISE
        )
        nested = 13.0 * eye_mat - jnp.einsum(
            "...ij,...jk->...ik", product, nested, precision=PRECISE
        )
        approx = 0.25 * jnp.einsum("...ij,...jk->...ik", approx, nested, precision=PRECISE)
    return approx


def gelu_exact(values):
    return jax.nn.gelu(values, approximate=False)


def softmax_last(scores):
    return jax.nn.softmax(scores, axis=-1)


def combine_stats(former, latter):
    largest = jnp.maximum(former[0], latter[0])
    summed = former[1] * jnp.exp(former[0] - largest) + latter[1] * jnp.exp(latter[0] - largest)
    return (largest, summed)


def keep_pair(largest, summed):
    return (largest, summed)


def keep_one(values):
    return values


def linear(values, weight):
    return jnp.einsum("bnk,km->bnm", values, weight, preferred_element_type=jnp.float32)


def linear_back(upstream, weight):
    return jnp.einsum("bnm,km->bnk", upstream, weight, preferred_element_type=jnp.float32)


def weight_grad(values, upstream):
    return jnp.einsum("bnk,bnm->km", values, upstream, preferred_element_type=jnp.float32)


def conv_apply(padded, conv_taps, row_count):
    item_count = padded.shape[0]
    widened = padded.reshape(item_count, padded.shape[1], H, HD).astype(jnp.float32)
    result = jnp.zeros((item_count, row_count, H, HD), jnp.float32)
    for offset in range(2 * HALF + 1):
        result = (
            result
            + conv_taps[offset][None, None, :, None] * widened[:, offset : offset + row_count]
        )
    return result


def conv_back(upstream, padded_grad, padded, conv_taps, row_count):
    item_count = upstream.shape[0]
    up_heads = upstream.reshape(item_count, row_count, H, HD).astype(jnp.float32)
    wide_vals = padded.reshape(item_count, padded.shape[1], H, HD).astype(jnp.float32)
    wide_grad = padded_grad.reshape(item_count, padded_grad.shape[1], H, HD).astype(jnp.float32)
    tap_grads = []
    back_sum = jnp.zeros((item_count, row_count, H, HD), jnp.float32)
    for offset in range(2 * HALF + 1):
        tap_grads.append(
            jnp.sum(up_heads * wide_vals[:, offset : offset + row_count], axis=(0, 1, 3))
        )
        first_row = 2 * HALF - offset
        back_sum = (
            back_sum
            + conv_taps[offset][None, None, :, None]
            * wide_grad[:, first_row : first_row + row_count]
        )
    return (jnp.stack(tap_grads), back_sum)


def attend(query, key, lm_query, lm_key, padded, key_valid, conv_taps, merge_stats, sum_mix):
    item_count, row_count = (query.shape[0], query.shape[1])
    score_scale = HD ** (-0.5)
    q_heads = query.reshape(item_count, row_count, H, HD)
    k_heads = key.reshape(item_count, row_count, H, HD)
    v_heads = padded[:, HALF : HALF + row_count].reshape(item_count, row_count, H, HD)
    lq_heads = lm_query.reshape(item_count, LM, H, HD)
    lk_heads = lm_key.reshape(item_count, LM, H, HD)
    scores_f = score_scale * jnp.einsum(
        "bnhe,blhe->bhnl", q_heads, lk_heads, preferred_element_type=jnp.float32
    )
    probs_fb = softmax_last(scores_f).astype(jnp.bfloat16)
    scores_a = score_scale * jnp.einsum(
        "bmhe,blhe->bhml", lq_heads, lk_heads, preferred_element_type=jnp.float32
    )
    probs_a = softmax_last(scores_a)
    scores_b = score_scale * jnp.einsum(
        "blhe,bnhe->bhln", lq_heads, k_heads, preferred_element_type=jnp.float32
    )
    scores_b = jnp.where(key_valid[:, None, None, :], scores_b, MASKED_SCORE)
    local_max = jnp.max(scores_b, axis=-1)
    largest, summed = merge_stats(
        local_max, jnp.sum(jnp.exp(scores_b - local_max[..., None]), axis=-1)
    )
    probs_b = jnp.exp(scores_b - largest[..., None]) / summed[..., None]
    probs_bb = probs_b.astype(jnp.bfloat16)
    mixed = sum_mix(
        jnp.einsum("bhln,bnhe->bhle", probs_bb, v_heads, preferred_element_type=jnp.float32)
    )
    inverse = newton_inverse(probs_a)
    lm_out = jnp.einsum("bhlm,bhme->bhle", inverse, mixed, precision=PRECISE).astype(jnp.bfloat16)
    attended = jnp.einsum("bhnl,bhle->bnhe", probs_fb, lm_out, preferred_element_type=jnp.float32)
    conv_sum = conv_apply(padded, conv_taps, row_count)
    context = (attended + conv_sum).reshape(item_count, row_count, D).astype(jnp.bfloat16)
    return (
        context,
        (scores_f, probs_fb, scores_a, probs_a, probs_b, probs_bb, mixed, inverse, lm_out),
    )


def landmark_grad(kept, upstream):
    item_count, row_count = (upstream.shape[0], upstream.shape[1])
    up_heads = upstream.reshape(item_count, row_count, H, HD)
    return jnp.einsum("bhnl,bnhe->bhle", kept[1], up_heads, preferred_element_type=jnp.float32)


def attend_back(upstream, lm_grad, query, key, lm_query, lm_key, padded, kept, sum_dots):
    scores_f, probs_fb, scores_a, probs_a, probs_b, probs_bb, mixed, inverse, lm_out = kept
    item_count, row_count = (query.shape[0], query.shape[1])
    score_scale = HD ** (-0.5)
    q_heads = query.reshape(item_count, row_count, H, HD)
    k_heads = key.reshape(item_count, row_count, H, HD)
    v_heads = padded[:, HALF : HALF + row_count].reshape(item_count, row_count, H, HD)
    lq_heads = lm_query.reshape(item_count, LM, H, HD)
    lk_heads = lm_key.reshape(item_count, LM, H, HD)
    up_heads = upstream.reshape(item_count, row_count, H, HD)
    grad_pf = jnp.einsum("bnhe,bhle->bhnl", up_heads, lm_out, preferred_element_type=jnp.float32)
    grad_sf = jax.vjp(softmax_last, scores_f)[1](grad_pf)[0].astype(jnp.bfloat16)
    grad_inverse = jnp.einsum("bhle,bhme->bhlm", lm_grad, mixed, precision=PRECISE)
    grad_mixed = jnp.einsum("bhml,bhme->bhle", inverse, lm_grad, precision=PRECISE).astype(
        jnp.bfloat16
    )
    grad_pa = jax.vjp(newton_inverse, probs_a)[1](grad_inverse)[0]
    grad_sa = jax.vjp(softmax_last, scores_a)[1](grad_pa)[0]
    grad_pb = jnp.einsum("bhle,bnhe->bhln", grad_mixed, v_heads, preferred_element_type=jnp.float32)
    row_dots = sum_dots(jnp.sum(probs_b * grad_pb, axis=-1))
    grad_sb = (probs_b * (grad_pb - row_dots[..., None])).astype(jnp.bfloat16)
    grad_q = score_scale * jnp.einsum(
        "bhnl,blhe->bnhe", grad_sf, lk_heads, preferred_element_type=jnp.float32
    )
    grad_lk_part = score_scale * jnp.einsum(
        "bhnl,bnhe->blhe", grad_sf, q_heads, preferred_element_type=jnp.float32
    )
    grad_k = score_scale * jnp.einsum(
        "bhln,blhe->bnhe", grad_sb, lq_heads, preferred_element_type=jnp.float32
    )
    grad_lq_part = score_scale * jnp.einsum(
        "bhln,bnhe->blhe", grad_sb, k_heads, preferred_element_type=jnp.float32
    )
    grad_v = jnp.einsum("bhln,bhle->bnhe", probs_bb, grad_mixed, preferred_element_type=jnp.float32)
    grad_lq_own = score_scale * jnp.einsum(
        "bhml,blhe->bmhe", grad_sa, lk_heads.astype(jnp.float32), precision=PRECISE
    )
    grad_lk_own = score_scale * jnp.einsum(
        "bhml,bmhe->blhe", grad_sa, lq_heads.astype(jnp.float32), precision=PRECISE
    )
    return (grad_q, grad_k, grad_v, grad_lq_part, grad_lk_part, grad_lq_own, grad_lk_own)


def dense_forward(tokens, context, dense_params):
    w_out, ln1_gain, ln1_bias, w_up, up_bias, w_down, down_bias, ln2_gain, ln2_bias = dense_params
    residual = tokens.astype(jnp.float32) + linear(context, w_out)
    hidden = layer_norm(residual, ln1_gain, ln1_bias).astype(jnp.bfloat16)
    pre_act = linear(hidden, w_up) + up_bias
    active = gelu_exact(pre_act).astype(jnp.bfloat16)
    second = hidden.astype(jnp.float32) + linear(active, w_down) + down_bias
    final = layer_norm(second, ln2_gain, ln2_bias)
    return (final.astype(jnp.bfloat16), (residual, hidden, pre_act, active, second))


def dense_backward(cotangent, saved, context, dense_params):
    w_out, ln1_gain, ln1_bias, w_up, up_bias, w_down, down_bias, ln2_gain, ln2_bias = dense_params
    residual, hidden, pre_act, active, second = saved
    grad_second, grad_g2, grad_b2 = jax.vjp(layer_norm, second, ln2_gain, ln2_bias)[1](
        cotangent.astype(jnp.float32)
    )
    grad_branch = grad_second.astype(jnp.bfloat16)
    grad_down_b = jnp.sum(grad_branch.astype(jnp.float32), axis=(0, 1))
    grad_down_w = weight_grad(active, grad_branch)
    grad_active = linear_back(grad_branch, w_down)
    grad_pre = jax.vjp(gelu_exact, pre_act)[1](grad_active)[0].astype(jnp.bfloat16)
    grad_up_b = jnp.sum(grad_pre.astype(jnp.float32), axis=(0, 1))
    grad_up_w = weight_grad(hidden, grad_pre)
    grad_hidden = grad_second + linear_back(grad_pre, w_up)
    grad_resid, grad_g1, grad_b1 = jax.vjp(layer_norm, residual, ln1_gain, ln1_bias)[1](grad_hidden)
    grad_attn = grad_resid.astype(jnp.bfloat16)
    grad_out_w = weight_grad(context, grad_attn)
    grad_context = linear_back(grad_attn, w_out).astype(jnp.bfloat16)
    return (
        grad_resid,
        grad_context,
        (grad_out_w, grad_up_w, grad_down_w),
        (grad_g1, grad_b1, grad_up_b, grad_down_b, grad_g2, grad_b2),
    )


def body(
    x_long,
    x_short,
    item_start,
    short_lengths,
    w_query,
    w_key,
    w_value,
    w_out,
    conv_taps,
    ln1_gain,
    ln1_bias,
    w_up,
    up_bias,
    w_down,
    down_bias,
    ln2_gain,
    ln2_bias,
    cot_long,
    cot_short,
):
    long_tokens = x_long[0]
    short_tokens = x_short[0, 0]
    item_total = long_tokens.shape[0]
    long_rows = long_tokens.shape[1]
    short_rows = short_tokens.shape[1]
    seg_len = LONG // LM
    lm_local = long_rows // seg_len
    seq_count = lax.axis_size("seq")
    seq_index = lax.axis_index("seq")
    dense_params = (w_out, ln1_gain, ln1_bias, w_up, up_bias, w_down, down_bias, ln2_gain, ln2_bias)

    def project(tokens):
        return (
            linear(tokens, w_query).astype(jnp.bfloat16),
            linear(tokens, w_key).astype(jnp.bfloat16),
            linear(tokens, w_value).astype(jnp.bfloat16),
        )

    long_q, long_k, long_v = project(long_tokens)
    short_q, short_k, short_v = project(short_tokens)

    def segment_means(values):
        sums = jnp.sum(values.reshape(item_total, lm_local, seg_len, D), axis=2, dtype=jnp.float32)
        return (sums / seg_len).astype(jnp.bfloat16)

    lm_query, lm_key = (
        lax.all_gather(segment_means(long_q), "seq", axis=1, tiled=True),
        lax.all_gather(segment_means(long_k), "seq", axis=1, tiled=True),
    )
    place = (seq_index - item_start[0]) % seq_count
    left_open = place > 0
    right_open = place < seq_count - 1
    rim_rows = jnp.arange(long_rows + 2 * HALF)
    rim_keep = jnp.where(
        rim_rows[None, :] < HALF,
        left_open[:, None],
        jnp.where(rim_rows[None, :] >= HALF + long_rows, right_open[:, None], True),
    )
    zero_bf = jnp.zeros((), jnp.bfloat16)
    long_padded = jnp.where(rim_keep[:, :, None], extended(long_v, (("seq", 1),), HALF), zero_bf)
    lengths = short_lengths[0, 0]
    seg_short = lengths // LM
    positions = jnp.arange(short_rows, dtype=jnp.int32)
    short_valid = positions[None, :] < lengths[:, None]
    member = (
        positions[None, None, :] // seg_short[:, None, None]
        == jnp.arange(LM, dtype=jnp.int32)[None, :, None]
    ) & short_valid[:, None, :]
    counts = seg_short.astype(jnp.float32)

    def short_means(values):
        sums = jnp.einsum(
            "bln,bnd->bld", member.astype(jnp.bfloat16), values, preferred_element_type=jnp.float32
        )
        return (sums / counts[:, None, None]).astype(jnp.bfloat16)

    short_lq = short_means(short_q)
    short_lk = short_means(short_k)
    short_padded = jnp.pad(
        jnp.where(short_valid[:, :, None], short_v, zero_bf), ((0, 0), (HALF, HALF), (0, 0))
    )

    def merge_stats(largest, summed):
        return merged((largest, summed), "seq", combine_stats)

    def sum_mix(partial_mix):
        return lax.psum(partial_mix, "seq")

    long_context, long_kept = attend(
        long_q,
        long_k,
        lm_query,
        lm_key,
        long_padded,
        jnp.ones((item_total, long_rows), bool),
        conv_taps,
        merge_stats,
        sum_mix,
    )
    short_context, short_kept = attend(
        short_q,
        short_k,
        short_lq,
        short_lk,
        short_padded,
        short_valid,
        conv_taps,
        keep_pair,
        keep_one,
    )
    long_out, long_saved = dense_forward(long_tokens, long_context, dense_params)
    short_out, short_saved = dense_forward(short_tokens, short_context, dense_params)
    long_resid, long_ctx_grad, long_wgrads, long_small = dense_backward(
        cot_long[0], long_saved, long_context, dense_params
    )
    short_resid, short_ctx_grad, short_wgrads, short_small = dense_backward(
        cot_short[0, 0], short_saved, short_context, dense_params
    )
    long_grad_pad = jnp.where(
        rim_keep[:, :, None], extended(long_ctx_grad, (("seq", 1),), HALF), zero_bf
    )
    short_grad_pad = jnp.pad(short_ctx_grad, ((0, 0), (HALF, HALF), (0, 0)))
    long_taps_g, long_conv_v = conv_back(
        long_ctx_grad, long_grad_pad, long_padded, conv_taps, long_rows
    )
    short_taps_g, short_conv_v = conv_back(
        short_ctx_grad, short_grad_pad, short_padded, conv_taps, short_rows
    )
    long_lm_grad, taps_sum, g1_sum, b1_sum, bu_sum, bd_sum, g2_sum, b2_sum = lax.psum(
        (
            landmark_grad(long_kept, long_ctx_grad),
            long_taps_g + short_taps_g,
            long_small[0] + short_small[0],
            long_small[1] + short_small[1],
            long_small[2] + short_small[2],
            long_small[3] + short_small[3],
            long_small[4] + short_small[4],
            long_small[5] + short_small[5],
        ),
        "seq",
    )
    short_lm_grad = landmark_grad(short_kept, short_ctx_grad)

    def sum_dots(row_dots):
        return lax.psum(row_dots, "seq")

    lg_q, lg_k, lg_v, lq_part, lk_part, lq_own, lk_own = attend_back(
        long_ctx_grad,
        long_lm_grad,
        long_q,
        long_k,
        lm_query,
        lm_key,
        long_padded,
        long_kept,
        sum_dots,
    )
    lq_sum, lk_sum = (
        lax.psum_scatter(lq_part, "seq", scatter_dimension=1, tiled=True),
        lax.psum_scatter(lk_part, "seq", scatter_dimension=1, tiled=True),
    )
    lq_total = lq_sum + lax.dynamic_slice_in_dim(lq_own, seq_index * lm_local, lm_local, 1)
    lk_total = lk_sum + lax.dynamic_slice_in_dim(lk_own, seq_index * lm_local, lm_local, 1)

    def spread_long(totals):
        shares = jnp.broadcast_to(
            (totals / seg_len)[:, :, None], (item_total, lm_local, seg_len, H, HD)
        )
        return shares.reshape(item_total, long_rows, H, HD)

    long_gq = (lg_q + spread_long(lq_total)).reshape(item_total, long_rows, D).astype(jnp.bfloat16)
    long_gk = (lg_k + spread_long(lk_total)).reshape(item_total, long_rows, D).astype(jnp.bfloat16)
    long_gv = (lg_v + long_conv_v).reshape(item_total, long_rows, D).astype(jnp.bfloat16)
    sg_q, sg_k, sg_v, sq_part, sk_part, sq_own, sk_own = attend_back(
        short_ctx_grad,
        short_lm_grad,
        short_q,
        short_k,
        short_lq,
        short_lk,
        short_padded,
        short_kept,
        keep_one,
    )
    owner = jnp.minimum(positions[None, :] // seg_short[:, None], LM - 1)

    def spread_short(totals):
        shares = totals / counts[:, None, None, None]
        picked = jnp.take_along_axis(shares, owner[:, :, None, None], axis=1)
        return jnp.where(short_valid[:, :, None, None], picked, 0.0)

    short_items = short_tokens.shape[0]
    short_gq = (
        (sg_q + spread_short(sq_part + sq_own))
        .reshape(short_items, short_rows, D)
        .astype(jnp.bfloat16)
    )
    short_gk = (
        (sg_k + spread_short(sk_part + sk_own))
        .reshape(short_items, short_rows, D)
        .astype(jnp.bfloat16)
    )
    short_gv = (
        (sg_v + short_valid[:, :, None, None] * short_conv_v)
        .reshape(short_items, short_rows, D)
        .astype(jnp.bfloat16)
    )

    def input_grad(resid_grad, grad_q, grad_k, grad_v):
        return (
            resid_grad
            + linear_back(grad_q, w_query)
            + linear_back(grad_k, w_key)
            + linear_back(grad_v, w_value)
        ).astype(jnp.bfloat16)

    grad_long = input_grad(long_resid, long_gq, long_gk, long_gv)
    grad_short = input_grad(short_resid, short_gq, short_gk, short_gv)
    gw_query = weight_grad(long_tokens, long_gq) + weight_grad(short_tokens, short_gq)
    gw_key = weight_grad(long_tokens, long_gk) + weight_grad(short_tokens, short_gk)
    gw_value = weight_grad(long_tokens, long_gv) + weight_grad(short_tokens, short_gv)
    gw_out = long_wgrads[0] + short_wgrads[0]
    gw_up = long_wgrads[1] + short_wgrads[1]
    gw_down = long_wgrads[2] + short_wgrads[2]
    pieces = (
        lax.psum_scatter(gw_query, "seq", scatter_dimension=0, tiled=True),
        lax.psum_scatter(gw_key, "seq", scatter_dimension=0, tiled=True),
        lax.psum_scatter(gw_value, "seq", scatter_dimension=0, tiled=True),
        lax.psum_scatter(gw_out, "seq", scatter_dimension=0, tiled=True),
        lax.psum_scatter(gw_up, "seq", scatter_dimension=0, tiled=True),
        lax.psum_scatter(gw_down, "seq", scatter_dimension=0, tiled=True),
    )
    summed = lax.psum(
        (
            pieces[0],
            pieces[1],
            pieces[2],
            pieces[3],
            pieces[4],
            pieces[5],
            taps_sum,
            g1_sum,
            b1_sum,
            bu_sum,
            bd_sum,
            g2_sum,
            b2_sum,
        ),
        "dp",
    )
    big_out = summed[:6]
    small_out = summed[6:]
    return (
        long_out[None],
        short_out[None, None],
        grad_long[None],
        grad_short[None, None],
        big_out[0],
        big_out[1],
        big_out[2],
        big_out[3],
        small_out[0],
        small_out[1],
        small_out[2],
        big_out[4],
        small_out[3],
        big_out[5],
        small_out[4],
        small_out[5],
        small_out[6],
    )


def solution(mesh):
    placed = (
        P("dp", None, "seq", None),
        P("dp", "seq", None, None, None),
        P("dp", None),
        P("dp", "seq", None),
        P(),
        P(),
        P(),
        P(),
        P(),
        P(),
        P(),
        P(),
        P(),
        P(),
        P(),
        P(),
        P(),
        P("dp", None, "seq", None),
        P("dp", "seq", None, None, None),
    )
    return jax.shard_map(
        body,
        mesh=mesh,
        in_specs=placed,
        out_specs=(
            P("dp", None, "seq", None),
            P("dp", "seq", None, None, None),
            P("dp", None, "seq", None),
            P("dp", "seq", None, None, None),
            P("seq", None),
            P("seq", None),
            P("seq", None),
            P("seq", None),
            P(),
            P(),
            P(),
            P("seq", None),
            P(),
            P("seq", None),
            P(),
            P(),
            P(),
        ),
        check_vma=False,
    )
```

profile of v0, /device:TPU:0, one launch (start us, length us, event | category | flops | bytes accessed | tf_op | source)
XLA Modules:
  0.0 2260.7 jit_solution(12590160166267715639)
XLA Ops:
  57.4 33.0 %all_gather.18 = bf16[4,64,768]{2,1,0:T(8,128)(2,1)} all-gather(bf16[4,8,768]{2,1,0:T(8,128)(2,1)S(1)} %multiply_convert_fusion.7), channel_id=1, replica_groups=mesh['dp'=4,'seq'=8] {'seq'}, dimensions={1}, use_global_device_ids=true | all-gather | bytes 442368 | tf_op jit(solution)/shard_map/all_gather | solution.py:309
  92.1 33.0 %all_gather.19 = bf16[4,64,768]{2,1,0:T(8,128)(2,1)} all-gather(bf16[4,8,768]{2,1,0:T(8,128)(2,1)S(1)} %multiply_convert_fusion.6), channel_id=1, replica_groups=mesh['dp'=4,'seq'=8] {'seq'}, dimensions={1}, use_global_device_ids=true | all-gather | bytes 442368 | tf_op jit(solution)/shard_map/all_gather | solution.py:310
  173.4 15.9 fusion.214
  191.2 19.8 multiply_convert_fusion.3
  222.1 9.6 convert_reduce_fusion.5
  287.4 8.8 multiply_reduce_fusion.27
  296.2 9.3 multiply_reduce_fusion.9
  385.4 30.9 %all-gather = f32[32,12,64]{2,1,0:T(8,128)S(1)} all-gather(f32[4,12,64]{2,1,0:T(8,128)S(1)} %get-tuple-element.402), channel_id=2, replica_groups=mesh['dp'=4,'seq'=8] {'seq'}, dimensions={0}, use_global_device_ids=true | all-gather | bytes 110592 | tf_op jit(solution)/shard_map/all_gather | solution.py:37
  417.9 30.7 %all-gather.1 = f32[32,12,64]{2,1,0:T(8,128)S(1)} all-gather(f32[4,12,64]{2,1,0:T(8,128)S(1)} %exponential_reduce_fusion), channel_id=3, replica_groups=mesh['dp'=4,'seq'=8] {'seq'}, dimensions={0}, use_global_device_ids=true | all-gather | bytes 110592 | tf_op jit(solution)/shard_map/all_gather | solution.py:37
  525.8 42.9 %fusion.180 = bf16[1,512,12,64]{1,3,2,0:T(8,128)(2,1)S(1)} fusion(f32[1,544,12,64]{1,3,2,0:T(8,128)} %bitcast.1054, bf16[12,64,64]{2,1,0:T(8,128)(2,1)} %convolution_convert_fusion.7, f32[512]{0:T(512)} %get-tuple-element.449, f32[12]{0:T(128)} %get-tuple-element.319, f32[12]{0:T(128)} %get-tuple-element.320, f32[12]{0:T(128)} %get-tuple-element.289, ...), kind=kOutput, calls=%fused_computation.309 | convolution fusion | flops 77856768 | bytes 54368816 | tf_op jit(solution)/shard_map/bhln,bhle->bnhe/dot_general | solution.py:215
  614.8 71.7 %all-reduce.9.cloned.1.call-done = f32[4,12,64,64]{3,2,1,0:T(8,128)} async-done(((f32[4,12,64,64]{3,2,1,0:T(8,128)}), f32[4,12,64,64]{3,2,1,0:T(8,128)}) %all-reduce.9.cloned.1.call-update) | async-done | bytes 786448 | tf_op jit(solution)/shard_map/psum | solution.py:349
  689.8 111.2 %fusion.87 = bf16[4,512,12,64]{1,3,2,0:T(8,128)(2,1)} fusion(f32[4,544,12,64]{1,3,2,0:T(8,128)} %fusion.105, f32[12]{0:T(128)} %get-tuple-element.319, f32[12]{0:T(128)} %get-tuple-element.320, f32[12]{0:T(128)} %get-tuple-element.289, f32[12]{0:T(128)} %get-tuple-element.290, f32[12]{0:T(128)} %get-tuple-element.291, f32[12]{0:T(128)} %get-tuple-element.292, ...), kind=kOutput, calls=%fused_computation.186 | convolution fusion | flops 306708480 | bytes 214304304 | tf_op jit(solution)/shard_map/bhnl,bhle->bnhe/dot_general | solution.py:167
  811.0 25.8 %fusion.94 = (u8[512,3072]{1,0:T(8,128)(4,1)}, u8[512,3072]{1,0:T(8,128)(4,1)}, f32[4,512,3072]{2,1,0:T(8,128)}) fusion(f32[3072]{0:T(1024)S(1)} %copy-done.298, bf16[4,512,768]{2,1,0:T(8,128)(2,1)} %add_convert_fusion.4, bf16[768,3072]{1,0:T(8,128)(2,1)} %param.34), kind=kOutput, calls=%fused_computation.222 | convolution fusion | flops 9748611072 | bytes 36188160 | tf_op jit(solution)/shard_map/bnk,km->bnm/dot_general | solution.py:93
  836.9 61.4 %multiply_convert_fusion = (bf16[4,512,3072]{2,1,0:T(8,128)(2,1)S(1)}, f32[4,512,3072]{2,1,0:T(8,128)}) fusion(f32[4,512,3072]{2,1,0:T(8,128)} %get-tuple-element.408, f32[3072]{0:T(1024)S(1)} %copy-done.298, u8[512,3072]{1,0:T(8,128)(4,1)} %get-tuple-element.205, u8[512,3072]{1,0:T(8,128)(4,1)} %get-tuple-element.204), kind=kLoop, calls=%fused_computation.52 | loop fusion | flops 446693376 | bytes 66072576 | tf_op jit(solution)/shard_map/convert_element_type | solution.py:230
  898.4 16.5 fusion.486
  926.0 32.9 %convert_reduce_fusion = (f32[3072]{0:T(1024)S(1)}, bf16[4,512,3072]{2,1,0:T(8,128)(2,1)}) fusion(f32[4,512,3072]{2,1,0:T(8,128)} %get-tuple-element.381, bf16[4,512,768]{2,1,0:T(8,128)(2,1)} %get-tuple-element.363, bf16[3072,768]{1,0:T(8,128)(2,1)} %param.36, f32[4,512,3072]{2,1,0:T(8,128)} %get-tuple-element.408, f32[3072]{0:T(1024)S(1)} %copy-done.298), kind=kOutput, calls=%fused_computation.50 | convolution fusion | flops 9770628096 | bytes 70803456 | tf_op jit(solution)/shard_map/bnm,km->bnk/dot_general | solution.py:97
  958.9 20.1 multiply_reduce_fusion
  999.4 47.7 %fusion.49 = (f32[12]{0:T(128)S(1)}, f32[12]{0:T(128)S(1)}, f32[12]{0:T(128)S(1)}, f32[12]{0:T(128)S(1)}, f32[12]{0:T(128)S(1)}, /*index=5*/f32[12]{0:T(128)S(1)...) fusion(bf16[4,512,12,64]{1,3,2,0:T(8,128)(2,1)} %bitcast.1009, ...), kind=kLoop, calls=%fused_computation.110 | loop fusion | flops 48758604 | bytes 97518288 | tf_op jit(solution)/shard_map/reduce_sum | solution.py:125
  1047.1 60.1 %fusion.50 = (f32[12]{0:T(128)S(1)}, f32[12]{0:T(128)S(1)}, f32[12]{0:T(128)S(1)}, f32[12]{0:T(128)S(1)}, f32[12]{0:T(128)S(1)}, /*index=5*/f32[12]{0:T(128)S(1)...) fusion(bf16[4,512,12,64]{1,3,2,0:T(8,128)(2,1)} %bitcast.1010, ...), kind=kLoop, calls=%fused_computation.111 | loop fusion | flops 58195752 | bytes 116392800 | tf_op jit(solution)/shard_map/reduce_sum | solution.py:125
  1136.7 59.9 %all-reduce.11.cloned.1.call-done = f32[4,12,64,64]{3,2,1,0:T(8,128)} async-done(((f32[4,12,64,64]{3,2,1,0:T(8,128)}), f32[4,12,64,64]{3,2,1,0:T(8,128)}) %all-reduce.11.cloned.1.call-update) | async-done | bytes 786448 | tf_op jit(solution)/shard_map/psum | solution.py:391
  1324.0 110.3 %fusion.53 = bf16[4,512,12,64]{1,3,2,0:T(8,128)(2,1)} fusion(f32[4,544,12,64]{1,3,2,0:T(8,128)} %fusion.106, f32[12]{0:T(128)} %get-tuple-element.319, f32[12]{0:T(128)} %get-tuple-element.320, f32[12]{0:T(128)} %get-tuple-element.289, f32[12]{0:T(128)} %get-tuple-element.290, f32[12]{0:T(128)} %get-tuple-element.291, f32[12]{0:T(128)} %get-tuple-element.292, ...), kind=kOutput, calls=%fused_computation.115 | convolution fusion | flops 312999936 | bytes 217474608 | tf_op jit(solution)/shard_map/bhln,bhle->bnhe/dot_general | solution.py:215
  1434.3 37.0 %all-reduce.2 = (f32[4,12,64]{2,1,0:T(8,128)S(1)}, f32[33,12]{0,1:T(8,128)}, f32[768]{0:T(1024)}, f32[768]{0:T(1024)}, f32[3072]{0:T(1024)S(1)}, /*index=5*/f32[768]{0:T(1024)}, f32[768]{0:T(1024)}, f32[768]{0:T(1024)}) all-reduce(f32[4,12,64]{2,1,0:T(8,128)S(1)} %get-tuple-element.429, ...), channel_id=1, replica_groups=mesh['dp'=4,'seq'=8] {'seq'}, use_global_device_ids=true, to_apply=%region_40.41 | all-reduce | flops 10380 | bytes 83040 | tf_op jit(solution)/shard_map/psum | solution.py:407
  1542.1 11.5 reshape.1826
  1590.4 11.7 reshape.1825
  1629.9 15.8 bitcast_add_fusion.1
  1651.7 15.5 bitcast_add_fusion
  1673.3 12.1 all-reduce.3
  1696.6 61.7 %reduce-scatter.25.cloned.1.call-done = f32[96,768]{1,0:T(8,128)} async-done(((f32[768,768]{1,0:T(8,128)}), f32[96,768]{1,0:T(8,128)}) %reduce-scatter.25.cloned.1.call-update) | async-done | bytes 294928
  1760.2 70.3 %reduce-scatter.19.cloned.1.call-done = f32[96,768]{1,0:T(8,128)} async-done(((f32[768,768]{1,0:T(8,128)}), f32[96,768]{1,0:T(8,128)}) %reduce-scatter.19.cloned.1.call-update) | async-done | bytes 294928 | tf_op jit(solution)/shard_map/reduce_scatter | solution.py:491
  1830.5 166.0 %reduce-scatter.21.cloned.1.call-done = f32[96,3072]{1,0:T(8,128)} async-done(((f32[768,3072]{1,0:T(8,128)}), f32[96,3072]{1,0:T(8,128)}) %reduce-scatter.21.cloned.1.call-update) | async-done | bytes 1179664 | tf_op jit(solution)/shard_map/reduce_scatter | solution.py:492
  1996.5 165.9 %reduce-scatter.23.cloned.1.call-done = f32[384,768]{1,0:T(8,128)} async-done(((f32[3072,768]{1,0:T(8,128)}), f32[384,768]{1,0:T(8,128)}) %reduce-scatter.23.cloned.1.call-update) | async-done | bytes 1179664 | tf_op jit(solution)/shard_map/reduce_scatter | solution.py:493
  2177.7 67.7 %all-reduce.13.cloned.1.call-done = (f32[96,768]{0,1:T(8,128)}, f32[96,768]{0,1:T(8,128)}, f32[96,768]{0,1:T(8,128)}, f32[96,768]{1,0:T(8,128)}, f32[96,3072]{1,0:T(8,128)}, /*index=5*/f32[384,768]{1,0:T(8,128)}) async-done(((f32[96,768]{0,1:T(8,128)}, f32[96,768]{0,1:T(8,128)}, f32[96,768]{0,1:T(8,128)}, f32[96,768]{1,0:T(8,128)}, f32[96,3072]{1,0:T(8,128)}, /*index=5*/f32[384,768]{1,0:T(8,128)}), ...) | async-done | bytes 3538960 | tf_op jit(solution)/shard_map/psum | solution.py:495
  (1207 shorter events, 753.3 us)
Async XLA Ops:
  7.2 679.2 %all-reduce.9.cloned.1.call-start = ((), (), s32[]{:S(2)}) async-start(), calls=%async_computation.8 | async-start | bytes 3145728 | tf_op jit(solution)/shard_map/psum | solution.py:349
  13.0 572.1 %collective-permute-start = (bf16[4,16,768]{2,1,0:T(8,128)(2,1)}, bf16[4,16,768]{2,1,0:T(8,128)(2,1)}, u32[]{:S(2)}, u32[]{:S(2)}) collective-permute-start(bf16[4,16,768]{2,1,0:T(8,128)(2,1)} %get-tuple-element.387), channel_id=1, source_target_pairs={{0,1},{1,2},{2,3},{3,4},{4,5},{5,6},{6,7},{7,0},{8,9},{9,10},{10,1... | collective-permute-start | bytes 294920 | tf_op jit(solution)/shard_map/ppermute | solution.py:27
  16.0 569.1 %collective-permute-start.1 = (bf16[4,16,768]{2,1,0:T(8,128)(2,1)}, bf16[4,16,768]{2,1,0:T(8,128)(2,1)}, u32[]{:S(2)}, u32[]{:S(2)}) collective-permute-start(bf16[4,16,768]{2,1,0:T(8,128)(2,1)} %get-tuple-element.388), channel_id=1, source_target_pairs={{1,0},{2,1},{3,2},{4,3},{5,4},{6,5},{7,6},{0,7},{9,8},{10,9},{11,1... | collective-permute-start | bytes 294920 | tf_op jit(solution)/shard_map/ppermute | solution.py:29
  24.1 442.3 %copy-start.31 = (f32[64,64]{1,0:T(8,128)}, f32[64,64]{1,0:T(8,128)S(1)}, u32[]{:S(2)}) copy-start(f32[64,64]{1,0:T(8,128)S(1)} %get-tuple-element.446) | copy-start | bytes 49156
  24.7 138.4 %copy-start.323 = (pred[512]{0:T(512)(128)(4,1)}, pred[512]{0:T(512)(128)(4,1)S(1)}, u32[]{:S(2)}) copy-start(pred[512]{0:T(512)(128)(4,1)S(1)} %get-tuple-element.448) | copy-start | bytes 1540
  29.5 135.4 %copy-start.87 = (bf16[512,768]{0,1:T(8,128)(2,1)}, bf16[512,768]{0,1:T(8,128)(2,1)S(1)}, u32[]{:S(2)}) copy-start(bf16[512,768]{0,1:T(8,128)(2,1)S(1)} %copy.367) | copy-start | bytes 2359300
  34.1 130.8 %copy-start.166 = (bf16[64,768]{0,1:T(8,128)(2,1)}, bf16[64,768]{0,1:T(8,128)(2,1)S(1)}, u32[]{:S(2)}) copy-start(bf16[64,768]{0,1:T(8,128)(2,1)S(1)} %copy.634) | copy-start | bytes 294916
  166.7 74.8 %copy-start.234 = (f32[12,512]{1,0:T(8,128)}, f32[12,512]{1,0:T(8,128)S(1)}, u32[]{:S(2)}) copy-start(f32[12,512]{1,0:T(8,128)S(1)} %get-tuple-element.415) | copy-start | bytes 73732
  306.2 302.0 %copy-start.241 = (pred[4,544]{1,0:T(4,128)(4,1)}, pred[4,544]{1,0:T(4,128)(4,1)S(1)}, u32[]{:S(2)}) copy-start(pred[4,544]{1,0:T(4,128)(4,1)S(1)} %select_select_fusion) | copy-start | bytes 6532
  369.3 231.4 %copy-start.28 = (f32[4,12,64,64]{3,2,1,0:T(8,128)}, f32[4,12,64,64]{3,2,1,0:T(8,128)S(1)}, u32[]{:S(2)}) copy-start(f32[4,12,64,64]{3,2,1,0:T(8,128)S(1)} %convolution_multiply_fusion.4) | copy-start | bytes 2359300
  449.5 142.9 %copy-start.186 = (f32[4,12,64]{2,1,0:T(8,128)}, f32[4,12,64]{2,1,0:T(8,128)S(1)}, u32[]{:S(2)}) copy-start(f32[4,12,64]{2,1,0:T(8,128)S(1)} %get-tuple-element.151) | copy-start | bytes 36868
  449.5 142.9 %copy-start.188 = (f32[4,12,64]{2,1,0:T(8,128)}, f32[4,12,64]{2,1,0:T(8,128)S(1)}, u32[]{:S(2)}) copy-start(f32[4,12,64]{2,1,0:T(8,128)S(1)} %get-tuple-element.152) | copy-start | bytes 36868
  598.6 598.0 %all-reduce.11.cloned.1.call-start = ((), (), s32[]{:S(2)}) async-start(), calls=%async_computation.9 | async-start | bytes 3145728 | tf_op jit(solution)/shard_map/psum | solution.py:391
  608.2 78.3 %copy-start.75 = (f32[4,12,64,64]{3,2,1,0:T(8,128)S(1)}, f32[4,12,64,64]{3,2,1,0:T(8,128)}, u32[]{:S(2)}) copy-start(f32[4,12,64,64]{3,2,1,0:T(8,128)} %convolution_multiply_fusion.3) | copy-start | bytes 2359300
  689.7 111.2 %copy-start.131 = (bf16[4,12,64,64]{3,2,1,0:T(8,128)(2,1)}, bf16[4,12,64,64]{3,2,1,0:T(8,128)(2,1)S(1)}, u32[]{:S(2)}) copy-start(bf16[4,12,64,64]{3,2,1,0:T(8,128)(2,1)S(1)} %convolution_convert_fusion.6) | copy-start | bytes 1179652
  689.7 111.2 %copy-start.347 = (bf16[1,4,512,768]{3,2,1,0:T(8,128)(2,1)S(1)}, bf16[1,4,512,768]{3,2,1,0:T(8,128)(2,1)}, u32[]{:S(2)}) copy-start(bf16[1,4,512,768]{3,2,1,0:T(8,128)(2,1)} %param.23) | copy-start | bytes 9437188
  689.7 111.2 %copy-start.352 = (bf16[768,768]{1,0:T(8,128)(2,1)S(1)}, bf16[768,768]{1,0:T(8,128)(2,1)}, u32[]{:S(2)}) copy-start(bf16[768,768]{1,0:T(8,128)(2,1)} %param.30) | copy-start | bytes 3538948
  836.8 61.5 %copy-start.356 = (f32[768]{0:T(1024)S(1)}, f32[768]{0:T(1024)}, u32[]{:S(2)}) copy-start(f32[768]{0:T(1024)} %param.37) | copy-start | bytes 9220
  1107.2 423.5 %reduce-scatter.17.cloned.1.call-start = ((), (), s32[]{:S(2)}) async-start(), calls=%async_computation.11 | async-start | bytes 1769472 | tf_op jit(solution)/shard_map/reduce_scatter | solution.py:422
  1107.3 22.6 collective-permute-start.2
  1108.8 20.7 collective-permute-start.3
  1129.4 452.4 %reduce-scatter.15.cloned.1.call-start = ((), (), s32[]{:S(2)}) async-start(), calls=%async_computation.10 | async-start | bytes 1769472 | tf_op jit(solution)/shard_map/reduce_scatter | solution.py:421
  1136.6 64.4 %copy-start.74 = (f32[4,12,64,64]{3,2,1,0:T(8,128)S(1)}, f32[4,12,64,64]{3,2,1,0:T(8,128)}, u32[]{:S(2)}) copy-start(f32[4,12,64,64]{3,2,1,0:T(8,128)} %convolution_subtract_fusion) | copy-start | bytes 2359300
  1324.0 110.3 %copy-start.294 = (f32[768]{0:T(1024)S(1)}, f32[768]{0:T(1024)}, u32[]{:S(2)}) copy-start(f32[768]{0:T(1024)} %add.969) | copy-start | bytes 9220
  1481.2 211.5 %reduce-scatter.29.cloned.1.call-start = ((), (), s32[]{:S(2)}) async-start(), calls=%async_computation.17 | async-start | bytes 2654208
  1505.6 189.2 %reduce-scatter.27.cloned.1.call-start = ((), (), s32[]{:S(2)}) async-start(), calls=%async_computation.16 | async-start | bytes 2654208
  1564.8 193.5 %reduce-scatter.25.cloned.1.call-start = ((), (), s32[]{:S(2)}) async-start(), calls=%async_computation.15 | async-start | bytes 2654208
  1613.2 217.3 %reduce-scatter.19.cloned.1.call-start = ((), (), s32[]{:S(2)}) async-start(), calls=%async_computation.12 | async-start | bytes 2654208 | tf_op jit(solution)/shard_map/reduce_scatter | solution.py:491
  1623.8 372.7 %reduce-scatter.21.cloned.1.call-start = ((), (), s32[]{:S(2)}) async-start(), calls=%async_computation.13 | async-start | bytes 10616832 | tf_op jit(solution)/shard_map/reduce_scatter | solution.py:492
  1645.7 516.7 %reduce-scatter.23.cloned.1.call-start = ((), (), s32[]{:S(2)}) async-start(), calls=%async_computation.14 | async-start | bytes 10616832 | tf_op jit(solution)/shard_map/reduce_scatter | solution.py:493
  1667.3 578.2 %all-reduce.13.cloned.1.call-start = ((), (), s32[]{:S(2)}) async-start(), calls=%async_computation.18 | async-start | bytes 7667712 | tf_op jit(solution)/shard_map/psum | solution.py:495
  1692.7 478.2 %slice-start.4 = ((s8[6291456]{0:T(1024)(128)(4,1)}), s8[2097152]{0:T(1024)(128)(4,1)S(1)}, s32[]{:S(2)}) async-start(s8[6291456]{0:T(1024)(128)(4,1)} %bitcast.1027), calls=%async_computation.23 | async-start | bytes 4194304
  (358 other events, 1571.2 us)
Sparse Core Ops, SparseCore 0:
  598.7 87.7 all-reduce.8
  1107.3 89.1 all-reduce.10
  1200.0 64.9 reduce-scatter.16
  1481.3 62.7 reduce-scatter.14
  1547.5 67.8 reduce-scatter.28
  1618.7 68.0 reduce-scatter.26
  1690.3 68.0 reduce-scatter.24
  1762.4 68.0 reduce-scatter.18
  1834.1 162.3 reduce-scatter.20
  2000.0 162.3 reduce-scatter.22
  2165.8 79.6 all-reduce.12
where the time goes:
time: 2280 us; the launch traced here: 2260 us
  matrix products  898 us (39%)
  waiting for transfers between devices  663 us (29%)
  other arithmetic  274 us (12%)
  local copies, waits for them, and re-layouts  215 us (9%)
  blocking collectives  177 us (8%)
    reduce_scatter x1, waiting for transfers between devices, body(): lax.psum_scatter(gw_up, 'seq', scatter_dimension=0, tiled=True)  166 us
    reduce_scatter x1, waiting for transfers between devices, body(): lax.psum_scatter(gw_down, 'seq', scatter_dimension=0, tiled=True)  166 us
    dot_general x2, matrix products, attend_back(): jnp.einsum('bhln,bhle->bnhe', probs_bb, grad_mixed, preferred_element_typ...  153 us
    dot_general x2, matrix products, attend(): jnp.einsum('bhnl,bhle->bnhe', probs_fb, lm_out, preferred_element_type=jn...  127 us
    reduce_sum x4, other arithmetic, conv_back(): jnp.sum(up_heads * wide_vals[:, offset:offset + row_count], axis=(0, 1, 3))  126 us
    dot_general x72, matrix products, newton_inverse(): jnp.einsum('...ij,...jk->...ik', product, nested, precision=PRECISE)  119 us
    dot_general x12, matrix products, linear_back(): jnp.einsum('bnm,km->bnk', upstream, weight, preferred_element_type=jnp.fl...  98.8 us
    dot_general x12, matrix products, linear(): jnp.einsum('bnk,km->bnm', values, weight, preferred_element_type=jnp.floa...  94 us
  transfers between devices with their start and end apart: 15, of which 7 were waited for; matrix products, arithmetic and copies ran while one was open for 40% of the time, Pallas kernels for 0%

commit v1 on v0

v1 whole, which is shorter than its diff:
```python
import functools

import jax
import jax.numpy as jnp
from jax import lax
from jax.experimental import pallas as pl
from jax.experimental.pallas import tpu as pltpu
from jax.sharding import PartitionSpec as P

D = 768
H = 12
HD = 64
FF = 3072
LM = 64
NS_STEPS = 6
HALF = 16
TAPS = 33
LONG = 4096
GROUP = 256
EPSILON = 1e-05
MASKED_SCORE = -1e30
SCALE = 0.125
VMEM_BYTES = 63 * 1024 * 1024

f32 = jnp.float32
bf = jnp.bfloat16
sds = jax.ShapeDtypeStruct


def dot(a, b, ca, cb):
    return lax.dot_general(a, b, (((ca,), (cb,)), ((), ())), preferred_element_type=f32)


def split(v):
    hi = v.astype(bf)
    return hi, (v - hi.astype(f32)).astype(bf)


def mm(a, b, ca=1, cb=0):
    ah, al = split(a)
    bh, bl = split(b)
    return dot(ah, bh, ca, cb) + (dot(ah, bl, ca, cb) + dot(al, bh, ca, cb))


def iota(shape, dim):
    return lax.broadcasted_iota(jnp.int32, shape, dim)


def spread_heads(block):
    tiled = jnp.concatenate([block.astype(f32)] * 4, axis=0)
    same = (iota((GROUP, GROUP), 0) // HD) == (iota((GROUP, GROUP), 1) // HD)
    return jnp.where(same, tiled, 0.0).astype(bf)


def pick_heads(full):
    head = iota((LM, GROUP), 1) // HD
    out = full[:LM]
    for h in range(1, 4):
        out = jnp.where(head == h, full[h * LM : (h + 1) * LM], out)
    return out


def lanes_of(columns):
    n = columns[0].shape[0]
    lane = iota((n, 128), 1)
    wide = jnp.zeros((n, 128), f32)
    for k, col in enumerate(columns):
        wide = jnp.where(lane == k, col, wide)
    return wide.T[:8]


def three_parts(row):
    hi = row.astype(bf).astype(f32)
    mid = (row - hi).astype(bf).astype(f32)
    low = row - hi - mid
    r = iota((16, row.shape[1]), 0)
    return jnp.where(r == 0, hi, jnp.where(r == 1, mid, jnp.where(r == 2, low, 0.0))).astype(bf)


def from_parts(rows):
    v = rows.astype(f32)
    total = v[0:1] + v[1:2] + v[2:3]
    return jnp.broadcast_to(total, (8, total.shape[1])).T[:, 0:1]


def head_softmax(scores):
    rows = scores.shape[1]
    s3 = scores.reshape(4, LM, rows)
    e = jnp.exp(s3 - jnp.max(s3, axis=1, keepdims=True))
    return (e / jnp.sum(e, axis=1, keepdims=True)).reshape(GROUP, rows)


def params(vmem=VMEM_BYTES):
    return pltpu.CompilerParams(vmem_limit_bytes=vmem)


def cost(flops, nbytes, trans=0):
    return pl.CostEstimate(flops=int(flops), bytes_accessed=int(nbytes), transcendentals=int(trans))


SMEM_SPEC = pl.BlockSpec(memory_space=pltpu.SMEM)


def const_spec(shape):
    return pl.BlockSpec(shape, lambda i: tuple(0 for _ in shape), pipeline_mode=pl.Buffered(1))


def qkv_kernel(n_long, x_l, x_s, wq, wk, wv, q_l, k_l, v_l, q_s, k_s, v_s, w_t):
    i = pl.program_id(0)

    @pl.when(i == 0)
    def _():
        for j, w in enumerate((wq, wk, wv)):
            w_t[j] = w[...].T

    x = jnp.where(i < n_long, x_l[...], x_s[...])
    made = [dot(w_t[j], x, 1, 1).astype(bf) for j in range(3)]

    @pl.when(i < n_long)
    def _():
        for ref, v in zip((q_l, k_l, v_l), made):
            ref[...] = v

    @pl.when(i >= n_long)
    def _():
        for ref, v in zip((q_s, k_s, v_s), made):
            ref[...] = v


def qkv(x_l, x_s, wq, wk, wv, tile=512):
    nl, ns = x_l.shape[0] // tile, x_s.shape[0] // tile
    long_at = lambda i: jnp.minimum(i, nl - 1)
    short_at = lambda i: jnp.maximum(i - nl, 0)
    row = lambda f: pl.BlockSpec((tile, D), lambda i: (f(i), 0))
    col = lambda f: pl.BlockSpec((D, tile), lambda i: (0, f(i)))
    tl, ts = x_l.shape[0], x_s.shape[0]
    return pl.pallas_call(
        functools.partial(qkv_kernel, nl),
        grid=(nl + ns,),
        in_specs=[row(long_at), row(short_at)] + [const_spec((D, D))] * 3,
        out_specs=[col(long_at)] * 3 + [col(short_at)] * 3,
        out_shape=[sds((D, tl), bf)] * 3 + [sds((D, ts), bf)] * 3,
        scratch_shapes=[pltpu.VMEM((3, D, D), bf)],
        compiler_params=params(),
        cost_estimate=cost(6 * (tl + ts) * D * D, 8 * (tl + ts) * D),
        name="qkv",
    )(x_l, x_s, wq, wk, wv)


def short_member(length, rows):
    seg = length // LM
    lm = iota((LM, rows), 0)
    pos = iota((LM, rows), 1)
    return ((pos >= lm * seg) & (pos < (lm + 1) * seg)).astype(f32)


def short_marks_kernel(length, q, k, lq, lk):
    member = short_member(length[0], q.shape[1]).astype(bf)
    count = (length[0] // LM).astype(f32)
    lq[...] = (dot(member, q[...], 1, 1) / count).astype(bf)
    lk[...] = (dot(member, k[...], 1, 1) / count).astype(bf)


def short_marks(length, q, k):
    return pl.pallas_call(
        short_marks_kernel,
        in_specs=[SMEM_SPEC] + [pl.BlockSpec(memory_space=pltpu.VMEM)] * 2,
        out_shape=[sds((LM, D), bf)] * 2,
        compiler_params=params(),
        cost_estimate=cost(1e8, 2e6),
        name="short_marks",
    )(length, q, k)


def stats_kernel(masked, units, length, lq, k, v, msg):
    rows = k.shape[1]
    sums, stats = [], []
    for g in range(3):
        gs = slice(g * GROUP, (g + 1) * GROUP)
        scores = dot(spread_heads(lq[:, gs] * SCALE), k[gs, :], 1, 0)
        if masked:
            scores = jnp.where(iota((GROUP, rows), 1) < length[0], scores, MASKED_SCORE)
        most = jnp.max(scores, axis=1, keepdims=True)
        e = jnp.exp(scores - most)
        stats.append(lanes_of([most, jnp.sum(e, axis=1, keepdims=True)]))
        sums.append(pick_heads(dot(e.astype(bf), v[gs, :], 1, 1)))
    sums = jnp.concatenate(sums, axis=1)
    stats = jnp.concatenate(stats, axis=1)
    width = D // units
    for u in range(units):
        us = slice(u * width, (u + 1) * width)
        msg[u, :LM, :] = sums[:, us]
        msg[u, LM:, :] = stats[:, us]


def item_specs(rows):
    mark = pl.BlockSpec((LM, D), lambda i: (i, 0))
    tok = pl.BlockSpec((D, rows), lambda i: (0, i))
    return mark, tok


def stats(length, lq, k, v, items, units, masked):
    rows = k.shape[1] // items
    mark, tok = item_specs(rows)
    return pl.pallas_call(
        functools.partial(stats_kernel, masked, units),
        grid=(items,),
        in_specs=[SMEM_SPEC, mark, tok, tok],
        out_specs=pl.BlockSpec((units, LM + 8, D // units), lambda i: (i, 0, 0)),
        out_shape=sds((items * units, LM + 8, D // units), f32),
        compiler_params=params(),
        cost_estimate=cost(4 * items * rows * D * GROUP, 4 * items * rows * D, items * rows * D),
        name="stats",
    )(length, lq, k, v)


def eye():
    return jnp.where(iota((LM, LM), 0) == iota((LM, LM), 1), 1.0, 0.0).astype(f32)


def head_slices(count):
    return [slice(h * HD, (h + 1) * HD) for h in range(count)]


def mark_probs(q, k):
    s = SCALE * dot(q, k, 1, 1)
    e = jnp.exp(s - jnp.max(s, axis=-1, keepdims=True))
    return e / jnp.sum(e, axis=-1, keepdims=True)


def inverse_start(a):
    col = jnp.sum(a, axis=0, keepdims=True)
    row = jnp.sum(a, axis=1, keepdims=True)
    return col, row, jnp.max(col, axis=1, keepdims=True), jnp.max(row, axis=0, keepdims=True)


def inverse_steps(a_list, kept=None):
    ident = eye()
    z_list = []
    for a in a_list:
        _, _, cm, rm = inverse_start(a)
        z_list.append(a.T / (cm * rm))
    for _ in range(NS_STEPS):
        p_list = [mm(a, z) for a, z in zip(a_list, z_list)]
        t2 = [15.0 * ident - mm(p, 7.0 * ident - p) for p in p_list]
        t3 = [13.0 * ident - mm(p, t) for p, t in zip(p_list, t2)]
        if kept is not None:
            kept.append((z_list, p_list, t2, t3))
        z_list = [0.25 * mm(z, t) for z, t in zip(z_list, t3)]
    return z_list


def inverse_kernel(lq, lk, z_out):
    hs = head_slices(lq.shape[2] // HD)
    a_list = [mark_probs(lq[0, :, s], lk[0, :, s]) for s in hs]
    for s, z in zip(hs, inverse_steps(a_list)):
        z_out[0, :, s] = z


def inverse(lq, lk):
    units, _, width = lq.shape
    spec = pl.BlockSpec((1, LM, width), lambda i: (i, 0, 0))
    return pl.pallas_call(
        inverse_kernel,
        grid=(units,),
        in_specs=[spec, spec],
        out_specs=spec,
        out_shape=sds((units, LM, width), f32),
        compiler_params=params(),
        cost_estimate=cost(units * (width // HD) * 24 * 3 * 2 * 64**3 * 16, 1e6),
        name="inverse",
    )(lq, lk)


def combine_kernel(senders, msg, z, out, bv_out):
    width = z.shape[2]
    most = jnp.concatenate([msg[0, d, LM : LM + 1, :] for d in range(senders)], axis=0)
    part = jnp.concatenate([msg[0, d, LM + 1 : LM + 2, :] for d in range(senders)], axis=0)
    top = jnp.max(most, axis=0, keepdims=True)
    e = jnp.exp(most - top)
    total = jnp.sum(part * e, axis=0, keepdims=True)
    weight = e / total
    if senders < 8:
        weight = jnp.concatenate([weight] + [jnp.zeros((8 - senders, width), f32)], axis=0)
    weight = weight.T
    w_all = []
    for s in head_slices(width // HD):
        bv = jnp.zeros((LM, HD), f32)
        for d in range(senders):
            bv = bv + weight[s, d : d + 1] * msg[0, d, :LM, s]
        bv_out[0, :, s] = bv
        w_all.append(mm(z[0, :, s], bv))
    out[0, :LM, :] = jnp.concatenate(w_all, axis=1).astype(bf)
    out[0, LM:, :] = three_parts(top + jnp.log(total))


def combine(msg, z):
    units, senders, _, width = msg.shape
    spec = pl.BlockSpec((1, LM, width), lambda i: (i, 0, 0))
    return pl.pallas_call(
        functools.partial(combine_kernel, senders),
        grid=(units,),
        in_specs=[pl.BlockSpec((1, senders, LM + 8, width), lambda i: (i, 0, 0, 0)), spec],
        out_specs=[pl.BlockSpec((1, LM + 16, width), lambda i: (i, 0, 0)), spec],
        out_shape=[sds((units, LM + 16, width), bf), sds((units, LM, width), f32)],
        compiler_params=params(),
        cost_estimate=cost(1e7, 2e6),
        name="combine",
    )(msg, z)


def joined(ref, units, rows):
    return jnp.concatenate([ref[u, rows, :] for u in range(units)], axis=1)


def mix_kernel(units, lk, w, q, conv, out):
    w_all = joined(w, units, slice(0, LM))
    for g in range(3):
        gs = slice(g * GROUP, (g + 1) * GROUP)
        probs = head_softmax(dot(spread_heads(lk[:, gs] * SCALE), q[gs, :], 1, 0)).astype(bf)
        out[gs, :] = (dot(spread_heads(w_all[:, gs]), probs, 0, 0) + conv[gs, :]).astype(bf)


def unit_spec(units, rows, width):
    return pl.BlockSpec((units, rows, width), lambda i: (i, 0, 0))


def mix(lk, w, q, conv, items, units):
    rows = q.shape[1] // items
    mark, tok = item_specs(rows)
    return pl.pallas_call(
        functools.partial(mix_kernel, units),
        grid=(items,),
        in_specs=[mark, unit_spec(units, LM + 16, D // units), tok, tok],
        out_specs=tok,
        out_shape=sds(q.shape, bf),
        compiler_params=params(),
        cost_estimate=cost(4 * items * rows * D * GROUP, 8 * items * rows * D, items * rows * D),
        name="mix",
    )(lk, w, q, conv)


def windows(body, rim, items, rows, limit):
    out = []
    for j in range(items):
        own = body[:, j * rows : (j + 1) * rows]
        if limit is not None:
            own = jnp.where(iota(own.shape, 1) < limit, own.astype(f32), 0.0).astype(bf)
        wide = jnp.concatenate(
            [rim[:, 32 * j : 32 * j + HALF], own, rim[:, 32 * j + HALF : 32 * j + 2 * HALF]], axis=1
        )
        for t in range(rows // 128):
            out.append(wide[:, t * 128 : t * 128 + 128 + 2 * HALF])
    return jnp.concatenate(out, axis=0)


def band(row):
    wide = jnp.concatenate([row, jnp.zeros((1, 128), f32)], axis=1)
    rolled = pltpu.roll(jnp.broadcast_to(wide, (128, 256)), 0, 1, stride=1, stride_axis=0)
    return split(rolled[:, : 128 + 2 * HALF])


def unstack(stacked, out, items, rows, limit=None):
    k = 0
    for j in range(items):
        for t in range(rows // 128):
            v = stacked[k * HD : (k + 1) * HD]
            if limit is not None:
                v = jnp.where(iota(v.shape, 1) + t * 128 < limit, v, 0.0)
            out[:, j * rows + t * 128 : j * rows + (t + 1) * 128] = v
            k += 1


def conv_kernel(items, rows, masked, length, v, rim, taps, out):
    limit = length[0] if masked else None
    wins = windows(v[...], rim[...], items, rows, limit)
    hi, lo = band(taps[0, 0:1, :])
    unstack(dot(wins, hi, 1, 1) + dot(wins, lo, 1, 1), out, items, rows)


def conv(length, v, rim, taps, items, masked):
    rows = v.shape[1] // items
    tok = pl.BlockSpec((HD, items * rows), lambda h: (h, 0))
    return pl.pallas_call(
        functools.partial(conv_kernel, items, rows, masked),
        grid=(H,),
        in_specs=[
            SMEM_SPEC,
            tok,
            pl.BlockSpec((HD, rim.shape[1]), lambda h: (h, 0)),
            pl.BlockSpec((1, 8, 128), lambda h: (h, 0, 0)),
        ],
        out_specs=tok,
        out_shape=sds(v.shape, f32),
        compiler_params=params(),
        cost_estimate=cost(4 * 512 * v.size, 6 * v.size),
        name="conv",
    )(length, v, rim, taps)


def conv_back_kernel(items, rows, masked, length, v, rim, up, up_rim, taps, out, tap_grad):
    limit = length[0] if masked else None
    wins = windows(v[...], rim[...], items, rows, limit)
    up_wins = windows(up[...], up_rim[...], items, rows, None)
    hi, lo = band(taps[0, 1:2, :])
    unstack(dot(up_wins, hi, 1, 1) + dot(up_wins, lo, 1, 1), out, items, rows, limit)
    ups = jnp.concatenate(
        [up[:, t * 128 : (t + 1) * 128] for t in range(items * rows // 128)], axis=0
    )
    gram = dot(ups, wins, 0, 0)
    flip = (iota((128, 128), 0) + iota((128, 128), 1) == 127).astype(f32).astype(bf)
    hi, lo = split(gram)
    gram = dot(flip, hi, 1, 0) + dot(flip, lo, 1, 0)
    gram = jnp.concatenate([gram, jnp.zeros((128, 256 - gram.shape[1]), f32)], axis=1)
    skewed = pltpu.roll(gram, 129, 1, stride=1, stride_axis=0)
    tap_grad[0] = jnp.broadcast_to(jnp.sum(skewed, axis=0, keepdims=True)[:, :128], (8, 128))


def conv_back(length, v, rim, up, up_rim, taps, items, masked):
    rows = v.shape[1] // items
    tok = pl.BlockSpec((HD, items * rows), lambda h: (h, 0))
    rim_spec = pl.BlockSpec((HD, rim.shape[1]), lambda h: (h, 0))
    tap_spec = pl.BlockSpec((1, 8, 128), lambda h: (h, 0, 0))
    return pl.pallas_call(
        functools.partial(conv_back_kernel, items, rows, masked),
        grid=(H,),
        in_specs=[SMEM_SPEC, tok, rim_spec, tok, rim_spec, tap_spec],
        out_specs=[tok, tap_spec],
        out_shape=[sds(v.shape, f32), sds((H, 8, 128), f32)],
        compiler_params=params(),
        cost_estimate=cost(6 * 512 * v.size, 8 * v.size),
        name="conv_back",
    )(length, v, rim, up, up_rim, taps)


def fold_rows(v):
    return jnp.sum(v.reshape(v.shape[0] // 8, 8, v.shape[1]), axis=0)


def gelu_parts(x):
    e = jnp.exp(x * x * (-0.5))
    t = pl.reciprocal(1.0 + jnp.abs(x) * (0.3275911 * 0.7071067811865476), approx=False)
    poly = t * (
        0.127414796 + t * (-0.142248368 + t * (0.7107068705 + t * (-0.7265760135 + t * 0.5307027145)))
    )
    tail = poly * e
    phi = jnp.where(x >= 0, 1.0 - tail, tail)
    return x * phi, phi + x * e * 0.3989422804014327


def put_bf16(pairs, stage, sem):
    pend = []
    for acc, dst in pairs:
        for c in range(0, acc.shape[1], D):
            slot = len(pend) % 2
            if len(pend) >= 2:
                pend[-2].wait()
            stage[slot] = acc[:, c : c + D].astype(bf)
            pend.append(pltpu.make_async_copy(stage.at[slot], dst.at[:, c : c + D], sem.at[slot]))
            pend[-1].start()
    pend[-2].wait()
    pend[-1].wait()


def dense_kernel(n_long, chunk, x_l, x_s, o_l, o_s, c_l, c_s, w_out, w_up, w_down, g1, b1, bu, bd, g2, b2,
                 out_l, out_s, dr_l, dr_s, do_l, do_s, gup, gdn, gout, small, small_up,
                 acc_up, acc_dn, acc_out, act, dact, accs, accu, stage, sem):
    i = pl.program_id(0)
    last = pl.num_programs(0) - 1
    is_long = i < n_long

    @pl.when(i == 0)
    def _():
        for ref in (acc_up, acc_dn, acc_out, accs, accu):
            ref[...] = jnp.zeros_like(ref)

    x = jnp.where(is_long, x_l[...], x_s[...]).astype(f32)
    o_t = jnp.where(is_long, o_l[...], o_s[...])
    r1 = x + dot(o_t, w_out[...], 0, 0)
    cen = r1 - jnp.mean(r1, axis=-1, keepdims=True)
    rstd1 = lax.rsqrt(jnp.mean(cen * cen, axis=-1, keepdims=True) + EPSILON)
    xh1 = cen * rstd1
    h1 = (xh1 * g1[...] + b1[...]).astype(bf)
    r2 = h1.astype(f32) + bd[...]
    for c in range(FF // chunk):
        cs = slice(c * chunk, (c + 1) * chunk)
        a, dg = gelu_parts(dot(h1, w_up[:, cs], 1, 0) + bu[:, cs])
        a = a.astype(bf)
        act[:, cs] = a
        dact[:, cs] = dg
        r2 = r2 + dot(a, w_down[cs, :], 1, 0)
    cen2 = r2 - jnp.mean(r2, axis=-1, keepdims=True)
    rstd2 = lax.rsqrt(jnp.mean(cen2 * cen2, axis=-1, keepdims=True) + EPSILON)
    xh2 = cen2 * rstd2
    out = (xh2 * g2[...] + b2[...]).astype(bf)
    g = jnp.where(is_long, c_l[...], c_s[...]).astype(f32)
    dxh = g * g2[...]
    dr2 = rstd2 * (
        dxh - jnp.mean(dxh, axis=-1, keepdims=True) - xh2 * jnp.mean(dxh * xh2, axis=-1, keepdims=True)
    )
    dz2 = dr2.astype(bf)
    accs[4] += fold_rows(g * xh2)
    accs[5] += fold_rows(g)
    accs[2] += fold_rows(dz2.astype(f32))
    dz2_t = dz2.T
    h1_t = h1.T
    dh1 = dr2
    for c in range(FF // chunk):
        cs = slice(c * chunk, (c + 1) * chunk)
        dp1 = (dot(dz2, w_down[cs, :], 1, 1) * dact[:, cs]).astype(bf)
        accu[:, cs] += fold_rows(dp1.astype(f32))
        dh1 = dh1 + dot(dp1, w_up[:, cs], 1, 1)
        acc_up[:, cs] += dot(h1_t, dp1, 1, 0)
        acc_dn[:, cs] += dot(dz2_t, act[:, cs], 1, 0)
    accs[0] += fold_rows(dh1 * xh1)
    accs[1] += fold_rows(dh1)
    dx = dh1 * g1[...]
    dr1 = rstd1 * (
        dx - jnp.mean(dx, axis=-1, keepdims=True) - xh1 * jnp.mean(dx * xh1, axis=-1, keepdims=True)
    )
    da1 = dr1.astype(bf)
    acc_out[...] += dot(o_t, da1, 1, 0)
    do_t = dot(w_out[...], da1, 1, 1).astype(bf)

    @pl.when(is_long)
    def _():
        out_l[...] = out
        dr_l[...] = dr1
        do_l[...] = do_t

    @pl.when(jnp.logical_not(is_long))
    def _():
        out_s[...] = out
        dr_s[...] = dr1
        do_s[...] = do_t

    @pl.when(i == last)
    def _():
        put_bf16(((acc_up, gup), (acc_dn, gdn), (acc_out, gout)), stage, sem)
        small[...] = jnp.sum(accs[...], axis=1)
        small_up[...] = jnp.sum(accu[...], axis=0, keepdims=True)


def dense(x_l, x_s, o_l, o_s, c_l, c_s, w_out, w_up, w_down, g1, b1, bu, bd, g2, b2, tile=256, chunk=768):
    nl, ns = x_l.shape[0] // tile, x_s.shape[0] // tile
    long_at = lambda i: jnp.minimum(i, nl - 1)
    short_at = lambda i: jnp.maximum(i - nl, 0)
    row = lambda f: pl.BlockSpec((tile, D), lambda i: (f(i), 0))
    col = lambda f: pl.BlockSpec((D, tile), lambda i: (0, f(i)))
    anywhere = pl.BlockSpec(memory_space=pl.ANY)
    tl, ts = x_l.shape[0], x_s.shape[0]
    vec = const_spec((1, D))
    return pl.pallas_call(
        functools.partial(dense_kernel, nl, chunk),
        grid=(nl + ns,),
        in_specs=[row(long_at), row(short_at), col(long_at), col(short_at), row(long_at), row(short_at)]
        + [const_spec((D, D)), const_spec((D, FF)), const_spec((FF, D))]
        + [vec, vec, const_spec((1, FF)), vec, vec, vec],
        out_specs=[row(long_at), row(short_at), row(long_at), row(short_at), col(long_at), col(short_at)]
        + [anywhere] * 3
        + [const_spec((6, D)), const_spec((1, FF))],
        out_shape=[sds((tl, D), bf), sds((ts, D), bf), sds((tl, D), f32), sds((ts, D), f32)]
        + [sds((D, tl), bf), sds((D, ts), bf), sds((D, FF), bf), sds((D, FF), bf), sds((D, D), bf)]
        + [sds((6, D), f32), sds((1, FF), f32)],
        scratch_shapes=[
            pltpu.VMEM((D, FF), f32),
            pltpu.VMEM((D, FF), f32),
            pltpu.VMEM((D, D), f32),
            pltpu.VMEM((tile, FF), bf),
            pltpu.VMEM((tile, FF), f32),
            pltpu.VMEM((6, 8, D), f32),
            pltpu.VMEM((8, FF), f32),
            pltpu.VMEM((2, D, D), bf),
            pltpu.SemaphoreType.DMA((2,)),
        ],
        compiler_params=params(),
        cost_estimate=cost(2 * (tl + ts) * (3 * D * D + 6 * D * FF), 60e6, (tl + ts) * FF),
        name="dense",
    )(x_l, x_s, o_l, o_s, c_l, c_s, w_out, w_up, w_down, g1, b1, bu, bd, g2, b2)


def back_f_kernel(units, lk, w, q, up, dw_out, dlk_out, dsf_out):
    w_all = joined(w, units, slice(0, LM))
    dws = []
    for g in range(3):
        gs = slice(g * GROUP, (g + 1) * GROUP)
        q_g, up_g = q[gs, :], up[gs, :]
        rows = q_g.shape[1]
        probs = head_softmax(dot(spread_heads(lk[:, gs] * SCALE), q_g, 1, 0))
        dws.append(pick_heads(dot(probs.astype(bf), up_g, 1, 1)))
        dprobs = dot(spread_heads(w_all[:, gs]), up_g, 1, 0)
        weighted = jnp.sum((probs * dprobs).reshape(4, LM, rows), axis=1, keepdims=True)
        dsf = probs * (dprobs.reshape(4, LM, rows) - weighted).reshape(GROUP, rows)
        dsf = dsf.astype(bf)
        dsf_out[gs, :] = dsf
        dlk_out[:, gs] = SCALE * pick_heads(dot(dsf, q_g, 1, 1))
    dws = jnp.concatenate(dws, axis=1)
    width = D // units
    for u in range(units):
        dw_out[u] = dws[:, u * width : (u + 1) * width]


def back_f(lk, w, q, up, items, units):
    rows = q.shape[1] // items
    mark, tok = item_specs(rows)
    width = D // units
    return pl.pallas_call(
        functools.partial(back_f_kernel, units),
        grid=(items,),
        in_specs=[mark, unit_spec(units, LM + 16, width), tok, tok],
        out_specs=[unit_spec(units, LM, width), mark, tok],
        out_shape=[sds((items * units, LM, width), f32), sds((items * LM, D), f32), sds(q.shape, bf)],
        compiler_params=params(),
        cost_estimate=cost(8 * items * rows * D * GROUP, 6 * items * rows * D, items * rows * D),
        name="back_f",
    )(lk, w, q, up)


def back_mix_kernel(senders, dw_in, z, bv, out, dw_out):
    width = z.shape[2]
    dw = dw_in[0, 0]
    for d in range(1, senders):
        dw = dw + dw_in[0, d]
    dw_out[0] = dw
    dbvs, dots = [], []
    for s in head_slices(width // HD):
        dbv = mm(z[0, :, s], dw[:, s], 0, 0).astype(bf)
        dots.append(jnp.sum(dbv.astype(f32) * bv[0, :, s], axis=1, keepdims=True))
        dbvs.append(dbv)
    out[0, :LM, :] = jnp.concatenate(dbvs, axis=1)
    out[0, LM:, :] = three_parts(lanes_of([jnp.concatenate(dots, axis=0)])[:1])


def back_mix(dw, z, bv):
    units, senders, _, width = dw.shape
    spec = pl.BlockSpec((1, LM, width), lambda i: (i, 0, 0))
    return pl.pallas_call(
        functools.partial(back_mix_kernel, senders),
        grid=(units,),
        in_specs=[pl.BlockSpec((1, senders, LM, width), lambda i: (i, 0, 0, 0)), spec, spec],
        out_specs=[pl.BlockSpec((1, LM + 16, width), lambda i: (i, 0, 0)), spec],
        out_shape=[sds((units, LM + 16, width), bf), sds((units, LM, width), f32)],
        compiler_params=params(),
        cost_estimate=cost(1e7, 2e6),
        name="back_mix",
    )(dw, z, bv)


def back_inverse_kernel(lq, lk, dw, bv, dlq_out, dlk_out):
    hs = head_slices(lq.shape[2] // HD)
    a_list = [mark_probs(lq[0, :, s], lk[0, :, s]) for s in hs]
    kept = []
    inverse_steps(a_list, kept)
    ident = eye()
    dz = [mm(dw[0, :, s], bv[0, :, s], 1, 1) for s in hs]
    da = [jnp.zeros((LM, LM), f32) for _ in hs]
    for z, p, t2, t3 in reversed(kept):
        dt3 = [0.25 * mm(zz, d, 0, 0) for zz, d in zip(z, dz)]
        dz = [0.25 * mm(d, t, 1, 1) for d, t in zip(dz, t3)]
        dp = [-mm(d, t, 1, 1) for d, t in zip(dt3, t2)]
        dt2 = [-mm(pp, d, 0, 0) for pp, d in zip(p, dt3)]
        dp = [x - mm(d, 7.0 * ident - pp, 1, 1) for x, d, pp in zip(dp, dt2, p)]
        dp = [x + mm(pp, d, 0, 0) for x, pp, d in zip(dp, p, dt2)]
        da = [x + mm(d, zz, 1, 1) for x, d, zz in zip(da, dp, z)]
        dz = [x + mm(a, d, 0, 0) for x, a, d in zip(dz, a_list, dp)]
    for s, a, g, d in zip(hs, a_list, da, dz):
        col, row, cm, rm = inverse_start(a)
        norm = cm * rm
        g = g + d.T / norm
        dnorm = -jnp.sum(jnp.sum(d.T * a, axis=1, keepdims=True), axis=0, keepdims=True) / (norm * norm)
        at_col = (col == cm).astype(f32)
        at_row = (row == rm).astype(f32)
        g = g + dnorm * rm * at_col / jnp.sum(at_col, axis=1, keepdims=True)
        g = g + dnorm * cm * at_row / jnp.sum(at_row, axis=0, keepdims=True)
        ds = a * (g - jnp.sum(a * g, axis=1, keepdims=True))
        dlq_out[0, :, s] = SCALE * mm(ds, lk[0, :, s].astype(f32))
        dlk_out[0, :, s] = SCALE * mm(ds, lq[0, :, s].astype(f32), 0, 0)


def back_inverse(lq, lk, dw, bv):
    units, _, width = lq.shape
    spec = pl.BlockSpec((1, LM, width), lambda i: (i, 0, 0))
    return pl.pallas_call(
        back_inverse_kernel,
        grid=(units,),
        in_specs=[spec] * 4,
        out_specs=[spec] * 2,
        out_shape=[sds((units, LM, width), f32)] * 2,
        compiler_params=params(),
        cost_estimate=cost(units * (width // HD) * 72 * 3 * 2 * 64**3 * 16, 2e6),
        name="back_inverse",
    )(lq, lk, dw, bv)


def back_b_kernel(masked, units, length, lq, w, dbv, k, v, dconv, dsb_out, dv_out, dlq_out):
    rows = k.shape[1]
    level = from_parts(joined(w, units, slice(LM, LM + 16)))
    dots = from_parts(joined(dbv, units, slice(LM, LM + 16)))
    dbv_all = joined(dbv, units, slice(0, LM))
    for g in range(3):
        gs = slice(g * GROUP, (g + 1) * GROUP)
        scores = dot(spread_heads(lq[:, gs] * SCALE), k[gs, :], 1, 0)
        if masked:
            scores = jnp.where(iota((GROUP, rows), 1) < length[0], scores, MASKED_SCORE)
        probs = jnp.exp(scores - level[gs])
        wide = spread_heads(dbv_all[:, gs])
        dsb = (probs * (dot(wide, v[gs, :], 1, 0) - dots[gs])).astype(bf)
        dsb_out[gs, :] = dsb
        dv_out[gs, :] = (dot(wide, probs.astype(bf), 0, 0) + dconv[gs, :]).astype(bf)
        dlq_out[:, gs] = SCALE * pick_heads(dot(dsb, k[gs, :], 1, 1))


def back_b(length, lq, w, dbv, k, v, dconv, items, units, masked):
    rows = k.shape[1] // items
    mark, tok = item_specs(rows)
    unit = unit_spec(units, LM + 16, D // units)
    return pl.pallas_call(
        functools.partial(back_b_kernel, masked, units),
        grid=(items,),
        in_specs=[SMEM_SPEC, mark, unit, unit, tok, tok, tok],
        out_specs=[tok, tok, mark],
        out_shape=[sds(k.shape, bf), sds(k.shape, bf), sds((items * LM, D), f32)],
        compiler_params=params(),
        cost_estimate=cost(10 * items * rows * D * GROUP, 12 * items * rows * D, items * rows * D),
        name="back_b",
    )(length, lq, w, dbv, k, v, dconv)


def final_part(member, x, dr, lq, lk, dsf, dsb, dv, sq, sk, wq, wk, wv, acc):
    member2 = jnp.concatenate([member, member], axis=0)
    x_t = x[...].T
    made = []
    for marks, scores, sums in ((lk, dsf, sq), (lq, dsb, sk)):
        hi, lo = split(sums[...])
        back = dot(jnp.concatenate([hi, lo], axis=0), member2, 0, 0)
        parts = []
        for g in range(3):
            gs = slice(g * GROUP, (g + 1) * GROUP)
            part = dot(spread_heads(marks[:, gs] * SCALE), scores[gs, :], 0, 0) + back[gs]
            parts.append(part.astype(bf).T)
        made.append(jnp.concatenate(parts, axis=1))
    made.append(dv[...].T)
    total = dr[...]
    for j, (grad, w) in enumerate(zip(made, (wq, wk, wv))):
        total = total + dot(grad, w[...], 1, 1)
        acc[j] += dot(x_t, grad, 1, 0)
    return total.astype(bf)


def final_kernel(n_long, length, x_l, dr_l, lq_l, lk_l, dsf_l, dsb_l, dv_l, sq_l, sk_l,
                 x_s, dr_s, lq_s, lk_s, dsf_s, dsb_s, dv_s, sq_s, sk_s, wq, wk, wv,
                 out_l, out_s, gq, gk, gv, acc, stage, sem):
    i = pl.program_id(0)

    @pl.when(i == 0)
    def _():
        acc[...] = jnp.zeros_like(acc)

    @pl.when(i < n_long)
    def _():
        count, rows = sq_l.shape[0], x_l.shape[0]
        member = (iota((count, rows), 1) // (LONG // LM) == iota((count, rows), 0)).astype(f32).astype(bf)
        out_l[...] = final_part(member, x_l, dr_l, lq_l, lk_l, dsf_l, dsb_l, dv_l, sq_l, sk_l, wq, wk, wv, acc)

    @pl.when(i >= n_long)
    def _():
        member = short_member(length[0], x_s.shape[0]).astype(bf)
        out_s[...] = final_part(member, x_s, dr_s, lq_s, lk_s, dsf_s, dsb_s, dv_s, sq_s, sk_s, wq, wk, wv, acc)
        put_bf16(((acc.at[0], gq), (acc.at[1], gk), (acc.at[2], gv)), stage, sem)


def final(length, long_args, short_args, weights, items):
    x_l, x_s = long_args[0], short_args[0]
    tl, ts = x_l.shape[0], x_s.shape[0]
    rows = tl // items
    marks_l = long_args[7].shape[0] // items
    at = lambda i: jnp.minimum(i, items - 1)

    def specs(n, r, marks, f):
        row = pl.BlockSpec((r, D), lambda i: (f(i), 0))
        mark = pl.BlockSpec((LM, D), lambda i: (f(i), 0))
        tok = pl.BlockSpec((D, r), lambda i: (0, f(i)))
        own = pl.BlockSpec((marks, D), lambda i: (f(i), 0))
        return [row, row, mark, mark, tok, tok, tok, own, own]

    anywhere = pl.BlockSpec(memory_space=pl.ANY)
    return pl.pallas_call(
        functools.partial(final_kernel, items),
        grid=(items + 1,),
        in_specs=[SMEM_SPEC]
        + specs(items, rows, marks_l, at)
        + specs(1, ts, LM, lambda i: 0)
        + [const_spec((D, D))] * 3,
        out_specs=[
            pl.BlockSpec((rows, D), lambda i: (at(i), 0)),
            pl.BlockSpec((ts, D), lambda i: (0, 0)),
        ]
        + [anywhere] * 3,
        out_shape=[sds((tl, D), bf), sds((ts, D), bf)] + [sds((D, D), bf)] * 3,
        scratch_shapes=[
            pltpu.VMEM((3, D, D), f32),
            pltpu.VMEM((2, D, D), bf),
            pltpu.SemaphoreType.DMA((2,)),
        ],
        compiler_params=params(),
        cost_estimate=cost(12 * (tl + ts) * D * D, 20 * (tl + ts) * D),
        name="final",
    )(length, *long_args, *short_args, *weights)


def swap(values, axis, bit):
    count = lax.axis_size(axis)
    return lax.ppermute(values, axis, [(i, i ^ bit) for i in range(count)])


def side(axis, bit):
    return (lax.axis_index(axis) // bit) % 2


def halve(values, dim, axis, bit):
    mine = side(axis, bit)
    keep = lax.dynamic_index_in_dim(values, mine, dim, keepdims=False)
    send = lax.dynamic_index_in_dim(values, 1 - mine, dim, keepdims=False)
    return keep.astype(f32) + swap(send.astype(bf), axis, bit).astype(f32)


def join(values, dim, axis, bit):
    mine = side(axis, bit)
    other = swap(values, axis, bit)
    return jnp.where(
        mine == 0,
        jnp.concatenate([values, other], axis=dim),
        jnp.concatenate([other, values], axis=dim),
    )


def is_small_mesh():
    return lax.axis_size("dp") == 4 and lax.axis_size("seq") == 8


def reduce_rows(grad, order):
    n = grad.shape[1]
    if not is_small_mesh():
        own = lax.psum_scatter(grad, "seq", scatter_dimension=0, tiled=True)
        return lax.psum(own.astype(f32), "dp")
    v = grad.reshape(2, 2, 2, 2, 48, n)
    v = halve(v, 3, "dp", 1).astype(bf)
    dims = ["z1", "z0", "y"]
    for step in order:
        if step == "x":
            v = halve(v.reshape(v.shape[:-1] + (2, n // 2)), v.ndim - 1, "dp", 2)
        else:
            dim = dims.index(step)
            dims.pop(dim)
            v = halve(v, dim, "seq", {"y": 1, "z0": 2, "z1": 4}[step])
        v = v.astype(bf)
    v = join(v, 1, "dp", 2)
    return join(v, 0, "dp", 1).astype(f32)


def reduce_columns(grad, order):
    if not is_small_mesh():
        own = lax.psum_scatter(grad, "seq", scatter_dimension=1, tiled=True)
        return lax.psum(own.astype(f32), "dp").T
    v = halve(grad.reshape(2, D // 2, FF), 0, "dp", 1).astype(bf)
    v = v.reshape(D // 2, 2, 2, 2, FF // 8)
    dims = ["z1", "z0", "y"]
    for step in order:
        if step == "x":
            v = halve(v.reshape((2, D // 4) + v.shape[1:]), 0, "dp", 2)
        else:
            dim = dims.index(step)
            dims.pop(dim)
            v = halve(v, dim + 1, "seq", {"y": 1, "z0": 2, "z1": 4}[step])
        v = v.astype(bf)
    v = join(v, 0, "dp", 2)
    return join(v, 0, "dp", 1).astype(f32).T


def sum_everywhere(values):
    if not is_small_mesh():
        return lax.psum(values, ("dp", "seq"))
    for axis, bit in (("dp", 1), ("dp", 2), ("seq", 1), ("seq", 2), ("seq", 4)):
        values = values + swap(values, axis, bit)
    return values


def gather(values):
    return lax.all_gather(values, "seq", axis=0)


def exchange(values):
    return lax.all_to_all(values, "seq", 0, 0, tiled=True)


def neighbours(first, last):
    count = lax.axis_size("seq")
    right = lax.ppermute(first, "seq", [((i + 1) % count, i) for i in range(count)])
    left = lax.ppermute(last, "seq", [(i, (i + 1) % count) for i in range(count)])
    return left, right


def pad_units(values, count):
    have = values.shape[0]
    if have == count:
        return values
    return jnp.concatenate([values, jnp.zeros((count - have,) + values.shape[1:], values.dtype)], axis=0)


def body(x_long, x_short, item_start, short_lengths, w_query, w_key, w_value, w_out, conv_taps, ln1_gain, ln1_bias,
         w_up, up_bias, w_down, down_bias, ln2_gain, ln2_bias, cot_long, cot_short):
    _, items, rows, _ = x_long.shape
    short_rows = x_short.shape[3]
    seg = LONG // LM
    own_marks = rows // seg
    n_seq = lax.axis_size("seq")
    me = lax.axis_index("seq")
    heads_each = next(h for h in (1, 2, 3, 4, 6, 12) if H % h == 0 and items * H // h <= n_seq and (h * HD) % 128 == 0)
    units = H // heads_each
    width = heads_each * HD
    owners = items * units

    x_l = x_long.reshape(items * rows, D)
    x_s = x_short.reshape(short_rows, D)
    length = short_lengths.reshape(1)
    no_length = jnp.zeros((1,), jnp.int32)

    x_mean = jnp.sum(x_long[0].reshape(items, own_marks, seg, D).astype(f32), axis=2) * (1.0 / seg)
    means = gather(x_mean)
    means = means.transpose(1, 0, 2, 3).reshape(items * LM, D)
    mean_hi, mean_lo = split(means)

    def marks_of(w):
        return (
            jnp.dot(mean_hi, w, preferred_element_type=f32) + jnp.dot(mean_lo, w, preferred_element_type=f32)
        ).astype(bf)

    lq_l, lk_l = marks_of(w_query), marks_of(w_key)

    place = (me - item_start[0]) % n_seq
    open_left = (place > 0)[:, None, None]
    open_right = (place < n_seq - 1)[:, None, None]

    def rims(left, right):
        return jnp.concatenate(
            [jnp.where(open_left, left, jnp.zeros_like(left)), jnp.where(open_right, right, jnp.zeros_like(right))], axis=1
        ).reshape(items * 2 * HALF, D)

    x_rim = rims(*neighbours(x_long[0, :, :HALF], x_long[0, :, rows - HALF :]))
    v_rim = jnp.einsum("ke,nk->en", w_value, x_rim, preferred_element_type=f32).astype(bf)
    no_rim = jnp.zeros((D, 2 * HALF), bf)

    tap_rows = jnp.stack([conv_taps.T, conv_taps[::-1].T], axis=1)
    tap_rows = jnp.pad(tap_rows, ((0, 0), (0, 6), (0, 128 - TAPS)))

    q_l, k_l, v_l, q_s, k_s, v_s = qkv(x_l, x_s, w_query, w_key, w_value)
    lq_s, lk_s = short_marks(length, q_s, k_s)

    msg_l = stats(no_length, lq_l, k_l, v_l, items, units, False)
    msg_s = stats(length, lq_s, k_s, v_s, 1, units, True)
    got_l = exchange(pad_units(msg_l, n_seq))

    mine = jnp.minimum(me, owners - 1)

    def my_unit(marks):
        return lax.dynamic_slice(
            marks, ((mine // units) * LM, (mine % units) * width), (LM, width)
        )

    def unit_rows(marks):
        return marks.reshape(LM, units, width).transpose(1, 0, 2)

    lq_u = jnp.concatenate([my_unit(lq_l)[None], unit_rows(lq_s)], axis=0)
    lk_u = jnp.concatenate([my_unit(lk_l)[None], unit_rows(lk_s)], axis=0)
    z_u = inverse(lq_u, lk_u)

    c_l = conv(no_length, v_l, v_rim, tap_rows, items, False)
    c_s = conv(length, v_s, no_rim, tap_rows, 1, True)

    w_own, bv_own = combine(got_l[None], z_u[:1])
    w_s, bv_s = combine(msg_s[:, None], z_u[1:])
    w_l = gather(w_own[0])

    o_l = mix(lk_l, w_l[:owners], q_l, c_l, items, units)
    o_s = mix(lk_s, w_s, q_s, c_s, 1, units)

    vec = lambda v: v.reshape(1, -1)
    out_l, out_s, dr_l, dr_s, do_l, do_s, g_up, g_dn, g_out, small, small_up = dense(
        x_l, x_s, o_l, o_s, cot_long.reshape(items * rows, D), cot_short.reshape(short_rows, D), w_out, w_up, w_down,
        vec(ln1_gain), vec(ln1_bias), vec(up_bias), vec(down_bias), vec(ln2_gain), vec(ln2_bias),
    )

    do_items = do_l.reshape(D, items, rows)
    do_rim = rims(
        *neighbours(do_items[:, :, :HALF].transpose(1, 2, 0), do_items[:, :, rows - HALF :].transpose(1, 2, 0))
    ).T
    dw_l, dlk_part, dsf_l = back_f(lk_l, w_l[:owners], q_l, do_l, items, units)
    dw_s, dlk_part_s, dsf_s = back_f(lk_s, w_s, q_s, do_s, 1, units)
    got_dw = exchange(pad_units(dw_l, n_seq))

    dc_l, tap_l = conv_back(no_length, v_l, v_rim, do_l, do_rim, tap_rows, items, False)
    dc_s, tap_s = conv_back(length, v_s, no_rim, do_s, no_rim, tap_rows, 1, True)

    dbv_own, dw_own = back_mix(got_dw[None], z_u[:1], bv_own)
    dbv_s, dw_sum_s = back_mix(dw_s[:, None], z_u[1:], bv_s)
    dbv_l = gather(dbv_own[0])

    dlq_u, dlk_u = back_inverse(
        lq_u, lk_u, jnp.concatenate([dw_own, dw_sum_s], axis=0), jnp.concatenate([bv_own, bv_s], axis=0)
    )
    dsb_l, dv_l, dlq_part = back_b(no_length, lq_l, w_l[:owners], dbv_l[:owners], k_l, v_l, dc_l, items, units, False)
    dsb_s, dv_s, dlq_part_s = back_b(length, lq_s, w_s, dbv_s, k_s, v_s, dc_s, 1, units, True)

    owned = (jnp.arange(owners) == me).astype(f32).reshape(items, units, 1, 1)

    def with_own(part, own):
        return part.reshape(items, LM, D) + (owned * own[None, None]).transpose(0, 2, 1, 3).reshape(items, LM, D)

    dl = jnp.stack([with_own(dlq_part, dlq_u[0]), with_own(dlk_part, dlk_u[0])]).astype(bf)
    dl = dl.reshape(2 * items, n_seq, own_marks, D).transpose(1, 0, 2, 3)
    dl = jnp.sum(exchange(dl).astype(f32), axis=0) * (1.0 / seg)
    dl = jnp.pad(dl.reshape(2, items, own_marks, D), ((0, 0), (0, 0), (0, 16 - own_marks), (0, 0)))
    dl = dl.reshape(2, items * 16, D)

    count = (length[0] // LM).astype(f32)
    from_units = lambda u: u.transpose(1, 0, 2).reshape(LM, D)
    sq_s = (dlq_part_s + from_units(dlq_u[1:])) / count
    sk_s = (dlk_part_s + from_units(dlk_u[1:])) / count

    grad_l, grad_s, g_q, g_k, g_v = final(
        length,
        (x_l, dr_l, lq_l, lk_l, dsf_l, dsb_l, dv_l, dl[0], dl[1]),
        (x_s, dr_s, lq_s, lk_s, dsf_s, dsb_s, dv_s, sq_s, sk_s),
        (w_query, w_key, w_value),
        items,
    )

    packed = jnp.concatenate(
        [small.reshape(-1), small_up.reshape(-1), (tap_l + tap_s)[:, 0, :].reshape(-1)]
    ).reshape(-1, 128)
    packed = sum_everywhere(packed).reshape(-1)
    small = packed[: 6 * D].reshape(6, D)
    small_up = packed[6 * D : 6 * D + FF]
    taps_g = packed[6 * D + FF :].reshape(H, 128)[:, :TAPS].T

    up_g = reduce_rows(g_up, ("x", "y", "z0", "z1"))
    down_g = reduce_columns(g_dn, ("y", "z0", "x", "z1"))
    out_g = reduce_rows(g_out, ("z0", "x", "y", "z1"))
    q_g = reduce_rows(g_q, ("x", "y", "z0", "z1"))
    k_g = reduce_rows(g_k, ("y", "z0", "x", "z1"))
    v_g = reduce_rows(g_v, ("z0", "x", "y", "z1"))
    return (
        out_l.reshape(x_long.shape),
        out_s.reshape(x_short.shape),
        grad_l.reshape(x_long.shape),
        grad_s.reshape(x_short.shape),
        q_g,
        k_g,
        v_g,
        out_g,
        taps_g,
        small[0],
        small[1],
        up_g,
        small_up,
        down_g,
        small[2],
        small[4],
        small[5],
    )


def solution(mesh):
    tokens = P("dp", None, "seq", None)
    shorts = P("dp", "seq", None, None, None)
    rows = P("seq", None)
    return jax.shard_map(
        body,
        mesh=mesh,
        in_specs=(tokens, shorts, P("dp", None), P("dp", "seq", None)) + (P(),) * 13 + (tokens, shorts),
        out_specs=(tokens, shorts, tokens, shorts, rows, rows, rows, rows, P(), P(), P(), rows, P(), rows, P(), P(), P()),
        check_vma=False,
    )
```

time: 2280 us -> 696 us (0.31)
  matrix products: 898 us -> 5.2 us
  waiting for transfers between devices: 663 us -> 57 us
  Pallas kernels: 0 us -> 345 us
  other arithmetic: 274 us -> 43.1 us
  local copies, waits for them, and re-layouts: 215 us -> 64.4 us
  blocking collectives: 177 us -> 100 us
  starting transfers between devices: 12.4 us -> 69.5 us
    dot_general x214 -> x5, matrix products: 883 us -> 5.2 us  [the longest x1 2.54 us: body(): jnp.einsum('ke,nk->en', w_value, x_rim, preferred_element_type=f32)]
    reduce_scatter x5 -> x0, waiting for transfers between devices: 402 us -> none  [the longest x1 166 us: body(): lax.psum_scatter(gw_up, 'seq', scatter_dimension=0, tiled=True)]
    pallas_call x0 -> x22, Pallas kernels: none -> 345 us  [the longest x1 135 us: dense(): pl.pallas_call(functools.partial(dense_kernel, nl, chunk), grid=(nl + ns,...]
    psum x3 -> x0, waiting for transfers between devices: 199 us -> none  [the longest x1 71.7 us: sum_mix(): return lax.psum(partial_mix, 'seq')]
    reduce_sum x24 -> x2, other arithmetic: 161 us -> 2.61 us  [the longest x1 2.51 us: body(): jnp.sum(x_long[0].reshape(items, own_marks, seg, D).astype(f32), axis=2)]
    convert_element_type x13 -> x37, other arithmetic: 98.7 us -> 22.6 us  [the longest x20 8.34 us: reduce_rows(): v = v.astype(bf)]
    unnamed x14 -> x0, waiting for transfers between devices: 61.9 us -> none
    ppermute x4 -> x51, waiting for transfers between devices: 0.01 us -> 57 us  [the longest x47 57 us: swap(): return lax.ppermute(values, axis, [(i, i ^ bit) for i in range(count)])]
  transfers between devices with their start and end apart: 15 -> 54, of which waited for: 7 -> 15; matrix products, arithmetic and copies ran while one was open for 40% -> 14% of each run, Pallas kernels for 0% -> 25%
where the time goes in v1:
time: 696 us; the launch traced here: 687 us
  Pallas kernels  345 us (50%)
  blocking collectives  100 us (14%)
  starting transfers between devices  69.5 us (10%)
  local copies, waits for them, and re-layouts  64.4 us (9%)
  waiting for transfers between devices  57 us (8%)
  other arithmetic  43.1 us (6%)
    pallas_call x1, Pallas kernels, dense(): pl.pallas_call(functools.partial(dense_kernel, nl, chunk), grid=(nl + ns,...  135 us
    all_gather x3, blocking collectives, gather(): return lax.all_gather(values, 'seq', axis=0)  100 us
    ppermute x47, waiting for transfers between devices, swap(): return lax.ppermute(values, axis, [(i, i ^ bit) for i in range(count)])  57 us
    ppermute x47, starting transfers between devices, swap(): return lax.ppermute(values, axis, [(i, i ^ bit) for i in range(count)])  43.7 us
    pallas_call x1, Pallas kernels, back_inverse(): pl.pallas_call(back_inverse_kernel, grid=(units,), in_specs=[spec] * 4, o...  37 us
    pallas_call x1, Pallas kernels, final(): pl.pallas_call(functools.partial(final_kernel, items), grid=(items + 1,),...  32.7 us
    pallas_call x2, Pallas kernels, conv_back(): pl.pallas_call(functools.partial(conv_back_kernel, items, rows, masked),...  23.7 us
    pallas_call x2, Pallas kernels, conv(): pl.pallas_call(functools.partial(conv_kernel, items, rows, masked), grid=...  20 us
  transfers between devices with their start and end apart: 54, of which 15 were waited for; matrix products, arithmetic and copies ran while one was open for 14% of the time, Pallas kernels for 25%

profile of v1, /device:TPU:0, one launch (start us, length us, event | category | flops | bytes accessed | tf_op | source)
XLA Modules:
  0.0 687.4 jit_solution(15110342016479779381)
XLA Ops:
  3.2 33.8 %all-gather = f32[32,8,768]{2,1,0:T(8,128)S(1)} all-gather(f32[4,8,768]{2,1,0:T(8,128)S(1)} %broadcast_multiply_fusion.1), channel_id=2, replica_groups=mesh['dp'=4,'seq'=8] {'seq'}, dimensions={0}, use_global_device_ids=true | all-gather | bytes 884736 | tf_op jit(solution)/shard_map/all_gather | solution.py:889
  40.0 17.2 %qkv.1 = (bf16[768,2048]{1,0:T(8,128)(2,1)}, bf16[768,2048]{1,0:T(8,128)(2,1)}, bf16[768,2048]{1,0:T(8,128)(2,1)}, bf16[768,512]{1,0:T(8,128)(2,1)}, bf16[768,512]{1,0:T(8,128)(2,1)}, /*index=5*/bf16[768,512]{1,0:T(8,128)(2,1)}) custom-call(bf16[2048,768]{1,0:T(8,128)(2,1)} %bitcast.331, bf16[512,768]{1,0:T(8,128)(2,1)} %bitcast.380, bf16[768,768]{1,0:T(8,128)(2,1)} %wq.3, ...), custom_call_target="tpu_custom_call" | custom-call | flops 9059696640 | bytes 15728640 | tf_op jit(solution)/shard_map/qkv/pallas_call | solution.py:137
  57.2 7.3 %stats.2 = f32[8,72,384]{2,1,0:T(8,128)} custom-call(s32[1]{0:T(128)} %constant.440.clone.1.length, bf16[256,768]{1,0:T(8,128)(2,1)} %fusion.5.lq.lq_l, bf16[768,2048]{1,0:T(8,128)(2,1)} %get-tuple-element.67.k, bf16[768,2048]{1,0:T(8,128)(2,1)} %get-tuple-element.68.v), custom_call_target="tpu_custom_call" | custom-call | flops 1610612736 | bytes 6291456 | tf_op jit(solution)/shard_map/stats/pallas_call | solution.py:205
  64.5 5.7 all-to-all-start
  71.9 4.7 collective-permute-start.1
  85.1 14.1 %inverse.1 = f32[3,64,384]{2,1,0:T(8,128)} custom-call(bf16[3,64,384]{2,1,0:T(8,128)(2,1)} %pad_maximum_fusion.5.lq, bf16[3,64,384]{2,1,0:T(8,128)(2,1)} %pad_maximum_fusion.6.lk), custom_call_target="tpu_custom_call" | custom-call | flops 10871635968 | bytes 1000000 | tf_op jit(solution)/shard_map/inverse/pallas_call | solution.py:263
  113.6 8.6 %conv.3 = f32[768,512]{1,0:T(8,128)} custom-call(s32[1]{0:T(128)} %bitcast.317.length, bf16[768,512]{1,0:T(8,128)(2,1)} %get-tuple-element.75.v, bf16[768,32]{1,0:T(8,128)(2,1)} %broadcast_in_dim.48.rim.up_rim, f32[12,8,128]{2,1,0:T(8,128)} %select_maximum_fusion.taps), custom_call_target="tpu_custom_call" | custom-call | flops 805306368 | bytes 2359296 | tf_op jit(solution)/shard_map/conv/pallas_call | solution.py:384
  122.2 4.0 mix.3.o_s
  128.9 11.4 %conv.2 = f32[768,2048]{1,0:T(8,128)} custom-call(s32[1]{0:T(128)} %constant.440.clone.1.length, bf16[768,2048]{1,0:T(8,128)(2,1)} %get-tuple-element.68.v, bf16[768,128]{1,0:T(8,128)(2,1)} %fusion.12.rim, f32[12,8,128]{2,1,0:T(8,128)} %select_maximum_fusion.taps), custom_call_target="tpu_custom_call" | custom-call | flops 3221225472 | bytes 9437184 | tf_op jit(solution)/shard_map/conv/pallas_call | solution.py:384
  143.3 33.3 %all_gather.11.w = bf16[8,80,384]{2,1,0:T(8,128)(2,1)} all-gather(bf16[1,80,384]{2,1,0:T(8,128)(2,1)} %get-tuple-element.73), channel_id=1, replica_groups=mesh['dp'=4,'seq'=8] {'seq'}, dimensions={0}, use_global_device_ids=true | all-gather | bytes 552960 | tf_op jit(solution)/shard_map/all_gather | solution.py:889
  176.6 8.9 %mix.2.o_l = bf16[768,2048]{1,0:T(8,128)(2,1)} custom-call(bf16[256,768]{1,0:T(8,128)(2,1)} %copy-done.14, bf16[8,80,384]{2,1,0:T(8,128)(2,1)} %all_gather.11.w, bf16[768,2048]{1,0:T(8,128)(2,1)} %get-tuple-element.74.q, f32[768,2048]{1,0:T(8,128)} %conv.2), custom_call_target="tpu_custom_call" | custom-call | flops 1610612736 | bytes 12582912 | tf_op jit(solution)/shard_map/mix/pallas_call | solution.py:331
  185.5 134.7 %dense.1 = (bf16[2048,768]{1,0:T(8,128)(2,1)}, bf16[512,768]{1,0:T(8,128)(2,1)}, f32[2048,768]{1,0:T(8,128)}, f32[512,768]{1,0:T(8,128)}, bf16[768,2048]{1,0:T(8...) custom-call(bf16[2048,768]{1,0:T(8,128)(2,1)} %bitcast.332, ...), custom_call_target="tpu_custom_call" | custom-call | flops 81537269760 | bytes 60000000 | tf_op jit(solution)/shard_map/dense/pallas_call | solution.py:553
  324.0 4.9 collective-permute-start.3
  329.0 4.9 constant_dynamic-slice_fusion.1
  334.9 9.9 %conv_back.3 = (f32[768,512]{1,0:T(8,128)}, f32[12,8,128]{2,1,0:T(8,128)}) custom-call(s32[1]{0:T(128)} %bitcast.318.length, bf16[768,512]{1,0:T(8,128)(2,1)} %get-tuple-element.75.v, bf16[768,32]{1,0:T(8,128)(2,1)} %broadcast_in_dim.48.rim.up_rim, bf16[768,512]{1,0:T(8,128)(2,1)} %get-tuple-element.90.up, bf16[768,32]{1,0:T(8,128)(2,1)} %broadcast_in_dim.48.rim.up_rim, ...), custom_call_target="tpu_custom_call" | custom-call | flops 1207959552 | bytes 3145728 | tf_op jit(solution)/shard_map/conv_back/pallas_call | solution.py:424
  345.8 13.8 %conv_back.2 = (f32[768,2048]{1,0:T(8,128)}, f32[12,8,128]{2,1,0:T(8,128)}) custom-call(s32[1]{0:T(128)} %constant.440.clone.1.length, bf16[768,2048]{1,0:T(8,128)(2,1)} %get-tuple-element.68.v, bf16[768,128]{1,0:T(8,128)(2,1)} %fusion.12.rim, bf16[768,2048]{1,0:T(8,128)(2,1)} %get-tuple-element.80.up, bf16[768,128]{1,0:T(8,128)(2,1)} %bitcast.363, ...), custom_call_target="tpu_custom_call" | custom-call | flops 4831838208 | bytes 12582912 | tf_op jit(solution)/shard_map/conv_back/pallas_call | solution.py:424
  361.0 8.6 %back_f.2 = (f32[8,64,384]{2,1,0:T(8,128)}, f32[256,768]{1,0:T(8,128)}, bf16[768,2048]{1,0:T(8,128)(2,1)}) custom-call(bf16[256,768]{1,0:T(8,128)(2,1)} %copy-done.14, bf16[8,80,384]{2,1,0:T(8,128)(2,1)} %all_gather.11.w, bf16[768,2048]{1,0:T(8,128)(2,1)} %get-tuple-element.74.q, bf16[768,2048]{1,0:T(8,128)(2,1)} %get-tuple-element.80.up), custom_call_target="tpu_custom_call" | custom-call | flops 3221225472 | bytes 9437184 | tf_op jit(solution)/shard_map/back_f/pallas_call | solution.py:607
  369.7 4.3 copy.148
  380.3 6.3 all-to-all-start.1
  396.3 3.9 back_f.3
  409.9 4.7 back_b.3
  414.6 4.3 copy.172
  437.4 37.0 %back_inverse.1 = (f32[3,64,384]{2,1,0:T(8,128)}, f32[3,64,384]{2,1,0:T(8,128)}) custom-call(bf16[3,64,384]{2,1,0:T(8,128)(2,1)} %pad_maximum_fusion.5.lq, bf16[3,64,384]{2,1,0:T(8,128)(2,1)} %pad_maximum_fusion.6.lk, f32[3,64,384]{2,1,0:T(8,128)} %pad_maximum_fusion.1.dw, f32[3,64,384]{2,1,0:T(8,128)} %pad_maximum_fusion.2.bv), custom_call_target="tpu_custom_call" | custom-call | flops 32614907904 | bytes 2000000 | tf_op jit(solution)/shard_map/back_inverse/pallas_call | solution.py:683
  478.1 33.2 %all_gather.12.dbv = bf16[8,80,384]{2,1,0:T(8,128)(2,1)} all-gather(bf16[1,80,384]{2,1,0:T(8,128)(2,1)S(1)} %copy-done.21), channel_id=1, replica_groups=mesh['dp'=4,'seq'=8] {'seq'}, dimensions={0}, use_global_device_ids=true | all-gather | bytes 552960 | tf_op jit(solution)/shard_map/all_gather | solution.py:889
  511.5 10.6 %back_b.2 = (bf16[768,2048]{1,0:T(8,128)(2,1)}, bf16[768,2048]{1,0:T(8,128)(2,1)}, f32[256,768]{1,0:T(8,128)}) custom-call(s32[1]{0:T(128)} %constant.440.clone.1.length, bf16[256,768]{1,0:T(8,128)(2,1)} %fusion.5.lq.lq_l, bf16[8,80,384]{2,1,0:T(8,128)(2,1)} %all_gather.11.w, bf16[8,80,384]{2,1,0:T(8,128)(2,1)} %all_gather.12.dbv, ...), custom_call_target="tpu_custom_call" | custom-call | flops 4026531840 | bytes 18874368 | tf_op jit(solution)/shard_map/back_b/pallas_call | solution.py:717
  524.7 3.9 all-to-all-start.2
  545.1 32.7 %final.1 = (bf16[2048,768]{1,0:T(8,128)(2,1)}, bf16[512,768]{1,0:T(8,128)(2,1)}, bf16[768,768]{1,0:T(8,128)(2,1)}, bf16[768,768]{1,0:T(8,128)(2,1)}, bf16[768,768]{1,0:T(8,128)(2,1)}) custom-call(s32[1]{0:T(128)} %bitcast.320.length, bf16[2048,768]{1,0:T(8,128)(2,1)} %bitcast.333, f32[2048,768]{1,0:T(8,128)} %get-tuple-element.79.dr_l, ...), custom_call_target="tpu_custom_call" | custom-call | flops 18119393280 | bytes 39321600 | tf_op jit(solution)/shard_map/final/pallas_call | solution.py:787
  582.1 4.3 constant_dynamic-slice_fusion.2
  599.5 17.3 %collective-permute-done.38 = bf16[2,2,2,48,1536]{4,3,2,1,0:T(8,128)(2,1)} collective-permute-done((bf16[2,2,2,48,1536]{4,3,2,1,0:T(8,128)(2,1)}, bf16[2,2,2,48,1536]{4,3,2,1,0:T(8,128)(2,1)}, u32[]{:S(2)}, u32[]{:S(2)}) %collective-permute-start.38) | collective-permute-done | bytes 1179680 | tf_op jit(solution)/shard_map/ppermute | solution.py:813
  630.4 5.1 collective-permute-done.6
  654.6 6.2 collective-permute-done.47
  664.7 9.6 %collective-permute-done.48 = bf16[192,384]{1,0:T(8,128)(2,1)S(1)} collective-permute-done((bf16[192,384]{1,0:T(8,128)(2,1)S(1)}, bf16[192,384]{1,0:T(8,128)(2,1)S(1)}, u32[]{:S(2)}, u32[]{:S(2)}) %collective-permute-start.48) | collective-permute-done | bytes 147488 | tf_op jit(solution)/shard_map/ppermute | solution.py:813
  (332 shorter events, 175.3 us)
Async XLA Ops:
  64.5 75.8 %all-to-all-start = ((f32[8,72,384]{2,1,0:T(8,128)}), f32[8,72,384]{2,1,0:T(8,128)}, u32[]{:S(2)}, u32[]{:S(2)}) async-start(f32[8,72,384]{2,1,0:T(8,128)} %stats.2), calls=%async_computation | async-start | bytes 1769472 | tf_op jit(solution)/shard_map/all_to_all | solution.py:893
  71.9 54.3 %collective-permute-start.1 = (bf16[4,16,768]{2,1,0:T(8,128)(2,1)}, bf16[4,16,768]{2,1,0:T(8,128)(2,1)S(1)}, u32[]{:S(2)}, u32[]{:S(2)}) collective-permute-start(bf16[4,16,768]{2,1,0:T(8,128)(2,1)} %get-tuple-element.194), channel_id=1, source_target_pairs={{1,0},{2,1},{3,2},{4,3},{5,4},{6,5},{7,6},{0,7},{9,8},{10,9},{11,1... | collective-permute-start | bytes 294920 | tf_op jit(solution)/shard_map/ppermute | solution.py:898
  76.6 49.6 %collective-permute-start = (bf16[4,16,768]{2,1,0:T(8,128)(2,1)}, bf16[4,16,768]{2,1,0:T(8,128)(2,1)S(1)}, u32[]{:S(2)}, u32[]{:S(2)}) collective-permute-start(bf16[4,16,768]{2,1,0:T(8,128)(2,1)} %get-tuple-element.193), channel_id=1, source_target_pairs={{0,1},{1,2},{2,3},{3,4},{4,5},{5,6},{6,7},{7,0},{8,9},{9,10},{10,1... | collective-permute-start | bytes 294920 | tf_op jit(solution)/shard_map/ppermute | solution.py:899
  324.0 20.8 %collective-permute-start.3 = (bf16[4,16,768]{2,1,0:T(8,128)(2,1)}, bf16[4,16,768]{2,1,0:T(8,128)(2,1)S(1)}, u32[]{:S(2)}, u32[]{:S(2)}) collective-permute-start(bf16[4,16,768]{2,1,0:T(8,128)(2,1)} %get-tuple-element.192), channel_id=1, source_target_pairs={{1,0},{2,1},{3,2},{4,3},{5,4},{6,5},{7,6},{0,7},{9,8},{10,9},{11,1... | collective-permute-start | bytes 294920 | tf_op jit(solution)/shard_map/ppermute | solution.py:898
  328.9 16.0 %collective-permute-start.2 = (bf16[4,16,768]{2,1,0:T(8,128)(2,1)S(1)}, bf16[4,16,768]{2,1,0:T(8,128)(2,1)S(1)}, u32[]{:S(2)}, u32[]{:S(2)}) collective-permute-start(bf16[4,16,768]{2,1,0:T(8,128)(2,1)S(1)} %get-tuple-element.191), channel_id=1, source_target_pairs={{0,1},{1,2},{2,3},{3,4},{4,5},{5,6},{6,7},{7,0},{8,9},{9,10},{10,1... | collective-permute-start | bytes 294920 | tf_op jit(solution)/shard_map/ppermute | solution.py:899
  334.9 40.7 %collective-permute-start.25 = (bf16[2,2,2,48,768]{4,3,2,0,1:T(8,128)(2,1)}, bf16[2,2,2,48,768]{4,3,2,0,1:T(8,128)(2,1)}, u32[]{:S(2)}, u32[]{:S(2)}) collective-permute-start(bf16[2,2,2,48,768]{4,3,2,0,1:T(8,128)(2,1)} %bitcast.304), channel_id=1, source_target_pairs={{0,8},{8,0},{16,24},{24,16},{1,9},{9,1},{17,25},{25,17},{2,10},{10... | collective-permute-start | bytes 1769480 | tf_op jit(solution)/shard_map/ppermute | solution.py:813
  360.5 13.5 %collective-permute-start.32 = (f32[72,128]{1,0:T(8,128)S(1)}, f32[72,128]{1,0:T(8,128)S(1)}, u32[]{:S(2)}, u32[]{:S(2)}) collective-permute-start(f32[72,128]{1,0:T(8,128)S(1)} %maximum_bitcast_fusion), channel_id=1, source_target_pairs={{0,8},{8,0},{16,24},{24,16},{1,9},{9,1},{17,25},{25,17},{2,10},{10... | collective-permute-start | bytes 110600 | tf_op jit(solution)/shard_map/ppermute | solution.py:813
  373.9 157.9 %collective-permute-start.44 = (bf16[384,3072]{0,1:T(8,128)(2,1)}, bf16[384,3072]{0,1:T(8,128)(2,1)}, u32[]{:S(2)}, u32[]{:S(2)}) collective-permute-start(bf16[384,3072]{0,1:T(8,128)(2,1)} %bitcast.103), channel_id=1, source_target_pairs={{0,8},{8,0},{16,24},{24,16},{1,9},{9,1},{17,25},{25,17},{2,10},{10... | collective-permute-start | bytes 7077896 | tf_op jit(solution)/shard_map/ppermute | solution.py:813
  374.0 12.7 %collective-permute-start.33 = (f32[72,128]{1,0:T(8,128)S(1)}, f32[72,128]{1,0:T(8,128)S(1)}, u32[]{:S(2)}, u32[]{:S(2)}) collective-permute-start(f32[72,128]{1,0:T(8,128)S(1)} %fusion.54), channel_id=1, source_target_pairs={{0,16},{8,24},{16,0},{24,8},{1,17},{9,25},{17,1},{25,9},{2,18},{10... | collective-permute-start | bytes 110600 | tf_op jit(solution)/shard_map/ppermute | solution.py:813
  376.8 12.0 %collective-permute-start.26 = (bf16[2,2,48,768]{3,2,1,0:T(8,128)(2,1)S(1)}, bf16[2,2,48,768]{3,2,1,0:T(8,128)(2,1)S(1)}, u32[]{:S(2)}, u32[]{:S(2)}) collective-permute-start(bf16[2,2,48,768]{3,2,1,0:T(8,128)(2,1)S(1)} %dynamic-slice_bitcast_fusion.7), channel_id=1, source_target_pairs={{0,2},{1,3},{2,0},{3,1},{4,6},{5,7},{6,4},{7,5},{8,10},{9,11},{10,... | collective-permute-start | bytes 884744 | tf_op jit(solution)/shard_map/ppermute | solution.py:813
  380.1 157.8 %collective-permute-start.37 = (bf16[2,2,2,48,3072]{4,3,2,1,0:T(8,128)(2,1)}, bf16[2,2,2,48,3072]{4,3,2,1,0:T(8,128)(2,1)}, u32[]{:S(2)}, u32[]{:S(2)}) collective-permute-start(bf16[2,2,2,48,3072]{4,3,2,1,0:T(8,128)(2,1)} %dynamic-slice_bitcast_fusion), channel_id=1, source_target_pairs={{0,8},{8,0},{16,24},{24,16},{1,9},{9,1},{17,25},{25,17},{2,10},{10... | collective-permute-start | bytes 7077896 | tf_op jit(solution)/shard_map/ppermute | solution.py:813
  380.3 51.8 %all-to-all-start.1 = ((f32[8,64,384]{2,1,0:T(8,128)}), f32[8,64,384]{2,1,0:T(8,128)S(1)}, u32[]{:S(2)}, u32[]{:S(2)}) async-start(f32[8,64,384]{2,1,0:T(8,128)} %get-tuple-element.82), calls=%async_computation.1 | async-start | bytes 1572864 | tf_op jit(solution)/shard_map/all_to_all | solution.py:893
  390.9 14.8 %collective-permute-start.27 = (bf16[2,2,48,384]{3,2,0,1:T(8,128)(2,1)}, bf16[2,2,48,384]{3,2,0,1:T(8,128)(2,1)}, u32[]{:S(2)}, u32[]{:S(2)}) collective-permute-start(bf16[2,2,48,384]{3,2,0,1:T(8,128)(2,1)} %bitcast.308), channel_id=1, source_target_pairs={{0,16},{8,24},{16,0},{24,8},{1,17},{9,25},{17,1},{25,9},{2,18},{10... | collective-permute-start | bytes 442376 | tf_op jit(solution)/shard_map/ppermute | solution.py:813
  403.5 15.4 %collective-permute-start.36 = (f32[72,128]{1,0:T(8,128)S(1)}, f32[72,128]{1,0:T(8,128)}, u32[]{:S(2)}, u32[]{:S(2)}) collective-permute-start(f32[72,128]{1,0:T(8,128)S(1)} %add.387), channel_id=1, source_target_pairs={{0,4},{1,5},{2,6},{3,7},{4,0},{5,1},{6,2},{7,3},{8,12},{9,13},{10,... | collective-permute-start | bytes 110600 | tf_op jit(solution)/shard_map/ppermute | solution.py:813
  407.4 12.3 %collective-permute-start.28 = (bf16[2,48,384]{2,1,0:T(8,128)(2,1)}, bf16[2,48,384]{2,1,0:T(8,128)(2,1)}, u32[]{:S(2)}, u32[]{:S(2)}) collective-permute-start(bf16[2,48,384]{2,1,0:T(8,128)(2,1)} %dynamic-slice_bitcast_fusion.14), channel_id=1, source_target_pairs={{0,1},{1,0},{2,3},{3,2},{4,5},{5,4},{6,7},{7,6},{8,9},{9,8},{10,11... | collective-permute-start | bytes 221192 | tf_op jit(solution)/shard_map/ppermute | solution.py:813
  524.7 19.5 %all-to-all-start.2 = ((bf16[8,8,8,768]{3,2,1,0:T(8,128)(2,1)}), bf16[8,8,8,768]{3,2,1,0:T(8,128)(2,1)S(1)}, u32[]{:S(2)}, u32[]{:S(2)}) async-start(bf16[8,8,8,768]{3,2,1,0:T(8,128)(2,1)} %copy.131), calls=%async_computation.2 | async-start | bytes 1572864 | tf_op jit(solution)/shard_map/all_to_all | solution.py:893
  536.0 60.7 %collective-permute-start.45 = (bf16[384,2,2,384]{0,3,2,1:T(8,128)(2,1)}, bf16[384,2,2,384]{0,3,2,1:T(8,128)(2,1)}, u32[]{:S(2)}, u32[]{:S(2)}) collective-permute-start(bf16[384,2,2,384]{0,3,2,1:T(8,128)(2,1)} %dynamic-slice_bitcast_fusion.1), channel_id=1, source_target_pairs={{0,1},{1,0},{2,3},{3,2},{4,5},{5,4},{6,7},{7,6},{8,9},{9,8},{10,11... | collective-permute-start | bytes 3538952 | tf_op jit(solution)/shard_map/ppermute | solution.py:813
  580.6 10.1 %collective-permute-start.11 = (bf16[2,2,2,48,768]{4,3,0,1,2:T(8,128)(2,1)S(1)}, bf16[2,2,2,48,768]{4,3,0,1,2:T(8,128)(2,1)S(1)}, u32[]{:S(2)}, u32[]{:S(2)}) collective-permute-start(bf16[2,2,2,48,768]{4,3,0,1,2:T(8,128)(2,1)S(1)} %bitcast.357), channel_id=1, source_target_pairs={{0,8},{8,0},{16,24},{24,16},{1,9},{9,1},{17,25},{25,17},{2,10},{10... | collective-permute-start | bytes 1769480 | tf_op jit(solution)/shard_map/ppermute | solution.py:813
  587.6 29.2 %collective-permute-start.38 = (bf16[2,2,2,48,1536]{4,3,2,1,0:T(8,128)(2,1)}, bf16[2,2,2,48,1536]{4,3,2,1,0:T(8,128)(2,1)}, u32[]{:S(2)}, u32[]{:S(2)}) collective-permute-start(bf16[2,2,2,48,1536]{4,3,2,1,0:T(8,128)(2,1)} %bitcast.303), channel_id=1, source_target_pairs={{0,16},{8,24},{16,0},{24,8},{1,17},{9,25},{17,1},{25,9},{2,18},{10... | collective-permute-start | bytes 3538952 | tf_op jit(solution)/shard_map/ppermute | solution.py:813
  589.2 30.3 %collective-permute-start.19 = (bf16[2,2,48,768]{3,2,1,0:T(8,128)(2,1)}, bf16[2,2,48,768]{3,2,1,0:T(8,128)(2,1)}, u32[]{:S(2)}, u32[]{:S(2)}) collective-permute-start(bf16[2,2,48,768]{3,2,1,0:T(8,128)(2,1)} %dynamic-slice_bitcast_fusion.8), channel_id=1, source_target_pairs={{0,2},{1,3},{2,0},{3,1},{4,6},{5,7},{6,4},{7,5},{8,10},{9,11},{10,... | collective-permute-start | bytes 884744 | tf_op jit(solution)/shard_map/ppermute | solution.py:813
  591.6 30.5 %collective-permute-start.12 = (bf16[2,2,48,768]{3,2,0,1:T(8,128)(2,1)}, bf16[2,2,48,768]{3,2,0,1:T(8,128)(2,1)}, u32[]{:S(2)}, u32[]{:S(2)}) collective-permute-start(bf16[2,2,48,768]{3,2,0,1:T(8,128)(2,1)} %dynamic-slice_bitcast_fusion.9), channel_id=1, source_target_pairs={{0,1},{1,0},{2,3},{3,2},{4,5},{5,4},{6,7},{7,6},{8,9},{9,8},{10,11... | collective-permute-start | bytes 884744 | tf_op jit(solution)/shard_map/ppermute | solution.py:813
  595.2 29.7 %collective-permute-start.5 = (bf16[2,2,2,48,384]{4,3,2,1,0:T(8,128)(2,1)}, bf16[2,2,2,48,384]{4,3,2,1,0:T(8,128)(2,1)}, u32[]{:S(2)}, u32[]{:S(2)}) collective-permute-start(bf16[2,2,2,48,384]{4,3,2,1,0:T(8,128)(2,1)} %bitcast.307), channel_id=1, source_target_pairs={{0,16},{8,24},{16,0},{24,8},{1,17},{9,25},{17,1},{25,9},{2,18},{10... | collective-permute-start | bytes 884744 | tf_op jit(solution)/shard_map/ppermute | solution.py:813
  599.3 50.4 %collective-permute-start.46 = (bf16[384,2,384]{0,2,1:T(8,128)(2,1)}, bf16[384,2,384]{0,2,1:T(8,128)(2,1)}, u32[]{:S(2)}, u32[]{:S(2)}) collective-permute-start(bf16[384,2,384]{0,2,1:T(8,128)(2,1)} %dynamic-slice_bitcast_fusion.2), channel_id=1, source_target_pairs={{0,2},{1,3},{2,0},{3,1},{4,6},{5,7},{6,4},{7,5},{8,10},{9,11},{10,... | collective-permute-start | bytes 1769480 | tf_op jit(solution)/shard_map/ppermute | solution.py:813
  619.3 33.6 %collective-permute-start.39 = (bf16[2,2,48,1536]{3,2,1,0:T(8,128)(2,1)}, bf16[2,2,48,1536]{3,2,1,0:T(8,128)(2,1)}, u32[]{:S(2)}, u32[]{:S(2)}) collective-permute-start(bf16[2,2,48,1536]{3,2,1,0:T(8,128)(2,1)} %dynamic-slice_bitcast_fusion.3), channel_id=1, source_target_pairs={{0,1},{1,0},{2,3},{3,2},{4,5},{5,4},{6,7},{7,6},{8,9},{9,8},{10,11... | collective-permute-start | bytes 1769480 | tf_op jit(solution)/shard_map/ppermute | solution.py:813
  625.9 9.6 %collective-permute-start.6 = (bf16[2,2,48,384]{3,2,1,0:T(8,128)(2,1)S(1)}, bf16[2,2,48,384]{3,2,1,0:T(8,128)(2,1)S(1)}, u32[]{:S(2)}, u32[]{:S(2)}) collective-permute-start(bf16[2,2,48,384]{3,2,1,0:T(8,128)(2,1)S(1)} %dynamic-slice_bitcast_fusion.13), channel_id=1, source_target_pairs={{0,1},{1,0},{2,3},{3,2},{4,5},{5,4},{6,7},{7,6},{8,9},{9,8},{10,11... | collective-permute-start | bytes 442376 | tf_op jit(solution)/shard_map/ppermute | solution.py:813
  627.6 9.6 %collective-permute-start.21 = (bf16[2,48,384]{2,1,0:T(8,128)(2,1)S(1)}, bf16[2,48,384]{2,1,0:T(8,128)(2,1)S(1)}, u32[]{:S(2)}, u32[]{:S(2)}) collective-permute-start(bf16[2,48,384]{2,1,0:T(8,128)(2,1)S(1)} %dynamic-slice_bitcast_fusion.15), channel_id=1, source_target_pairs={{0,1},{1,0},{2,3},{3,2},{4,5},{5,4},{6,7},{7,6},{8,9},{9,8},{10,11... | collective-permute-start | bytes 221192 | tf_op jit(solution)/shard_map/ppermute | solution.py:813
  628.9 10.7 %collective-permute-start.14 = (bf16[2,48,384]{2,1,0:T(8,128)(2,1)S(1)}, bf16[2,48,384]{2,1,0:T(8,128)(2,1)S(1)}, u32[]{:S(2)}, u32[]{:S(2)}) collective-permute-start(bf16[2,48,384]{2,1,0:T(8,128)(2,1)S(1)} %bitcast.374), channel_id=1, source_target_pairs={{0,16},{8,24},{16,0},{24,8},{1,17},{9,25},{17,1},{25,9},{2,18},{10... | collective-permute-start | bytes 221192 | tf_op jit(solution)/shard_map/ppermute | solution.py:813
  647.2 31.0 %collective-permute-start.24 = (bf16[48,768]{1,0:T(8,128)(2,1)S(1)}, bf16[48,768]{1,0:T(8,128)(2,1)S(1)}, u32[]{:S(2)}, u32[]{:S(2)}) collective-permute-start(bf16[48,768]{1,0:T(8,128)(2,1)S(1)} %maximum_select_fusion.10), channel_id=1, source_target_pairs={{0,8},{8,0},{16,24},{24,16},{1,9},{9,1},{17,25},{25,17},{2,10},{10... | collective-permute-start | bytes 221192 | tf_op jit(solution)/shard_map/ppermute | solution.py:813
  649.1 33.8 %collective-permute-start.17 = (bf16[48,768]{1,0:T(8,128)(2,1)S(1)}, bf16[48,768]{1,0:T(8,128)(2,1)S(1)}, u32[]{:S(2)}, u32[]{:S(2)}) collective-permute-start(bf16[48,768]{1,0:T(8,128)(2,1)S(1)} %maximum_select_fusion.9), channel_id=1, source_target_pairs={{0,8},{8,0},{16,24},{24,16},{1,9},{9,1},{17,25},{25,17},{2,10},{10... | collective-permute-start | bytes 221192 | tf_op jit(solution)/shard_map/ppermute | solution.py:813
  649.7 33.9 %collective-permute-start.10 = (bf16[48,768]{1,0:T(8,128)(2,1)S(1)}, bf16[48,768]{1,0:T(8,128)(2,1)S(1)}, u32[]{:S(2)}, u32[]{:S(2)}) collective-permute-start(bf16[48,768]{1,0:T(8,128)(2,1)S(1)} %maximum_select_fusion.8), channel_id=1, source_target_pairs={{0,8},{8,0},{16,24},{24,16},{1,9},{9,1},{17,25},{25,17},{2,10},{10... | collective-permute-start | bytes 221192 | tf_op jit(solution)/shard_map/ppermute | solution.py:813
  660.9 13.3 %collective-permute-start.48 = (bf16[192,384]{1,0:T(8,128)(2,1)S(1)}, bf16[192,384]{1,0:T(8,128)(2,1)S(1)}, u32[]{:S(2)}, u32[]{:S(2)}) collective-permute-start(bf16[192,384]{1,0:T(8,128)(2,1)S(1)} %dynamic-slice_bitcast_fusion.10), channel_id=1, source_target_pairs={{0,4},{1,5},{2,6},{3,7},{4,0},{5,1},{6,2},{7,3},{8,12},{9,13},{10,... | collective-permute-start | bytes 442376 | tf_op jit(solution)/shard_map/ppermute | solution.py:813
  663.4 13.4 %collective-permute-start.41 = (bf16[48,1536]{1,0:T(8,128)(2,1)S(1)}, bf16[48,1536]{1,0:T(8,128)(2,1)S(1)}, u32[]{:S(2)}, u32[]{:S(2)}) collective-permute-start(bf16[48,1536]{1,0:T(8,128)(2,1)S(1)} %dynamic-slice_bitcast_fusion.11), channel_id=1, source_target_pairs={{0,4},{1,5},{2,6},{3,7},{4,0},{5,1},{6,2},{7,3},{8,12},{9,13},{10,... | collective-permute-start | bytes 442376 | tf_op jit(solution)/shard_map/ppermute | solution.py:813
  (57 other events, 443.6 us)

commit v2 on v1

v2 whole, which is shorter than its diff:
```python
import functools

import jax
import jax.numpy as jnp
from jax import lax
from jax.experimental import pallas as pl
from jax.experimental.pallas import tpu as pltpu
from jax.sharding import PartitionSpec as P

D = 768
H = 12
HD = 64
FF = 3072
LM = 64
NS_STEPS = 6
HALF = 16
TAPS = 33
LONG = 4096
GROUP = 256
EPSILON = 1e-05
MASKED_SCORE = -1e30
SCALE = 0.125
VMEM_BYTES = 63 * 1024 * 1024

f32 = jnp.float32
bf = jnp.bfloat16
sds = jax.ShapeDtypeStruct


def dot(a, b, ca, cb):
    return lax.dot_general(a, b, (((ca,), (cb,)), ((), ())), preferred_element_type=f32)


def split(v):
    hi = v.astype(bf)
    return hi, (v - hi.astype(f32)).astype(bf)


def mm(a, b, ca=1, cb=0):
    ah, al = split(a)
    bh, bl = split(b)
    return dot(ah, bh, ca, cb) + (dot(ah, bl, ca, cb) + dot(al, bh, ca, cb))


def iota(shape, dim):
    return lax.broadcasted_iota(jnp.int32, shape, dim)


def spread_heads(block):
    tiled = jnp.concatenate([block.astype(f32)] * 4, axis=0)
    same = (iota((GROUP, GROUP), 0) // HD) == (iota((GROUP, GROUP), 1) // HD)
    return jnp.where(same, tiled, 0.0).astype(bf)


def pick_heads(full):
    head = iota((LM, GROUP), 1) // HD
    out = full[:LM]
    for h in range(1, 4):
        out = jnp.where(head == h, full[h * LM : (h + 1) * LM], out)
    return out


def lanes_of(columns):
    n = columns[0].shape[0]
    lane = iota((n, 128), 1)
    wide = jnp.zeros((n, 128), f32)
    for k, col in enumerate(columns):
        wide = jnp.where(lane == k, col, wide)
    return wide.T[:8]


def three_parts(row):
    hi = row.astype(bf).astype(f32)
    mid = (row - hi).astype(bf).astype(f32)
    low = row - hi - mid
    r = iota((16, row.shape[1]), 0)
    return jnp.where(r == 0, hi, jnp.where(r == 1, mid, jnp.where(r == 2, low, 0.0))).astype(bf)


def from_parts(rows):
    v = rows.astype(f32)
    total = v[0:1] + v[1:2] + v[2:3]
    return jnp.broadcast_to(total, (8, total.shape[1])).T[:, 0:1]


def head_softmax(scores):
    rows = scores.shape[1]
    s3 = scores.reshape(4, LM, rows)
    e = jnp.exp(s3 - jnp.max(s3, axis=1, keepdims=True))
    return (e / jnp.sum(e, axis=1, keepdims=True)).reshape(GROUP, rows)


def params(vmem=VMEM_BYTES):
    return pltpu.CompilerParams(vmem_limit_bytes=vmem)


def cost(flops, nbytes, trans=0):
    return pl.CostEstimate(flops=int(flops), bytes_accessed=int(nbytes), transcendentals=int(trans))


SMEM_SPEC = pl.BlockSpec(memory_space=pltpu.SMEM)
ANY_SPEC = pl.BlockSpec(memory_space=pl.ANY)


def after(kernel, count, deps):
    return lambda *refs: kernel(*refs[:count], *refs[count + len(deps) :])


def const_spec(shape):
    return pl.BlockSpec(shape, lambda i: tuple(0 for _ in shape), pipeline_mode=pl.Buffered(1))


def short_member(length, rows):
    seg = length // LM
    lm = iota((LM, rows), 0)
    pos = iota((LM, rows), 1)
    return ((pos >= lm * seg) & (pos < (lm + 1) * seg)).astype(f32)


def qkv_kernel(n_long, length, x_l, x_s, wq, wk, wv, q_l, k_l, v_l, q_s, k_s, v_s, lq, lk, w_t):
    i = pl.program_id(0)

    @pl.when(i == 0)
    def _():
        for j, w in enumerate((wq, wk, wv)):
            w_t[j] = w[...].T

    x = jnp.where(i < n_long, x_l[...], x_s[...])
    made = [dot(w_t[j], x, 1, 1).astype(bf) for j in range(3)]

    @pl.when(i < n_long)
    def _():
        for ref, v in zip((q_l, k_l, v_l), made):
            ref[...] = v

    @pl.when(i >= n_long)
    def _():
        for ref, v in zip((q_s, k_s, v_s), made):
            ref[...] = v
        member = short_member(length[0], made[0].shape[1]).astype(bf)
        count = (length[0] // LM).astype(f32)
        lq[...] = (dot(member, made[0], 1, 1) / count).astype(bf)
        lk[...] = (dot(member, made[1], 1, 1) / count).astype(bf)


def qkv(length, x_l, x_s, wq, wk, wv):
    tile = x_s.shape[0]
    nl = x_l.shape[0] // tile
    long_at = lambda i: jnp.minimum(i, nl - 1)
    row = lambda f: pl.BlockSpec((tile, D), lambda i: (f(i), 0))
    col = lambda f: pl.BlockSpec((D, tile), lambda i: (0, f(i)))
    first = lambda i: 0
    tl, ts = x_l.shape[0], x_s.shape[0]
    return pl.pallas_call(
        functools.partial(qkv_kernel, nl),
        grid=(nl + 1,),
        in_specs=[SMEM_SPEC, row(long_at), row(first)] + [const_spec((D, D))] * 3,
        out_specs=[col(long_at)] * 3 + [col(first)] * 3 + [pl.BlockSpec((LM, D), lambda i: (0, 0))] * 2,
        out_shape=[sds((D, tl), bf)] * 3 + [sds((D, ts), bf)] * 3 + [sds((LM, D), bf)] * 2,
        scratch_shapes=[pltpu.VMEM((3, D, D), bf)],
        compiler_params=params(),
        cost_estimate=cost(6 * (tl + ts) * D * D, 8 * (tl + ts) * D),
        name="qkv",
    )(length, x_l, x_s, wq, wk, wv)


def mark_scores(lq_g, k_g, limit):
    scores = dot(spread_heads(lq_g * SCALE), k_g, 1, 0)
    if limit is not None:
        scores = jnp.where(iota(scores.shape, 1) < limit, scores, MASKED_SCORE)
    return scores


def group_slices():
    return [slice(g * GROUP, (g + 1) * GROUP) for g in range(3)]


def stats_kernel(units, lq, k, v, msg):
    sums, stats = [], []
    for gs in group_slices():
        scores = mark_scores(lq[:, gs], k[gs, :], None)
        most = jnp.max(scores, axis=1, keepdims=True)
        e = jnp.exp(scores - most)
        stats.append(lanes_of([most, jnp.sum(e, axis=1, keepdims=True)]))
        sums.append(pick_heads(dot(e.astype(bf), v[gs, :], 1, 1)))
    sums = jnp.concatenate(sums, axis=1)
    stats = jnp.concatenate(stats, axis=1)
    width = D // units
    for u in range(units):
        us = slice(u * width, (u + 1) * width)
        msg[u, :LM, :] = sums[:, us]
        msg[u, LM:, :] = stats[:, us]


def item_specs(rows):
    mark = pl.BlockSpec((LM, D), lambda i: (i, 0))
    tok = pl.BlockSpec((D, rows), lambda i: (0, i))
    return mark, tok


def stats(lq, k, v, items, units):
    rows = k.shape[1] // items
    mark, tok = item_specs(rows)
    return pl.pallas_call(
        functools.partial(stats_kernel, units),
        grid=(items,),
        in_specs=[mark, tok, tok],
        out_specs=pl.BlockSpec((units, LM + 8, D // units), lambda i: (i, 0, 0)),
        out_shape=sds((items * units, LM + 8, D // units), f32),
        compiler_params=params(),
        cost_estimate=cost(4 * items * rows * D * GROUP, 4 * items * rows * D, items * rows * D),
        name="stats",
    )(lq, k, v)


def eye():
    return jnp.where(iota((LM, LM), 0) == iota((LM, LM), 1), 1.0, 0.0).astype(f32)


def head_slices(count):
    return [slice(h * HD, (h + 1) * HD) for h in range(count)]


def mark_probs(q, k):
    s = SCALE * dot(q, k, 1, 1)
    e = jnp.exp(s - jnp.max(s, axis=-1, keepdims=True))
    return e / jnp.sum(e, axis=-1, keepdims=True)


def inverse_start(a):
    col = jnp.sum(a, axis=0, keepdims=True)
    row = jnp.sum(a, axis=1, keepdims=True)
    return col, row, jnp.max(col, axis=1, keepdims=True), jnp.max(row, axis=0, keepdims=True)


def inverse_steps(a_list, kept=None):
    ident = eye()
    z_list = []
    for a in a_list:
        _, _, cm, rm = inverse_start(a)
        z_list.append(a.T / (cm * rm))
    for _ in range(NS_STEPS):
        p_list = [mm(a, z) for a, z in zip(a_list, z_list)]
        t2 = [15.0 * ident - mm(p, 7.0 * ident - p) for p in p_list]
        t3 = [13.0 * ident - mm(p, t) for p, t in zip(p_list, t2)]
        if kept is not None:
            kept.append((z_list, p_list, t2, t3))
        z_list = [0.25 * mm(z, t) for z, t in zip(z_list, t3)]
    return z_list


def own_slices(*refs):
    return [(k, s) for k, ref in enumerate(refs) for s in head_slices(ref.shape[1] // HD)]


def inverse_kernel(at, lq_l, lk_l, lq_s, lk_s, z_l, z_s):
    qs, ks, zs = (lq_l, lq_s), (lk_l, lk_s), (z_l, z_s)
    heads = own_slices(lq_l, lq_s)
    a_list = [mark_probs(qs[n][:, s], ks[n][:, s]) for n, s in heads]
    for (n, s), z in zip(heads, inverse_steps(a_list)):
        zs[n][:, s] = z


def whole(shape):
    return pl.BlockSpec(shape, lambda i, at: tuple(0 for _ in shape))


def inverse(at, lq_l, lk_l, lq_s, lk_s, width):
    own = pl.BlockSpec((LM, width), lambda i, at: (at[0], at[1]))
    return pl.pallas_call(
        inverse_kernel,
        grid_spec=pltpu.PrefetchScalarGridSpec(
            num_scalar_prefetch=1,
            grid=(1,),
            in_specs=[own, own, whole((LM, D)), whole((LM, D))],
            out_specs=[whole((LM, width)), whole((LM, D))],
        ),
        out_shape=[sds((LM, width), f32), sds((LM, D), f32)],
        compiler_params=params(),
        cost_estimate=cost((width + D) // HD * 24 * 3 * 2 * 64**3 * 20, 1e6),
        name="inverse",
    )(at, lq_l, lk_l, lq_s, lk_s)


def combine_kernel(senders, msg, z, out, bv_out):
    width = z.shape[1]
    most = jnp.concatenate([msg[d, LM : LM + 1, :] for d in range(senders)], axis=0)
    part = jnp.concatenate([msg[d, LM + 1 : LM + 2, :] for d in range(senders)], axis=0)
    top = jnp.max(most, axis=0, keepdims=True)
    e = jnp.exp(most - top)
    total = jnp.sum(part * e, axis=0, keepdims=True)
    weight = (e / total).T
    w_all = []
    for s in head_slices(width // HD):
        bv = jnp.zeros((LM, HD), f32)
        for d in range(senders):
            bv = bv + weight[s, d : d + 1] * msg[d, :LM, s]
        bv_out[:, s] = bv
        w_all.append(mm(z[:, s], bv))
    out[:LM, :] = jnp.concatenate(w_all, axis=1).astype(bf)
    out[LM:, :] = three_parts(top + jnp.log(total))


VMEM_SPEC = pl.BlockSpec(memory_space=pltpu.VMEM)


def combine(msg, z):
    senders, _, width = msg.shape
    return pl.pallas_call(
        functools.partial(combine_kernel, senders),
        in_specs=[VMEM_SPEC] * 2,
        out_specs=[VMEM_SPEC] * 2,
        out_shape=[sds((LM + 16, width), bf), sds((LM, width), f32)],
        compiler_params=params(),
        cost_estimate=cost(1e8, 4e6),
        name="combine",
    )(msg, z)


def joined(ref, units, rows):
    return jnp.concatenate([ref[u, rows, :] for u in range(units)], axis=1)


def mark_mix(lk_g, w_g, q_g, conv_g):
    probs = head_softmax(dot(spread_heads(lk_g * SCALE), q_g, 1, 0)).astype(bf)
    return (dot(spread_heads(w_g), probs, 0, 0) + conv_g).astype(bf)


def mix_kernel(units, lk, w, q, conv, out):
    w_all = joined(w, units, slice(0, LM))
    for gs in group_slices():
        out[gs, :] = mark_mix(lk[:, gs], w_all[:, gs], q[gs, :], conv[gs, :])


def short_kernel(length, q, k, v, lq, lk, z, conv, out, w_out, bv_out):
    for gs in group_slices():
        scores = mark_scores(lq[:, gs], k[gs, :], length[0])
        e = jnp.exp(scores - jnp.max(scores, axis=1, keepdims=True))
        probs = e / jnp.sum(e, axis=1, keepdims=True)
        bv = pick_heads(dot(probs.astype(bf), v[gs, :], 1, 1))
        bv_out[:, gs] = bv
        z_g = z[:, gs]
        w = jnp.concatenate([mm(z_g[:, s], bv[:, s]) for s in head_slices(4)], axis=1).astype(bf)
        w_out[:, gs] = w
        out[gs, :] = mark_mix(lk[:, gs], w, q[gs, :], conv[gs, :])


def short_attend(length, q, k, v, lq, lk, z, conv):
    return pl.pallas_call(
        short_kernel,
        in_specs=[SMEM_SPEC] + [VMEM_SPEC] * 7,
        out_specs=[VMEM_SPEC] * 3,
        out_shape=[sds(q.shape, bf), sds((LM, D), bf), sds((LM, D), f32)],
        compiler_params=params(),
        cost_estimate=cost(4 * q.size * GROUP * 2, 10 * q.size, 2 * q.size),
        name="short_attend",
    )(length, q, k, v, lq, lk, z, conv)


def unit_spec(units, rows, width):
    return pl.BlockSpec((units, rows, width), lambda i: (i, 0, 0))


def mix(lk, w, q, conv, items, units):
    rows = q.shape[1] // items
    mark, tok = item_specs(rows)
    return pl.pallas_call(
        functools.partial(mix_kernel, units),
        grid=(items,),
        in_specs=[mark, unit_spec(units, LM + 16, D // units), tok, tok],
        out_specs=tok,
        out_shape=sds(q.shape, bf),
        compiler_params=params(),
        cost_estimate=cost(4 * items * rows * D * GROUP, 8 * items * rows * D, items * rows * D),
        name="mix",
    )(lk, w, q, conv)


def windows(body, rim, items, rows, limit):
    out = []
    for j in range(items):
        own = body[:, j * rows : (j + 1) * rows]
        if limit is not None:
            own = jnp.where(iota(own.shape, 1) < limit, own.astype(f32), 0.0).astype(bf)
        wide = jnp.concatenate(
            [rim[:, 32 * j : 32 * j + HALF], own, rim[:, 32 * j + HALF : 32 * j + 2 * HALF]], axis=1
        )
        for t in range(rows // 128):
            out.append(wide[:, t * 128 : t * 128 + 128 + 2 * HALF])
    return jnp.concatenate(out, axis=0)


def band(row):
    wide = jnp.concatenate([row, jnp.zeros((1, 128), f32)], axis=1)
    rolled = pltpu.roll(jnp.broadcast_to(wide, (128, 256)), 0, 1, stride=1, stride_axis=0)
    return split(rolled[:, : 128 + 2 * HALF])


HEAD_STEP = 3


def unstack(stacked, out, at, items, rows, limit=None):
    k = 0
    for j in range(items):
        for t in range(rows // 128):
            v = stacked[k * HD : (k + 1) * HD]
            if limit is not None:
                v = jnp.where(iota(v.shape, 1) + t * 128 < limit, v, 0.0)
            out[at, j * rows + t * 128 : j * rows + (t + 1) * 128] = v
            k += 1


def both_windows(v_l, v_s, rim, at, items, limit):
    no_rim = jnp.zeros((HD, 2 * HALF), bf)
    rows, short_rows = v_l.shape[1] // items, v_s.shape[1]
    return jnp.concatenate(
        [
            windows(v_l[at, :], rim[at, :], items, rows, None),
            windows(v_s[at, :], no_rim, 1, short_rows, limit),
        ],
        axis=0,
    )


def banded(wins, row, out_l, out_s, at, items, limit):
    hi, lo = band(row)
    made = dot(wins, hi, 1, 1) + dot(wins, lo, 1, 1)
    cut = HD * out_l.shape[1] // 128
    unstack(made[:cut], out_l, at, items, out_l.shape[1] // items)
    unstack(made[cut:], out_s, at, 1, out_s.shape[1], limit)


def conv_kernel(items, length, v_l, v_s, rim, taps, out_l, out_s):
    for h in range(HEAD_STEP):
        at = slice(h * HD, (h + 1) * HD)
        wins = both_windows(v_l, v_s, rim, at, items, length[0])
        banded(wins, taps[h, 0:1, :], out_l, out_s, at, items, None)


def conv_specs(v_l, v_s, rim):
    n = HEAD_STEP * HD
    spec = lambda a: pl.BlockSpec((n, a.shape[1]), lambda h: (h, 0))
    return spec(v_l), spec(v_s), spec(rim), pl.BlockSpec((HEAD_STEP, 8, 128), lambda h: (h, 0, 0))


def conv(length, v_l, v_s, rim, taps, items):
    tok_l, tok_s, rims, tap = conv_specs(v_l, v_s, rim)
    return pl.pallas_call(
        functools.partial(conv_kernel, items),
        grid=(H // HEAD_STEP,),
        in_specs=[SMEM_SPEC, tok_l, tok_s, rims, tap],
        out_specs=[tok_l, tok_s],
        out_shape=[sds(v_l.shape, f32), sds(v_s.shape, f32)],
        compiler_params=params(),
        cost_estimate=cost(4 * 512 * v_l.size, 8 * v_l.size),
        name="conv",
    )(length, v_l, v_s, rim, taps)


def conv_back_kernel(items, length, v_l, v_s, rim, up_l, up_s, up_rim, taps, out_l, out_s, tap_grad):
    flip = (iota((128, 128), 0) + iota((128, 128), 1) == 127).astype(f32).astype(bf)
    for h in range(HEAD_STEP):
        at = slice(h * HD, (h + 1) * HD)
        wins = both_windows(v_l, v_s, rim, at, items, length[0])
        up_wins = both_windows(up_l, up_s, up_rim, at, items, None)
        banded(up_wins, taps[h, 1:2, :], out_l, out_s, at, items, length[0])
        ups = [up_l[at, t * 128 : (t + 1) * 128] for t in range(up_l.shape[1] // 128)]
        ups += [up_s[at, t * 128 : (t + 1) * 128] for t in range(up_s.shape[1] // 128)]
        gram = dot(jnp.concatenate(ups, axis=0), wins, 0, 0)
        hi, lo = split(gram)
        gram = dot(flip, hi, 1, 0) + dot(flip, lo, 1, 0)
        gram = jnp.concatenate([gram, jnp.zeros((128, 256 - gram.shape[1]), f32)], axis=1)
        skewed = pltpu.roll(gram, 129, 1, stride=1, stride_axis=0)
        tap_grad[h] = jnp.broadcast_to(jnp.sum(skewed, axis=0, keepdims=True)[:, :128], (8, 128))


def conv_back(length, v_l, v_s, rim, up_l, up_s, up_rim, taps, items, deps=()):
    tok_l, tok_s, rims, tap = conv_specs(v_l, v_s, rim)
    return pl.pallas_call(
        after(functools.partial(conv_back_kernel, items), 8, deps),
        grid=(H // HEAD_STEP,),
        in_specs=[SMEM_SPEC, tok_l, tok_s, rims, tok_l, tok_s, rims, tap] + [ANY_SPEC] * len(deps),
        out_specs=[tok_l, tok_s, tap],
        out_shape=[sds(v_l.shape, f32), sds(v_s.shape, f32), sds((H, 8, 128), f32)],
        compiler_params=params(),
        cost_estimate=cost(6 * 512 * v_l.size, 12 * v_l.size),
        name="conv_back",
    )(length, v_l, v_s, rim, up_l, up_s, up_rim, taps, *deps)


def fold_rows(v):
    return jnp.sum(v.reshape(v.shape[0] // 8, 8, v.shape[1]), axis=0)


def gelu_parts(x):
    e = jnp.exp(x * x * (-0.5))
    t = pl.reciprocal(1.0 + jnp.abs(x) * (0.3275911 * 0.7071067811865476), approx=False)
    poly = t * (
        0.127414796 + t * (-0.142248368 + t * (0.7107068705 + t * (-0.7265760135 + t * 0.5307027145)))
    )
    tail = poly * e
    phi = jnp.where(x >= 0, 1.0 - tail, tail)
    return x * phi, phi + x * e * 0.3989422804014327


def put_bf16(jobs, stage, sem):
    pend = []
    for k, (load, copies) in enumerate(jobs):
        slot = k % 2
        if k >= 2:
            for cp in pend[k - 2]:
                cp.wait()
        stage[slot] = load().astype(bf)
        pend.append(copies(stage.at[slot], sem.at[slot]))
    for group in pend[-2:]:
        for cp in group:
            cp.wait()


def to_side(src, keep, send, keeps, sem):
    copy = pltpu.make_async_copy(src, keep, sem)

    @pl.when(keeps)
    def _():
        copy.start()

    @pl.when(jnp.logical_not(keeps))
    def _():
        pltpu.make_async_copy(src, send, sem).start()

    return [copy]


def column_jobs(acc, keep, send, core):
    n = acc.shape[1] // D
    jobs = []
    for c in range(n):
        half, at = c // (n // 2), (c % (n // 2)) * D
        jobs.append((
            lambda c=c: acc[:, c * D : (c + 1) * D],
            lambda src, sem, half=half, at=at: to_side(
                src, keep.at[:, at : at + D], send.at[:, at : at + D], core == half, sem
            ),
        ))
    return jobs


def row_jobs(acc, keep, send, core):
    half = D // 2

    def copies(src, sem, c):
        out = []
        for ref, which in ((keep, core), (send, 1 - core)):
            start = pl.multiple_of(which * half, half)
            out.append(pltpu.make_async_copy(src.at[pl.ds(start, half), :], ref.at[:, c * D : (c + 1) * D], sem))
            out[-1].start()
        return out

    return [
        (lambda c=c: acc[:, c * D : (c + 1) * D], lambda src, sem, c=c: copies(src, sem, c))
        for c in range(acc.shape[1] // D)
    ]


def plain_job(acc, dst):
    def copies(src, sem):
        copy = pltpu.make_async_copy(src, dst, sem)
        copy.start()
        return [copy]

    return (lambda: acc[...], copies)


def dense_kernel(n_long, chunk, core, x_l, x_s, o_l, o_s, c_l, c_s, w_out, w_up, w_down, g1, b1, bu, bd, g2, b2,
                 out_l, out_s, dr_l, dr_s, do_l, do_s, up_keep, up_send, dn_keep, dn_send, gout, small, small_up,
                 acc_up, acc_dn, acc_out, act, dact, accs, accu, stage, sem):
    i = pl.program_id(0)
    last = pl.num_programs(0) - 1
    is_long = i < n_long

    @pl.when(i == 0)
    def _():
        for ref in (acc_up, acc_dn, acc_out, accs, accu):
            ref[...] = jnp.zeros_like(ref)

    x = jnp.where(is_long, x_l[...], x_s[...]).astype(f32)
    o_t = jnp.where(is_long, o_l[...], o_s[...])
    r1 = x + dot(o_t, w_out[...], 0, 0)
    cen = r1 - jnp.mean(r1, axis=-1, keepdims=True)
    rstd1 = lax.rsqrt(jnp.mean(cen * cen, axis=-1, keepdims=True) + EPSILON)
    xh1 = cen * rstd1
    h1 = (xh1 * g1[...] + b1[...]).astype(bf)
    r2 = h1.astype(f32) + bd[...]
    for c in range(FF // chunk):
        cs = slice(c * chunk, (c + 1) * chunk)
        a, dg = gelu_parts(dot(h1, w_up[:, cs], 1, 0) + bu[:, cs])
        a = a.astype(bf)
        act[:, cs] = a
        dact[:, cs] = dg
        r2 = r2 + dot(a, w_down[cs, :], 1, 0)
    cen2 = r2 - jnp.mean(r2, axis=-1, keepdims=True)
    rstd2 = lax.rsqrt(jnp.mean(cen2 * cen2, axis=-1, keepdims=True) + EPSILON)
    xh2 = cen2 * rstd2
    out = (xh2 * g2[...] + b2[...]).astype(bf)
    g = jnp.where(is_long, c_l[...], c_s[...]).astype(f32)
    dxh = g * g2[...]
    dr2 = rstd2 * (
        dxh - jnp.mean(dxh, axis=-1, keepdims=True) - xh2 * jnp.mean(dxh * xh2, axis=-1, keepdims=True)
    )
    dz2 = dr2.astype(bf)
    accs[4] += fold_rows(g * xh2)
    accs[5] += fold_rows(g)
    accs[2] += fold_rows(dz2.astype(f32))
    dz2_t = dz2.T
    h1_t = h1.T
    dh1 = dr2
    for c in range(FF // chunk):
        cs = slice(c * chunk, (c + 1) * chunk)
        dp1 = (dot(dz2, w_down[cs, :], 1, 1) * dact[:, cs]).astype(bf)
        accu[:, cs] += fold_rows(dp1.astype(f32))
        dh1 = dh1 + dot(dp1, w_up[:, cs], 1, 1)
        acc_up[:, cs] += dot(h1_t, dp1, 1, 0)
        acc_dn[:, cs] += dot(dz2_t, act[:, cs], 1, 0)
    accs[0] += fold_rows(dh1 * xh1)
    accs[1] += fold_rows(dh1)
    dx = dh1 * g1[...]
    dr1 = rstd1 * (
        dx - jnp.mean(dx, axis=-1, keepdims=True) - xh1 * jnp.mean(dx * xh1, axis=-1, keepdims=True)
    )
    da1 = dr1.astype(bf)
    acc_out[...] += dot(o_t, da1, 1, 0)
    do_t = dot(w_out[...], da1, 1, 1).astype(bf)

    @pl.when(is_long)
    def _():
        out_l[...] = out
        dr_l[...] = dr1
        do_l[...] = do_t

    @pl.when(jnp.logical_not(is_long))
    def _():
        out_s[...] = out
        dr_s[...] = dr1
        do_s[...] = do_t

    @pl.when(i == last)
    def _():
        jobs = column_jobs(acc_up, up_keep, up_send, core[0])
        jobs += row_jobs(acc_dn, dn_keep, dn_send, core[0])
        put_bf16(jobs + [plain_job(acc_out, gout)], stage, sem)
        small[...] = jnp.sum(accs[...], axis=1)
        small_up[...] = jnp.sum(accu[...], axis=0, keepdims=True)


def dense(core, x_l, x_s, o_l, o_s, c_l, c_s, w_out, w_up, w_down, g1, b1, bu, bd, g2, b2, tile=256, chunk=768):
    nl, ns = x_l.shape[0] // tile, x_s.shape[0] // tile
    long_at = lambda i: jnp.minimum(i, nl - 1)
    short_at = lambda i: jnp.maximum(i - nl, 0)
    row = lambda f: pl.BlockSpec((tile, D), lambda i: (f(i), 0))
    col = lambda f: pl.BlockSpec((D, tile), lambda i: (0, f(i)))
    anywhere = pl.BlockSpec(memory_space=pl.ANY)
    tl, ts = x_l.shape[0], x_s.shape[0]
    vec = const_spec((1, D))
    return pl.pallas_call(
        functools.partial(dense_kernel, nl, chunk),
        grid=(nl + ns,),
        in_specs=[SMEM_SPEC, row(long_at), row(short_at), col(long_at), col(short_at), row(long_at), row(short_at)]
        + [const_spec((D, D)), const_spec((D, FF)), const_spec((FF, D))]
        + [vec, vec, const_spec((1, FF)), vec, vec, vec],
        out_specs=[row(long_at), row(short_at), row(long_at), row(short_at), col(long_at), col(short_at)]
        + [anywhere] * 5
        + [const_spec((6, D)), const_spec((1, FF))],
        out_shape=[sds((tl, D), bf), sds((ts, D), bf), sds((tl, D), f32), sds((ts, D), f32)]
        + [sds((D, tl), bf), sds((D, ts), bf), sds((D, FF // 2), bf), sds((D, FF // 2), bf)]
        + [sds((D // 2, FF), bf), sds((D // 2, FF), bf), sds((D, D), bf)]
        + [sds((6, D), f32), sds((1, FF), f32)],
        scratch_shapes=[
            pltpu.VMEM((D, FF), f32),
            pltpu.VMEM((D, FF), f32),
            pltpu.VMEM((D, D), f32),
            pltpu.VMEM((tile, FF), bf),
            pltpu.VMEM((tile, FF), f32),
            pltpu.VMEM((6, 8, D), f32),
            pltpu.VMEM((8, FF), f32),
            pltpu.VMEM((2, D, D), bf),
            pltpu.SemaphoreType.DMA((2,)),
        ],
        compiler_params=params(),
        cost_estimate=cost(2 * (tl + ts) * (3 * D * D + 6 * D * FF), 60e6, (tl + ts) * FF),
        name="dense",
    )(core, x_l, x_s, o_l, o_s, c_l, c_s, w_out, w_up, w_down, g1, b1, bu, bd, g2, b2)


def back_f_group(lk_g, w_g, q_g, up_g):
    rows = q_g.shape[1]
    probs = head_softmax(dot(spread_heads(lk_g * SCALE), q_g, 1, 0))
    dw = pick_heads(dot(probs.astype(bf), up_g, 1, 1))
    dprobs = dot(spread_heads(w_g), up_g, 1, 0)
    weighted = jnp.sum((probs * dprobs).reshape(4, LM, rows), axis=1, keepdims=True)
    dsf = (probs * (dprobs.reshape(4, LM, rows) - weighted).reshape(GROUP, rows)).astype(bf)
    return dw, dsf, SCALE * pick_heads(dot(dsf, q_g, 1, 1))


def back_f_kernel(units, lk, w, q, up, dw_out, dlk_out, dsf_out, edges):
    w_all = joined(w, units, slice(0, LM))
    rows = q.shape[1]
    edges[0] = jnp.concatenate([up[:, :HALF], up[:, rows - HALF :]], axis=1).T
    dws = []
    for gs in group_slices():
        dw, dsf_out[gs, :], dlk_out[:, gs] = back_f_group(lk[:, gs], w_all[:, gs], q[gs, :], up[gs, :])
        dws.append(dw)
    dws = jnp.concatenate(dws, axis=1)
    width = D // units
    for u in range(units):
        dw_out[u] = dws[:, u * width : (u + 1) * width]


def back_f(lk, w, q, up, items, units):
    rows = q.shape[1] // items
    mark, tok = item_specs(rows)
    width = D // units
    return pl.pallas_call(
        functools.partial(back_f_kernel, units),
        grid=(items,),
        in_specs=[mark, unit_spec(units, LM + 16, width), tok, tok],
        out_specs=[unit_spec(units, LM, width), mark, tok, pl.BlockSpec((1, 2 * HALF, D), lambda i: (i, 0, 0))],
        out_shape=[
            sds((items * units, LM, width), f32),
            sds((items * LM, D), f32),
            sds(q.shape, bf),
            sds((items, 2 * HALF, D), bf),
        ],
        compiler_params=params(),
        cost_estimate=cost(8 * items * rows * D * GROUP, 6 * items * rows * D, items * rows * D),
        name="back_f",
    )(lk, w, q, up)


def back_mix_kernel(senders, dw_in, z, bv, out, dw_out):
    width = z.shape[1]
    dw = dw_in[0]
    for d in range(1, senders):
        dw = dw + dw_in[d]
    dw_out[...] = dw
    dbvs, dots = [], []
    for s in head_slices(width // HD):
        dbv = mm(z[:, s], dw[:, s], 0, 0).astype(bf)
        dots.append(jnp.sum(dbv.astype(f32) * bv[:, s], axis=1, keepdims=True))
        dbvs.append(dbv)
    out[:LM, :] = jnp.concatenate(dbvs, axis=1)
    out[LM:, :] = three_parts(lanes_of([jnp.concatenate(dots, axis=0)])[:1])


def back_mix(dw, z, bv, deps=()):
    senders, _, width = dw.shape
    return pl.pallas_call(
        after(functools.partial(back_mix_kernel, senders), 3, deps),
        in_specs=[VMEM_SPEC] * 3 + [ANY_SPEC] * len(deps),
        out_specs=[VMEM_SPEC] * 2,
        out_shape=[sds((LM + 16, width), bf), sds((LM, width), f32)],
        compiler_params=params(),
        cost_estimate=cost(1e8, 4e6),
        name="back_mix",
    )(dw, z, bv, *deps)


def back_inverse_kernel(at, lq_l, lk_l, lq_s, lk_s, dw_l, bv_l, dw_s, bv_s, dlq_l, dlk_l, dlq_s, dlk_s):
    qs, ks, dws, bvs = (lq_l, lq_s), (lk_l, lk_s), (dw_l, dw_s), (bv_l, bv_s)
    heads = own_slices(lq_l, lq_s)
    a_list = [mark_probs(qs[n][:, s], ks[n][:, s]) for n, s in heads]
    kept = []
    inverse_steps(a_list, kept)
    ident = eye()
    dz = [mm(dws[n][:, s], bvs[n][:, s], 1, 1) for n, s in heads]
    da = [jnp.zeros((LM, LM), f32) for _ in heads]
    for z, p, t2, t3 in reversed(kept):
        dt3 = [0.25 * mm(zz, d, 0, 0) for zz, d in zip(z, dz)]
        dz = [0.25 * mm(d, t, 1, 1) for d, t in zip(dz, t3)]
        dp = [-mm(d, t, 1, 1) for d, t in zip(dt3, t2)]
        dt2 = [-mm(pp, d, 0, 0) for pp, d in zip(p, dt3)]
        dp = [x - mm(d, 7.0 * ident - pp, 1, 1) for x, d, pp in zip(dp, dt2, p)]
        dp = [x + mm(pp, d, 0, 0) for x, pp, d in zip(dp, p, dt2)]
        da = [x + mm(d, zz, 1, 1) for x, d, zz in zip(da, dp, z)]
        dz = [x + mm(a, d, 0, 0) for x, a, d in zip(dz, a_list, dp)]
    for (n, s), a, g, d in zip(heads, a_list, da, dz):
        col, row, cm, rm = inverse_start(a)
        norm = cm * rm
        g = g + d.T / norm
        dnorm = -jnp.sum(jnp.sum(d.T * a, axis=1, keepdims=True), axis=0, keepdims=True) / (norm * norm)
        at_col = (col == cm).astype(f32)
        at_row = (row == rm).astype(f32)
        g = g + dnorm * rm * at_col / jnp.sum(at_col, axis=1, keepdims=True)
        g = g + dnorm * cm * at_row / jnp.sum(at_row, axis=0, keepdims=True)
        ds = a * (g - jnp.sum(a * g, axis=1, keepdims=True))
        (dlq_l, dlq_s)[n][:, s] = SCALE * mm(ds, ks[n][:, s].astype(f32))
        (dlk_l, dlk_s)[n][:, s] = SCALE * mm(ds, qs[n][:, s].astype(f32), 0, 0)


def back_inverse(at, lq_l, lk_l, lq_s, lk_s, dw_l, bv_l, dw_s, bv_s, deps=()):
    width = dw_l.shape[1]
    own = pl.BlockSpec((LM, width), lambda i, at: (at[0], at[1]))
    one, all_heads = whole((LM, width)), whole((LM, D))
    return pl.pallas_call(
        after(back_inverse_kernel, 9, deps),
        grid_spec=pltpu.PrefetchScalarGridSpec(
            num_scalar_prefetch=1,
            grid=(1,),
            in_specs=[own, own, all_heads, all_heads, one, one, all_heads, all_heads] + [ANY_SPEC] * len(deps),
            out_specs=[one, one, all_heads, all_heads],
        ),
        out_shape=[sds((LM, width), f32)] * 2 + [sds((LM, D), f32)] * 2,
        compiler_params=params(),
        cost_estimate=cost((width + D) // HD * 72 * 3 * 2 * 64**3 * 20, 2e6),
        name="back_inverse",
    )(at, lq_l, lk_l, lq_s, lk_s, dw_l, bv_l, dw_s, bv_s, *deps)


def back_b_group(lq_g, k_g, v_g, dbv_g, dots, dconv_g, probs):
    wide = spread_heads(dbv_g)
    dsb = (probs * (dot(wide, v_g, 1, 0) - dots)).astype(bf)
    dv = (dot(wide, probs.astype(bf), 0, 0) + dconv_g).astype(bf)
    return dsb, dv, SCALE * pick_heads(dot(dsb, k_g, 1, 1))


def back_b_kernel(units, lq, w, dbv, k, v, dconv, x, gv_in, dsb_out, dv_out, dlq_out, gv_out, acc):
    i = pl.program_id(0)

    @pl.when(i == 0)
    def _():
        acc[...] = gv_in[...]

    level = from_parts(joined(w, units, slice(LM, LM + 16)))
    dots = from_parts(joined(dbv, units, slice(LM, LM + 16)))
    dbv_all = joined(dbv, units, slice(0, LM))
    for gs in group_slices():
        probs = jnp.exp(mark_scores(lq[:, gs], k[gs, :], None) - level[gs])
        dsb_out[gs, :], dv, dlq_out[:, gs] = back_b_group(
            lq[:, gs], k[gs, :], v[gs, :], dbv_all[:, gs], dots[gs], dconv[gs, :], probs
        )
        dv_out[gs, :] = dv
        acc[gs, :] += dot(dv, x[...], 1, 0)

    @pl.when(i == pl.num_programs(0) - 1)
    def _():
        gv_out[...] = acc[...].astype(bf)


def back_b(lq, w, dbv, k, v, dconv, x, gv, items, units, deps=()):
    rows = k.shape[1] // items
    mark, tok = item_specs(rows)
    unit = unit_spec(units, LM + 16, D // units)
    square = const_spec((D, D))
    return pl.pallas_call(
        after(functools.partial(back_b_kernel, units), 8, deps),
        grid=(items,),
        in_specs=[mark, unit, unit, tok, tok, tok, pl.BlockSpec((rows, D), lambda i: (i, 0)), square]
        + [ANY_SPEC] * len(deps),
        out_specs=[tok, tok, mark, square],
        out_shape=[sds(k.shape, bf), sds(k.shape, bf), sds((items * LM, D), f32), sds((D, D), bf)],
        scratch_shapes=[pltpu.VMEM((D, D), f32)],
        compiler_params=params(),
        cost_estimate=cost(14 * items * rows * D * GROUP, 14 * items * rows * D, items * rows * D),
        name="back_b",
    )(lq, w, dbv, k, v, dconv, x, gv, *deps)


def short_back_kernel(length, q, k, v, lq, lk, z, w, bv, up, dconv, x, dsf_out, dsb_out, dv_out, dlq_out, dlk_out, dw_out, gv_out):
    for gs in group_slices():
        dw, dsf_out[gs, :], dlk_out[:, gs] = back_f_group(lk[:, gs], w[:, gs], q[gs, :], up[gs, :])
        dw_out[:, gs] = dw
        z_g, bv_g = z[:, gs], bv[:, gs]
        dbvs = [mm(z_g[:, s], dw[:, s], 0, 0).astype(bf) for s in head_slices(4)]
        dots = jnp.concatenate(
            [jnp.sum(d.astype(f32) * bv_g[:, s], axis=1, keepdims=True) for d, s in zip(dbvs, head_slices(4))], axis=0
        )
        scores = mark_scores(lq[:, gs], k[gs, :], length[0])
        e = jnp.exp(scores - jnp.max(scores, axis=1, keepdims=True))
        probs = e / jnp.sum(e, axis=1, keepdims=True)
        dsb_out[gs, :], dv, dlq_out[:, gs] = back_b_group(
            lq[:, gs], k[gs, :], v[gs, :], jnp.concatenate(dbvs, axis=1), dots, dconv[gs, :], probs
        )
        dv_out[gs, :] = dv
        gv_out[gs, :] = dot(dv, x[...], 1, 0)


def short_back(length, q, k, v, lq, lk, z, w, bv, up, dconv, x, deps=()):
    mark = sds((LM, D), f32)
    return pl.pallas_call(
        after(short_back_kernel, 12, deps),
        in_specs=[SMEM_SPEC] + [VMEM_SPEC] * 11 + [ANY_SPEC] * len(deps),
        out_specs=[VMEM_SPEC] * 7,
        out_shape=[sds(q.shape, bf)] * 3 + [mark] * 3 + [sds((D, D), f32)],
        compiler_params=params(),
        cost_estimate=cost(24 * q.size * GROUP, 20 * q.size, 2 * q.size),
        name="short_back",
    )(length, q, k, v, lq, lk, z, w, bv, up, dconv, x, *deps)


def score_part(member, x, lq, lk, dsf, dsb, sq, sk, dq_out, dk_out, acc):
    member2 = jnp.concatenate([member, member], axis=0)
    for n, (marks, scores, sums, out) in enumerate(((lk, dsf, sq, dq_out), (lq, dsb, sk, dk_out))):
        hi, lo = split(sums)
        back = dot(jnp.concatenate([hi, lo], axis=0), member2, 0, 0)
        for gs in group_slices():
            part = (dot(spread_heads(marks[:, gs] * SCALE), scores[gs, :], 0, 0) + back[gs]).astype(bf)
            out[gs, :] = part
            acc[n, gs, :] += dot(part, x[...], 1, 0)


def score_grads_kernel(n_long, length, core, x_l, lq_l, lk_l, dsf_l, dsb_l, sq_l, sk_l,
                       x_s, lq_s, lk_s, dsf_s, dsb_s, sq_s, sk_s, sq_own, sk_own,
                       dq_l, dk_l, dq_s, dk_s, keep, send, acc, stage, sem):
    i = pl.program_id(0)

    @pl.when(i == 0)
    def _():
        acc[...] = jnp.zeros_like(acc)
        member = short_member(length[0], x_s.shape[0]).astype(bf)
        count = (length[0] // LM).astype(f32)
        sq, sk = (sq_s[...] + sq_own[...]) / count, (sk_s[...] + sk_own[...]) / count
        score_part(member, x_s, lq_s, lk_s, dsf_s, dsb_s, sq, sk, dq_s, dk_s, acc)

    @pl.when(i > 0)
    def _():
        count, rows = sq_l.shape[0], x_l.shape[0]
        member = (iota((count, rows), 1) // (LONG // LM) == iota((count, rows), 0)).astype(f32).astype(bf)
        score_part(member, x_l, lq_l, lk_l, dsf_l, dsb_l, sq_l[...], sk_l[...], dq_l, dk_l, acc)

    @pl.when(i == n_long)
    def _():
        jobs = [
            (lambda: acc[0], lambda src, sem: to_side(src, keep, send, core[0] == 0, sem)),
            (lambda: acc[1], lambda src, sem: to_side(src, keep, send, core[0] == 1, sem)),
        ]
        put_bf16(jobs, stage, sem)


def score_grads(length, core, long_args, short_args, items, deps=()):
    x_l, x_s = long_args[0], short_args[0]
    tl, ts = x_l.shape[0], x_s.shape[0]
    rows = tl // items
    marks_l = long_args[5].shape[0] // items
    at = lambda i: jnp.maximum(i - 1, 0)
    first = lambda i: 0

    def specs(r, marks, f):
        row = pl.BlockSpec((r, D), lambda i: (f(i), 0))
        mark = pl.BlockSpec((LM, D), lambda i: (f(i), 0))
        tok = pl.BlockSpec((D, r), lambda i: (0, f(i)))
        own = pl.BlockSpec((marks, D), lambda i: (f(i), 0))
        return [row, mark, mark, tok, tok, own, own]

    long_out = pl.BlockSpec((D, rows), lambda i: (0, at(i)))
    short_out = pl.BlockSpec((D, ts), lambda i: (0, 0))
    return pl.pallas_call(
        after(functools.partial(score_grads_kernel, items), 18, deps),
        grid=(items + 1,),
        in_specs=[SMEM_SPEC, SMEM_SPEC]
        + specs(rows, marks_l, at)
        + specs(ts, LM, first)
        + [const_spec((LM, D))] * 2
        + [ANY_SPEC] * len(deps),
        out_specs=[long_out] * 2 + [short_out] * 2 + [ANY_SPEC] * 2,
        out_shape=[sds((D, tl), bf)] * 2 + [sds((D, ts), bf)] * 2 + [sds((D, D), bf)] * 2,
        scratch_shapes=[
            pltpu.VMEM((2, D, D), f32),
            pltpu.VMEM((2, D, D), bf),
            pltpu.SemaphoreType.DMA((2,)),
        ],
        compiler_params=params(),
        cost_estimate=cost(6 * (tl + ts) * D * D, 20 * (tl + ts) * D),
        name="score_grads",
    )(length, core, *long_args, *short_args, *deps)


def input_grad_kernel(n_long, dr_l, dq_l, dk_l, dv_l, dr_s, dq_s, dk_s, dv_s, wq, wk, wv, out_l, out_s):
    i = pl.program_id(0)
    is_long = i < n_long
    total = jnp.where(is_long, dr_l[...], dr_s[...])
    for long_ref, short_ref, w in ((dq_l, dq_s, wq), (dk_l, dk_s, wk), (dv_l, dv_s, wv)):
        grad = jnp.where(is_long, long_ref[...], short_ref[...])
        total = total + dot(grad, w[...], 0, 1)
    total = total.astype(bf)

    @pl.when(is_long)
    def _():
        out_l[...] = total

    @pl.when(jnp.logical_not(is_long))
    def _():
        out_s[...] = total


def input_grad(long_args, short_args, weights, deps=()):
    tl, ts = long_args[0].shape[0], short_args[0].shape[0]
    nl = tl // ts
    at = lambda i: jnp.minimum(i, nl - 1)
    row = lambda f: pl.BlockSpec((ts, D), lambda i: (f(i), 0))
    col = lambda f: pl.BlockSpec((D, ts), lambda i: (0, f(i)))
    first = lambda i: 0
    return pl.pallas_call(
        after(functools.partial(input_grad_kernel, nl), 11, deps),
        grid=(nl + 1,),
        in_specs=[row(at)] + [col(at)] * 3 + [row(first)] + [col(first)] * 3 + [const_spec((D, D))] * 3
        + [ANY_SPEC] * len(deps),
        out_specs=[row(at), row(first)],
        out_shape=[sds((tl, D), bf), sds((ts, D), bf)],
        compiler_params=params(),
        cost_estimate=cost(6 * (tl + ts) * D * D, 12 * (tl + ts) * D),
        name="input_grad",
    )(*long_args, *short_args, *weights, *deps)


def swap(values, axis, bit):
    count = lax.axis_size(axis)
    return lax.ppermute(values, axis, [(i, i ^ bit) for i in range(count)])


def side(axis, bit):
    return (lax.axis_index(axis) // bit) % 2


def exchange(values):
    return lax.all_to_all(values, "seq", 0, 0, tiled=True)


def gather(values):
    return exchange(jnp.broadcast_to(values[None], (lax.axis_size("seq"),) + values.shape))


def tied(values, dep):
    return lax.optimization_barrier(tuple(values) + (dep,))[:-1]


def is_small_mesh():
    return lax.axis_size("dp") == 4 and lax.axis_size("seq") == 8


def pair_sum(keep, send, axis, bit):
    return keep.astype(f32) + swap(send, axis, bit).astype(f32)


class Reduction:
    def __init__(self, keep, send, dim):
        self.dim, self.other = dim, 1 - dim
        self.core, self.x = side("dp", 1), side("dp", 2)
        v = pair_sum(keep, send, "dp", 1)
        if not is_small_mesh():
            self.theirs = v.astype(bf)
            return
        half = v.shape[self.other] // 2
        self.mine = lax.dynamic_slice_in_dim(v, self.x * half, half, self.other).astype(bf)
        self.theirs = lax.dynamic_slice_in_dim(v, (1 - self.x) * half, half, self.other).astype(bf)

    def wait_for(self, dep):
        if is_small_mesh():
            (self.mine,) = tied((self.mine,), dep)

    def over_x(self):
        if not is_small_mesh():
            self.value = self.theirs
            return self.value
        n_seq = lax.axis_size("seq")
        v = pair_sum(self.mine, self.theirs, "dp", 2).astype(bf)
        if self.dim == 0:
            v = v.reshape(n_seq, v.shape[0] // n_seq, v.shape[1])
        else:
            v = v.reshape(v.shape[0], n_seq, v.shape[1] // n_seq).transpose(1, 0, 2)
        self.value = v
        return v

    def over_seq(self):
        if not is_small_mesh():
            self.own = lax.psum_scatter(self.value, "seq", scatter_dimension=self.dim, tiled=True)
        else:
            self.own = jnp.sum(exchange(self.value).astype(f32), axis=0).astype(bf)
        return self.own

    def both(self):
        if not is_small_mesh():
            place = (jnp.arange(2) == self.core).astype(f32)[:, None, None]
            shares = lax.psum(self.own.astype(f32)[None] * place, "dp")
            return shares[0], shares[1]
        got = swap(self.own, "dp", 2)
        v = jnp.where(
            self.x == 0,
            jnp.concatenate([self.own, got], axis=self.other),
            jnp.concatenate([got, self.own], axis=self.other),
        )
        got = swap(v, "dp", 1)
        first = self.core == 0
        return jnp.where(first, v, got).astype(f32), jnp.where(first, got, v).astype(f32)


class Halving(Reduction):
    def __init__(self, keep, send, dim, order):
        if not is_small_mesh():
            super().__init__(keep, send, dim)
            return
        self.dim, self.other = dim, 1 - dim
        self.core, self.x = side("dp", 1), side("dp", 2)
        v = pair_sum(keep, send, "dp", 1)
        rows, n = v.shape
        if dim == 0:
            v = v.reshape(2, 2, 2, rows // 8, n)
        else:
            v = v.reshape(rows, 8, n // 8).transpose(1, 0, 2).reshape(2, 2, 2, rows, n // 8)
        self.left = ["z1", "z0", "y"]
        self.order = list(order)
        self.split(v)

    def split(self, v):
        step = self.order[0]
        if step == "x":
            dim = v.ndim - 1 if self.dim == 0 else v.ndim - 2
            bit = self.x
            size = v.shape[dim] // 2
        else:
            dim = self.left.index(step)
            self.left.pop(dim)
            bit = side("seq", {"y": 1, "z0": 2, "z1": 4}[step])
            size = 1
        take = lambda at: lax.dynamic_slice_in_dim(v, at * size, size, dim).astype(bf)
        self.mine, self.theirs = take(bit), take(1 - bit)
        if step != "x":
            self.mine, self.theirs = (lax.squeeze(u, (dim,)) for u in (self.mine, self.theirs))

    def step(self):
        if not is_small_mesh():
            self.value = self.theirs
            return self.theirs
        axis, bit = {"x": ("dp", 2), "y": ("seq", 1), "z0": ("seq", 2), "z1": ("seq", 4)}[self.order.pop(0)]
        v = pair_sum(self.mine, self.theirs, axis, bit)
        if self.order:
            self.split(v)
            return self.theirs
        self.own = v.astype(bf)
        return self.own

    def last(self):
        if not is_small_mesh():
            self.step()
            return self.over_seq()
        return self.step()


def hold(value, dep):
    return tied((value,), dep)[0]


class SumStages:
    def __init__(self, values):
        self.values = values
        self.steps = [("dp", 1), ("seq", 4), ("seq", 2), ("seq", 1), ("dp", 2)]

    def step(self, dep):
        if is_small_mesh():
            axis, bit = self.steps.pop(0)
            held = hold(self.values, dep)
            self.values = held + swap(held, axis, bit)
        elif len(self.steps) == 5:
            self.steps.pop(0)
            self.values = lax.psum(self.values, ("dp", "seq"))
        return self.values


def neighbours(first, last):
    count = lax.axis_size("seq")
    right = lax.ppermute(first, "seq", [((i + 1) % count, i) for i in range(count)])
    left = lax.ppermute(last, "seq", [(i, (i + 1) % count) for i in range(count)])
    return left, right


def pad_units(values, count):
    have = values.shape[0]
    if have == count:
        return values
    return jnp.concatenate([values, jnp.zeros((count - have,) + values.shape[1:], values.dtype)], axis=0)


def body(x_long, x_short, item_start, short_lengths, w_query, w_key, w_value, w_out, conv_taps, ln1_gain, ln1_bias,
         w_up, up_bias, w_down, down_bias, ln2_gain, ln2_bias, cot_long, cot_short):
    _, items, rows, _ = x_long.shape
    short_rows = x_short.shape[3]
    seg = LONG // LM
    own_marks = rows // seg
    n_seq = lax.axis_size("seq")
    me = lax.axis_index("seq")
    heads_each = next(h for h in (2, 4, 6, 12) if H % h == 0 and items * H // h <= n_seq)
    units = H // heads_each
    width = heads_each * HD
    owners = items * units

    x_l = x_long.reshape(items * rows, D)
    x_s = x_short.reshape(short_rows, D)
    length = short_lengths.reshape(1)
    core = side("dp", 1).astype(jnp.int32).reshape(1)
    mine = jnp.minimum(me, owners - 1).astype(jnp.int32)
    at = jnp.stack([mine // units, mine % units])

    x_mean = jnp.sum(x_long[0].reshape(items, own_marks, seg, D).astype(f32), axis=2) * (1.0 / seg)
    means = gather(x_mean.reshape(items * own_marks, D))
    means = means.reshape(n_seq, items, own_marks, D).transpose(1, 0, 2, 3).reshape(items * LM, D)
    mean_hi, mean_lo = split(means)

    def marks_of(w):
        return (
            jnp.dot(mean_hi, w, preferred_element_type=f32) + jnp.dot(mean_lo, w, preferred_element_type=f32)
        ).astype(bf)

    place = (me - item_start[0]) % n_seq
    open_left = (place > 0)[:, None, None]
    open_right = (place < n_seq - 1)[:, None, None]

    def rims(left, right):
        return jnp.concatenate(
            [jnp.where(open_left, left, jnp.zeros_like(left)), jnp.where(open_right, right, jnp.zeros_like(right))], axis=1
        ).reshape(items * 2 * HALF, D)

    x_rim = rims(*neighbours(x_long[0, :, :HALF], x_long[0, :, rows - HALF :]))
    v_rim = jnp.einsum("ke,nk->en", w_value, x_rim, preferred_element_type=f32).astype(bf)

    tap_rows = jnp.stack([conv_taps.T, conv_taps[::-1].T], axis=1)
    tap_rows = jnp.pad(tap_rows, ((0, 0), (0, 6), (0, 128 - TAPS)))

    q_l, k_l, v_l, q_s, k_s, v_s, lq_s, lk_s = qkv(length, x_l, x_s, w_query, w_key, w_value)
    c_l, c_s = conv(length, v_l, v_s, v_rim, tap_rows, items)
    lq_l, lk_l = marks_of(w_query), marks_of(w_key)

    msg_l = stats(lq_l, k_l, v_l, items, units)
    got_l = exchange(pad_units(msg_l, n_seq))
    z_own, z_s = inverse(at, lq_l, lk_l, lq_s, lk_s, width)
    w_own, bv_own = combine(got_l, z_own)
    w_l = gather(w_own)[:owners]
    o_s, w_s, bv_s = short_attend(length, q_s, k_s, v_s, lq_s, lk_s, z_s, c_s)
    o_l = mix(lk_l, w_l, q_l, c_l, items, units)

    vec = lambda v: v.reshape(1, -1)
    out_l, out_s, dr_l, dr_s, do_l, do_s, up_keep, up_send, dn_keep, dn_send, g_out, small, small_up = dense(
        core, x_l, x_s, o_l, o_s, cot_long.reshape(items * rows, D), cot_short.reshape(short_rows, D), w_out, w_up,
        w_down, vec(ln1_gain), vec(ln1_bias), vec(up_bias), vec(down_bias), vec(ln2_gain), vec(ln2_bias),
    )

    dw_l, dlk_part, dsf_l, edges = back_f(lk_l, w_l, q_l, do_l, items, units)
    got_dw = exchange(pad_units(dw_l, n_seq))
    up_keep, dn_keep = tied((up_keep, dn_keep), edges)
    up = Halving(up_keep, up_send, 0, ("x", "y", "z0", "z1"))
    down = Halving(dn_keep, dn_send, 1, ("y", "x", "z0", "z1"))
    do_rim = rims(*tied(neighbours(edges[:, :HALF], edges[:, HALF:]) + (up.theirs,), down.theirs)[:2]).T

    dc_l, dc_s, tap_g = conv_back(
        length, v_l, v_s, v_rim, do_l, do_s, do_rim, tap_rows, items, (up.theirs, down.theirs)
    )
    dsf_s, dsb_s, dv_s, dlq_s, dlk_s, dw_s, gv_s = short_back(
        length, q_s, k_s, v_s, lq_s, lk_s, z_s, w_s, bv_s, do_s, dc_s, x_s
    )
    packed = jnp.concatenate([small.reshape(-1), small_up.reshape(-1), tap_g[:, 0, :].reshape(-1)]).reshape(-1, 128)
    packed = SumStages(packed)
    dbv_own, dw_own = back_mix(got_dw, z_own, bv_own, (dv_s,))
    dbv_l = gather(dbv_own)[:owners]
    dlq_own, dlk_own, dlq_own_s, dlk_own_s = back_inverse(
        at, lq_l, lk_l, lq_s, lk_s, dw_own, bv_own, dw_s, bv_s, (up.step(), down.step())
    )
    dsb_l, dv_l, dlq_part, g_v = back_b(
        lq_l, w_l, dbv_l, k_l, v_l, dc_l, x_l, gv_s, items, units, (up.step(), down.step(), packed.step(dw_own))
    )

    owned = (jnp.arange(owners) == me).astype(f32).reshape(items, units, 1, 1)

    def with_own(part, own):
        return part.reshape(items, LM, D) + (owned * own[None, None]).transpose(0, 2, 1, 3).reshape(items, LM, D)

    dl = jnp.stack([with_own(dlq_part, dlq_own), with_own(dlk_part, dlk_own)]).astype(bf)
    dl = dl.reshape(2 * items, n_seq, own_marks, D).transpose(1, 0, 2, 3)
    dl = jnp.sum(exchange(dl).astype(f32), axis=0) * (1.0 / seg)
    dl = jnp.pad(dl.reshape(2, items, own_marks, D), ((0, 0), (0, 0), (0, 16 - own_marks), (0, 0)))
    dl = dl.reshape(2, items * 16, D)

    g_v = g_v.T
    is_first = core[0] == 0
    value_out = Reduction(jnp.where(is_first, g_v, g_out), jnp.where(is_first, g_out, g_v), 0)

    dq_l, dk_l, dq_s, dk_s, qk_keep, qk_send = score_grads(
        length,
        core,
        (x_l, lq_l, lk_l, dsf_l, dsb_l, dl[0], dl[1]),
        (x_s, lq_s, lk_s, dsf_s, dsb_s, dlq_s, dlk_s, dlq_own_s, dlk_own_s),
        items,
        (up.step(), down.step(), packed.step(dlq_part), value_out.theirs),
    )
    query_key = Reduction(qk_keep, qk_send, 1)
    grad_l, grad_s = input_grad(
        (dr_l, dq_l, dk_l, dv_l),
        (dr_s, dq_s, dk_s, dv_s),
        (w_query, w_key, w_value),
        (query_key.theirs, value_out.over_x()),
    )
    query_key.wait_for(grad_l)
    up.last()
    down.last()
    query_key.over_x()
    ready = query_key.value
    up.own, down.own = hold(up.own, ready), hold(down.own, ready)
    packed.step(grad_l)
    packed.step(ready)
    value_out.over_seq()
    query_key.over_seq()
    up_a, up_b = up.both()
    down_a, down_b = down.both()
    v_a, v_b = value_out.both()
    q_g, k_g = query_key.both()

    packed = packed.step(ready).reshape(-1)
    small = packed[: 6 * D].reshape(6, D)
    small_up = packed[6 * D : 6 * D + FF]
    taps_g = packed[6 * D + FF :].reshape(H, 128)[:, :TAPS].T

    return (
        out_l.reshape(x_long.shape),
        out_s.reshape(x_short.shape),
        grad_l.reshape(x_long.shape),
        grad_s.reshape(x_short.shape),
        q_g.T,
        k_g.T,
        v_a,
        v_b,
        taps_g,
        small[0],
        small[1],
        jnp.concatenate([up_a, up_b], axis=1),
        small_up,
        jnp.concatenate([down_a, down_b], axis=0).T,
        small[2],
        small[4],
        small[5],
    )


def solution(mesh):
    tokens = P("dp", None, "seq", None)
    shorts = P("dp", "seq", None, None, None)
    rows = P("seq", None)
    return jax.shard_map(
        body,
        mesh=mesh,
        in_specs=(tokens, shorts, P("dp", None), P("dp", "seq", None)) + (P(),) * 13 + (tokens, shorts),
        out_specs=(tokens, shorts, tokens, shorts, rows, rows, rows, rows, P(), P(), P(), rows, P(), rows, P(), P(), P()),
        check_vma=False,
    )
```

time: 696 us -> 542 us (0.78)
  blocking collectives: 100 us -> 0 us
  Pallas kernels: 345 us -> 317 us
  local copies, waits for them, and re-layouts: 64.4 us -> 48.3 us
  other arithmetic: 43.1 us -> 33.7 us
    all_gather x3 -> x0, blocking collectives: 100 us -> none  [gather(): return lax.all_gather(values, 'seq', axis=0)]
    pallas_call x17 -> x13, Pallas kernels: 185 us -> 155 us  [the longest x1 28.1 us: back_inverse(): pl.pallas_call(after(back_inverse_kernel, 9, deps), grid_spec=pltpu.Prefe...]
    all_to_all x3 -> x8, starting transfers between devices: 16 us -> 38.9 us  [exchange(): return lax.all_to_all(values, 'seq', 0, 0, tiled=True)]
    ppermute x47 -> x27, starting transfers between devices: 43.7 us -> 25.3 us  [swap(): return lax.ppermute(values, axis, [(i, i ^ bit) for i in range(count)])]
    ppermute x47 -> x27, waiting for transfers between devices: 57 us -> 38.6 us  [swap(): return lax.ppermute(values, axis, [(i, i ^ bit) for i in range(count)])]
    all_to_all x3 -> x8, waiting for transfers between devices: 0.01 us -> 17.6 us  [exchange(): return lax.all_to_all(values, 'seq', 0, 0, tiled=True)]
    convert_element_type x35 -> x5, other arithmetic: 22.6 us -> 6.26 us  [the longest x2 3.43 us: over_x(): v = pair_sum(self.mine, self.theirs, 'dp', 2).astype(bf)]
    add x5 -> x15, other arithmetic: 0.81 us -> 15.6 us  [the longest x10 14.4 us: pair_sum(): return keep.astype(f32) + swap(send, axis, bit).astype(f32)]
  transfers between devices with their start and end apart: 54 -> 39, of which waited for: 15 -> 9; matrix products, arithmetic and copies ran while one was open for 14% -> 14% of each run, Pallas kernels for 25% -> 27%
where the time goes in v2:
time: 542 us; the launch traced here: 540 us
  Pallas kernels  317 us (58%)
  starting transfers between devices  75 us (14%)
  waiting for transfers between devices  56.2 us (10%)
  local copies, waits for them, and re-layouts  48.3 us (9%)
  other arithmetic  33.7 us (6%)
  matrix products  6.72 us (1%)
    pallas_call x1, Pallas kernels, dense(): pl.pallas_call(functools.partial(dense_kernel, nl, chunk), grid=(nl + ns,...  145 us
    all_to_all x8, starting transfers between devices, exchange(): return lax.all_to_all(values, 'seq', 0, 0, tiled=True)  38.9 us
    ppermute x27, waiting for transfers between devices, swap(): return lax.ppermute(values, axis, [(i, i ^ bit) for i in range(count)])  38.6 us
    pallas_call x1, Pallas kernels, back_inverse(): pl.pallas_call(after(back_inverse_kernel, 9, deps), grid_spec=pltpu.Prefe...  28.1 us
    ppermute x27, starting transfers between devices, swap(): return lax.ppermute(values, axis, [(i, i ^ bit) for i in range(count)])  25.3 us
    pallas_call x1, Pallas kernels, score_grads(): pl.pallas_call(after(functools.partial(score_grads_kernel, items), 18, de...  20.6 us
    pallas_call x1, Pallas kernels, qkv(): pl.pallas_call(functools.partial(qkv_kernel, nl), grid=(nl + 1,), in_spec...  17.8 us
    all_to_all x8, waiting for transfers between devices, exchange(): return lax.all_to_all(values, 'seq', 0, 0, tiled=True)  17.6 us
  transfers between devices with their start and end apart: 39, of which 9 were waited for; matrix products, arithmetic and copies ran while one was open for 14% of the time, Pallas kernels for 27%

profile of v2, /device:TPU:0, one launch (start us, length us, event | category | flops | bytes accessed | tf_op | source)
XLA Modules:
  0.0 539.8 jit_solution(4093036484753013545)
XLA Ops:
  2.3 3.0 collective-permute-start
  5.2 3.0 collective-permute-start.1
  11.8 3.5 all-to-all-start
  20.8 17.8 %qkv.1 = (bf16[768,2048]{1,0:T(8,128)(2,1)}, bf16[768,2048]{1,0:T(8,128)(2,1)}, bf16[768,2048]{1,0:T(8,128)(2,1)}, bf16[768,512]{1,0:T(8,128)(2,1)}, bf16[768,51...) custom-call(s32[1]{0:T(128)} %bitcast.149.length, ...), custom_call_target="tpu_custom_call" | custom-call | flops 9059696640 | bytes 15728640 | tf_op jit(solution)/shard_map/qkv/pallas_call | solution.py:154
  45.2 7.3 %stats.1 = f32[8,72,384]{2,1,0:T(8,128)} custom-call(bf16[256,768]{1,0:T(8,128)(2,1)} %fusion.1.lq.lq_l.refs_0_.refs_1_.refs_3_, bf16[768,2048]{1,0:T(8,128)(2,1)} %get-tuple-element.91.k.refs_3_, bf16[768,2048]{1,0:T(8,128)(2,1)} %get-tuple-element.92.v.v_l.refs_1_.refs_4_), custom_call_target="tpu_custom_call" | custom-call | flops 1610612736 | bytes 6291456 | tf_op jit(solution)/shard_map/stats/pallas_call | solution.py:204
  52.5 6.5 %all-to-all-start.1 = ((f32[8,72,384]{2,1,0:T(8,128)}), f32[8,72,384]{2,1,0:T(8,128)S(1)}, u32[]{:S(2)}, u32[]{:S(2)}) async-start(f32[8,72,384]{2,1,0:T(8,128)} %stats.1), calls=%async_computation.1 | async-start | bytes 1769472 | tf_op jit(solution)/shard_map/all_to_all | solution.py:1024
  61.4 9.1 %inverse.1 = (f32[64,384]{1,0:T(8,128)}, f32[64,768]{1,0:T(8,128)}) custom-call(s32[2]{0:T(128)} %pad_add_fusion.at.refs_0_, bf16[256,768]{1,0:T(8,128)(2,1)} %fusion.1.lq.lq_l.refs_0_.refs_1_.refs_3_, bf16[256,768]{1,0:T(8,128)(2,1)} %fusion.lk_l.lk.refs_2_.refs_4_, bf16[64,768]{1,0:T(8,128)(2,1)} %get-tuple-element.93.lq_s.lq.refs_4_.refs_3_.refs_10_, ...), custom_call_target="tpu_custom_call" | custom-call | flops 13589544960 | bytes 1000000 | tf_op jit(solution)/shard_map/inverse/pallas_call | solution.py:270
  70.5 10.3 %all-to-all-done.1.msg = f32[8,72,384]{2,1,0:T(8,128)S(1)} async-done(((f32[8,72,384]{2,1,0:T(8,128)}), f32[8,72,384]{2,1,0:T(8,128)S(1)}, u32[]{:S(2)}, u32[]{:S(2)}) %all-to-all-start.1) | async-done | bytes 884768 | tf_op jit(solution)/shard_map/all_to_all | solution.py:1024
  81.8 2.9 combine.1
  86.5 3.5 all-to-all-start.2
  92.3 8.2 %conv.1 = (f32[768,2048]{1,0:T(8,128)}, f32[768,512]{1,0:T(8,128)}) custom-call(s32[1]{0:T(128)} %bitcast.150.length, bf16[768,2048]{1,0:T(8,128)(2,1)} %get-tuple-element.92.v.v_l.refs_1_.refs_4_, bf16[768,512]{1,0:T(8,128)(2,1)} %get-tuple-element.98.v_s.v.refs_2_.refs_3_, bf16[768,128]{1,0:T(8,128)(2,1)} %fusion.4.rim.refs_3_, ...), custom_call_target="tpu_custom_call" | custom-call | flops 3221225472 | bytes 12582912 | tf_op jit(solution)/shard_map/conv/pallas_call | solution.py:448
  100.5 6.5 %short_attend.1 = (bf16[768,512]{1,0:T(8,128)(2,1)}, bf16[64,768]{1,0:T(8,128)(2,1)}, f32[64,768]{1,0:T(8,128)}) custom-call(s32[1]{0:T(128)} %bitcast.151.length, bf16[768,512]{1,0:T(8,128)(2,1)} %get-tuple-element.100.q.refs_1_, bf16[768,512]{1,0:T(8,128)(2,1)} %get-tuple-element.101.k.refs_2_, bf16[768,512]{1,0:T(8,128)(2,1)} %get-tuple-element.98.v_s.v.refs_2_.refs_3_, ...), custom_call_target="tpu_custom_call" | custom-call | flops 805306368 | bytes 3932160 | tf_op jit(solution)/shard_map/short_attend/pallas_call | solution.py:349
  107.8 8.9 %mix.1.o_l = bf16[768,2048]{1,0:T(8,128)(2,1)} custom-call(bf16[256,768]{1,0:T(8,128)(2,1)} %fusion.lk_l.lk.refs_2_.refs_4_, bf16[8,80,384]{2,1,0:T(8,128)(2,1)} %copy-done.19, bf16[768,2048]{1,0:T(8,128)(2,1)} %get-tuple-element.97.q, f32[768,2048]{1,0:T(8,128)} %get-tuple-element.99.conv), custom_call_target="tpu_custom_call" | custom-call | flops 1610612736 | bytes 12582912 | tf_op jit(solution)/shard_map/mix/pallas_call | solution.py:367
  116.7 144.6 %dense.1 = (bf16[2048,768]{1,0:T(8,128)(2,1)}, bf16[512,768]{1,0:T(8,128)(2,1)}, f32[2048,768]{1,0:T(8,128)}, f32[512,768]{1,0:T(8,128)}, bf16[768,2048]{1,0:T(8...) custom-call(s32[1]{0:T(128)} %bitcast.core.refs_1_, ...), custom_call_target="tpu_custom_call" | custom-call | flops 81537269760 | bytes 60000000 | tf_op jit(solution)/shard_map/dense/pallas_call | solution.py:664
  262.6 8.6 %back_f.1 = (f32[8,64,384]{2,1,0:T(8,128)}, f32[256,768]{1,0:T(8,128)}, bf16[768,2048]{1,0:T(8,128)(2,1)}, bf16[4,32,768]{2,1,0:T(8,128)(2,1)}) custom-call(bf16[256,768]{1,0:T(8,128)(2,1)} %fusion.lk_l.lk.refs_2_.refs_4_, bf16[8,80,384]{2,1,0:T(8,128)(2,1)} %copy-done.19, bf16[768,2048]{1,0:T(8,128)(2,1)} %get-tuple-element.97.q, ...), custom_call_target="tpu_custom_call" | custom-call | flops 3221225472 | bytes 9437184 | tf_op jit(solution)/shard_map/back_f/pallas_call | solution.py:722
  271.2 6.1 %all-to-all-start.3 = ((f32[8,64,384]{2,1,0:T(8,128)}), f32[8,64,384]{2,1,0:T(8,128)S(1)}, u32[]{:S(2)}, u32[]{:S(2)}) async-start(f32[8,64,384]{2,1,0:T(8,128)} %get-tuple-element.110), calls=%async_computation.3 | async-start | bytes 1572864 | tf_op jit(solution)/shard_map/all_to_all | solution.py:1024
  277.3 4.8 collective-permute-start.3
  282.1 3.0 convert_add_fusion.1
  300.2 10.8 %conv_back.1 = (f32[768,2048]{1,0:T(8,128)}, f32[768,512]{1,0:T(8,128)}, f32[12,8,128]{2,1,0:T(8,128)}) custom-call(s32[1]{0:T(128)} %bitcast.152.refs_0_, bf16[768,2048]{1,0:T(8,128)(2,1)} %get-tuple-element.92.v.v_l.refs_1_.refs_4_, bf16[768,512]{1,0:T(8,128)(2,1)} %get-tuple-element.98.v_s.v.refs_2_.refs_3_, bf16[768,128]{1,0:T(8,128)(2,1)} %fusion.4.rim.refs_3_, ...), custom_call_target="tpu_custom_call" | custom-call | flops 4831838208 | bytes 18874368 | tf_op jit(solution)/shard_map/conv_back/pallas_call | solution.py:479
  311.0 9.6 %short_back.1 = (bf16[768,512]{1,0:T(8,128)(2,1)}, bf16[768,512]{1,0:T(8,128)(2,1)}, bf16[768,512]{1,0:T(8,128)(2,1)}, f32[64,768]{1,0:T(8,128)}, f32[64,768]{1,...) custom-call(s32[1]{0:T(128)} %bitcast.153.refs_0_, bf16[768,512]{1,0:T(8,128)(2,1)} %get-tuple-element.100.q.refs_1_, ...), custom_call_target="tpu_custom_call" | custom-call | flops 2415919104 | bytes 7864320 | tf_op jit(solution)/shard_map/short_back/pallas_call | solution.py:888
  327.5 6.5 %all-to-all-start.4 = ((bf16[8,80,384]{2,1,0:T(8,128)(2,1)}), bf16[8,80,384]{2,1,0:T(8,128)(2,1)}, u32[]{:S(2)}, u32[]{:S(2)}) async-start(bf16[8,80,384]{2,1,0:T(8,128)(2,1)} %broadcast_in_dim.44), calls=%async_computation.4 | async-start | bytes 983040 | tf_op jit(solution)/shard_map/all_to_all | solution.py:1024
  344.4 28.1 %back_inverse.1 = (f32[64,384]{1,0:T(8,128)}, f32[64,384]{1,0:T(8,128)}, f32[64,768]{1,0:T(8,128)}, f32[64,768]{1,0:T(8,128)}) custom-call(s32[2]{0:T(128)} %pad_add_fusion.at.refs_0_, bf16[256,768]{1,0:T(8,128)(2,1)} %fusion.1.lq.lq_l.refs_0_.refs_1_.refs_3_, bf16[256,768]{1,0:T(8,128)(2,1)} %fusion.lk_l.lk.refs_2_.refs_4_, ...), custom_call_target="tpu_custom_call" | custom-call | flops 40768634880 | bytes 2000000 | tf_op jit(solution)/shard_map/back_inverse/pallas_call | solution.py:803
  381.5 15.0 %back_b.1 = (bf16[768,2048]{1,0:T(8,128)(2,1)}, bf16[768,2048]{1,0:T(8,128)(2,1)}, f32[256,768]{1,0:T(8,128)}, bf16[768,768]{1,0:T(8,128)(2,1)}) custom-call(bf16[256,768]{1,0:T(8,128)(2,1)} %fusion.1.lq.lq_l.refs_0_.refs_1_.refs_3_, bf16[8,80,384]{2,1,0:T(8,128)(2,1)} %copy-done.19, bf16[8,80,384]{2,1,0:T(8,128)(2,1)} %all-to-all-done.4.refs_2_, ...), custom_call_target="tpu_custom_call" | custom-call | flops 5637144576 | bytes 22020096 | tf_op jit(solution)/shard_map/back_b/pallas_call | solution.py:853
  401.2 3.9 all-to-all-start.5
  405.1 2.9 collective-permute-start.13
  409.5 17.5 %collective-permute-done.13 = f32[72,128]{1,0:T(8,128)S(1)} collective-permute-done((f32[72,128]{1,0:T(8,128)S(1)}, f32[72,128]{1,0:T(8,128)S(1)}, u32[]{:S(2)}, u32[]{:S(2)}) %collective-permute-start.13) | collective-permute-done | bytes 36896 | tf_op jit(solution)/shard_map/ppermute | solution.py:1016
  434.8 20.6 %score_grads.1 = (bf16[768,2048]{1,0:T(8,128)(2,1)}, bf16[768,2048]{1,0:T(8,128)(2,1)}, bf16[768,512]{1,0:T(8,128)(2,1)}, bf16[768,512]{1,0:T(8,128)(2,1)}, bf16...) custom-call(s32[1]{0:T(128)} %bitcast.154.refs_0_, s32[1]{0:T(128)} %bitcast.core.refs_1_, bf16[2048,768]{1,0:T(8,128)(2,1)} %bitcast.162, ...), custom_call_target="tpu_custom_call" | custom-call | flops 9059696640 | bytes 39321600 | tf_op jit(solution)/shard_map/score_grads/pallas_call | solution.py:955
  460.0 11.4 %collective-permute-done.16 = bf16[768,384]{1,0:T(8,128)(2,1)} collective-permute-done((bf16[768,384]{1,0:T(8,128)(2,1)S(1)}, bf16[768,384]{1,0:T(8,128)(2,1)}, u32[]{:S(2)}, u32[]{:S(2)}) %collective-permute-start.16) | collective-permute-done | bytes 589856 | tf_op jit(solution)/shard_map/ppermute | solution.py:1016
  473.6 4.4 all-to-all-start.7
  480.7 16.8 %input_grad.1 = (bf16[2048,768]{1,0:T(8,128)(2,1)}, bf16[512,768]{1,0:T(8,128)(2,1)}) custom-call(f32[2048,768]{1,0:T(8,128)} %get-tuple-element.107.refs_0_, bf16[768,2048]{1,0:T(8,128)(2,1)} %get-tuple-element.149.refs_1_, bf16[768,2048]{1,0:T(8,128)(2,1)} %get-tuple-element.150.refs_2_, bf16[768,2048]{1,0:T(8,128)(2,1)} %get-tuple-element.151.refs_3_, ...), custom_call_target="tpu_custom_call" | custom-call | flops 9059696640 | bytes 23592960 | tf_op jit(solution)/shard_map/input_grad/pallas_call | solution.py:1001
  512.8 4.6 all-to-all-start.6
  525.3 7.2 %all-to-all-done.6 = bf16[8,384,96]{1,2,0:T(8,128)(2,1)S(1)} async-done(((bf16[8,384,96]{1,2,0:T(8,128)(2,1)}), bf16[8,384,96]{1,2,0:T(8,128)(2,1)S(1)}, u32[]{:S(2)}, u32[]{:S(2)}) %all-to-all-start.6) | async-done | bytes 589856 | tf_op jit(solution)/shard_map/all_to_all | solution.py:1024
  (247 shorter events, 120.6 us)
Async XLA Ops:
  2.3 36.9 %collective-permute-start = (bf16[4,16,768]{2,1,0:T(8,128)(2,1)S(1)}, bf16[4,16,768]{2,1,0:T(8,128)(2,1)S(1)}, u32[]{:S(2)}, u32[]{:S(2)}) collective-permute-start(bf16[4,16,768]{2,1,0:T(8,128)(2,1)S(1)} %get-tuple-element.254), channel_id=1, source_target_pairs={{0,1},{1,2},{2,3},{3,4},{4,5},{5,6},{6,7},{7,0},{8,9},{9,10},{10,1... | collective-permute-start | bytes 294920 | tf_op jit(solution)/shard_map/ppermute | solution.py:1170
  5.2 84.7 %collective-permute-start.1 = (bf16[4,16,768]{2,1,0:T(8,128)(2,1)}, bf16[4,16,768]{2,1,0:T(8,128)(2,1)}, u32[]{:S(2)}, u32[]{:S(2)}) collective-permute-start(bf16[4,16,768]{2,1,0:T(8,128)(2,1)} %get-tuple-element.255), channel_id=1, source_target_pairs={{1,0},{2,1},{3,2},{4,3},{5,4},{6,5},{7,6},{0,7},{9,8},{10,9},{11,1... | collective-permute-start | bytes 294920 | tf_op jit(solution)/shard_map/ppermute | solution.py:1169
  11.8 28.1 %all-to-all-start = ((f32[8,32,768]{2,1,0:T(8,128)}), f32[8,32,768]{2,1,0:T(8,128)S(1)}, u32[]{:S(2)}, u32[]{:S(2)}) async-start(f32[8,32,768]{2,1,0:T(8,128)} %broadcast_in_dim.40), calls=%async_computation | async-start | bytes 1572864 | tf_op jit(solution)/shard_map/all_to_all | solution.py:1024
  52.5 28.3 %all-to-all-start.1 = ((f32[8,72,384]{2,1,0:T(8,128)}), f32[8,72,384]{2,1,0:T(8,128)S(1)}, u32[]{:S(2)}, u32[]{:S(2)}) async-start(f32[8,72,384]{2,1,0:T(8,128)} %stats.1), calls=%async_computation.1 | async-start | bytes 1769472 | tf_op jit(solution)/shard_map/all_to_all | solution.py:1024
  86.5 20.5 %all-to-all-start.2 = ((bf16[8,80,384]{2,1,0:T(8,128)(2,1)}), bf16[8,80,384]{2,1,0:T(8,128)(2,1)S(1)}, u32[]{:S(2)}, u32[]{:S(2)}) async-start(bf16[8,80,384]{2,1,0:T(8,128)(2,1)} %broadcast_in_dim.41), calls=%async_computation.2 | async-start | bytes 983040 | tf_op jit(solution)/shard_map/all_to_all | solution.py:1024
  261.2 20.9 %collective-permute-start.4 = (bf16[768,1536]{1,0:T(8,128)(2,1)}, bf16[768,1536]{1,0:T(8,128)(2,1)}, u32[]{:S(2)}, u32[]{:S(2)}) collective-permute-start(bf16[768,1536]{1,0:T(8,128)(2,1)} %get-tuple-element.119), channel_id=1, source_target_pairs={{0,8},{8,0},{16,24},{24,16},{1,9},{9,1},{17,25},{25,17},{2,10},{10... | collective-permute-start | bytes 7077896 | tf_op jit(solution)/shard_map/ppermute | solution.py:1016
  261.3 30.1 %collective-permute-start.5 = (bf16[384,3072]{1,0:T(8,128)(2,1)}, bf16[384,3072]{1,0:T(8,128)(2,1)}, u32[]{:S(2)}, u32[]{:S(2)}) collective-permute-start(bf16[384,3072]{1,0:T(8,128)(2,1)} %get-tuple-element.121), channel_id=1, source_target_pairs={{0,8},{8,0},{16,24},{24,16},{1,9},{9,1},{17,25},{25,17},{2,10},{10... | collective-permute-start | bytes 7077896 | tf_op jit(solution)/shard_map/ppermute | solution.py:1016
  271.2 49.3 %all-to-all-start.3 = ((f32[8,64,384]{2,1,0:T(8,128)}), f32[8,64,384]{2,1,0:T(8,128)S(1)}, u32[]{:S(2)}, u32[]{:S(2)}) async-start(f32[8,64,384]{2,1,0:T(8,128)} %get-tuple-element.110), calls=%async_computation.3 | async-start | bytes 1572864 | tf_op jit(solution)/shard_map/all_to_all | solution.py:1024
  277.3 22.0 %collective-permute-start.3 = (bf16[4,16,768]{2,1,0:T(8,128)(2,1)S(1)}, bf16[4,16,768]{2,1,0:T(8,128)(2,1)S(1)}, u32[]{:S(2)}, u32[]{:S(2)}) collective-permute-start(bf16[4,16,768]{2,1,0:T(8,128)(2,1)S(1)} %get-tuple-element.272), channel_id=1, source_target_pairs={{1,0},{2,1},{3,2},{4,3},{5,4},{6,5},{7,6},{0,7},{9,8},{10,9},{11,1... | collective-permute-start | bytes 294920 | tf_op jit(solution)/shard_map/ppermute | solution.py:1169
  282.1 17.2 %collective-permute-start.2 = (bf16[4,16,768]{2,1,0:T(8,128)(2,1)S(1)}, bf16[4,16,768]{2,1,0:T(8,128)(2,1)S(1)}, u32[]{:S(2)}, u32[]{:S(2)}) collective-permute-start(bf16[4,16,768]{2,1,0:T(8,128)(2,1)S(1)} %get-tuple-element.273), channel_id=1, source_target_pairs={{0,1},{1,2},{2,3},{3,4},{4,5},{5,6},{6,7},{7,0},{8,9},{9,10},{10,1... | collective-permute-start | bytes 294920 | tf_op jit(solution)/shard_map/ppermute | solution.py:1170
  290.0 44.6 %collective-permute-start.6 = (bf16[2,2,2,96,768]{4,3,0,1,2:T(8,128)(2,1)}, bf16[2,2,2,96,768]{4,3,0,1,2:T(8,128)(2,1)}, u32[]{:S(2)}, u32[]{:S(2)}) collective-permute-start(bf16[2,2,2,96,768]{4,3,0,1,2:T(8,128)(2,1)} %copy.126), channel_id=1, source_target_pairs={{0,16},{8,24},{16,0},{24,8},{1,17},{9,25},{17,1},{25,9},{2,18},{10... | collective-permute-start | bytes 3538952 | tf_op jit(solution)/shard_map/ppermute | solution.py:1016
  299.1 40.3 %collective-permute-start.8 = (bf16[2,2,384,384]{3,2,0,1:T(8,128)(2,1)}, bf16[2,2,384,384]{3,2,0,1:T(8,128)(2,1)}, u32[]{:S(2)}, u32[]{:S(2)}) collective-permute-start(bf16[2,2,384,384]{3,2,0,1:T(8,128)(2,1)} %bitcast.148), channel_id=1, source_target_pairs={{0,1},{1,0},{2,3},{3,2},{4,5},{5,4},{6,7},{7,6},{8,9},{9,8},{10,11... | collective-permute-start | bytes 3538952 | tf_op jit(solution)/shard_map/ppermute | solution.py:1016
  325.1 8.9 %collective-permute-start.10 = (f32[72,128]{1,0:T(8,128)S(1)}, f32[72,128]{1,0:T(8,128)S(1)}, u32[]{:S(2)}, u32[]{:S(2)}) collective-permute-start(f32[72,128]{1,0:T(8,128)S(1)} %maximum_bitcast_fusion), channel_id=1, source_target_pairs={{0,8},{8,0},{16,24},{24,16},{1,9},{9,1},{17,25},{25,17},{2,10},{10... | collective-permute-start | bytes 110600 | tf_op jit(solution)/shard_map/ppermute | solution.py:1016
  327.5 54.0 %all-to-all-start.4 = ((bf16[8,80,384]{2,1,0:T(8,128)(2,1)}), bf16[8,80,384]{2,1,0:T(8,128)(2,1)}, u32[]{:S(2)}, u32[]{:S(2)}) async-start(bf16[8,80,384]{2,1,0:T(8,128)(2,1)} %broadcast_in_dim.44), calls=%async_computation.4 | async-start | bytes 983040 | tf_op jit(solution)/shard_map/all_to_all | solution.py:1024
  337.4 37.7 %collective-permute-start.7 = (bf16[2,2,96,768]{3,2,0,1:T(8,128)(2,1)S(1)}, bf16[2,2,96,768]{3,2,0,1:T(8,128)(2,1)}, u32[]{:S(2)}, u32[]{:S(2)}) collective-permute-start(bf16[2,2,96,768]{3,2,0,1:T(8,128)(2,1)S(1)} %fusion.7), channel_id=1, source_target_pairs={{0,1},{1,0},{2,3},{3,2},{4,5},{5,4},{6,7},{7,6},{8,9},{9,8},{10,11... | collective-permute-start | bytes 1769480 | tf_op jit(solution)/shard_map/ppermute | solution.py:1016
  343.9 34.8 %collective-permute-start.9 = (bf16[2,2,192,384]{3,2,0,1:T(8,128)(2,1)}, bf16[2,2,192,384]{3,2,0,1:T(8,128)(2,1)}, u32[]{:S(2)}, u32[]{:S(2)}) collective-permute-start(bf16[2,2,192,384]{3,2,0,1:T(8,128)(2,1)} %dynamic-slice_convert_fusion.4), channel_id=1, source_target_pairs={{0,16},{8,24},{16,0},{24,8},{1,17},{9,25},{17,1},{25,9},{2,18},{10... | collective-permute-start | bytes 1769480 | tf_op jit(solution)/shard_map/ppermute | solution.py:1016
  377.2 50.4 %collective-permute-start.11 = (bf16[2,96,768]{2,1,0:T(8,128)(2,1)}, bf16[2,96,768]{2,1,0:T(8,128)(2,1)}, u32[]{:S(2)}, u32[]{:S(2)}) collective-permute-start(bf16[2,96,768]{2,1,0:T(8,128)(2,1)} %fusion.8.refs_8_), channel_id=1, source_target_pairs={{0,2},{1,3},{2,0},{3,1},{4,6},{5,7},{6,4},{7,5},{8,10},{9,11},{10,... | collective-permute-start | bytes 884744 | tf_op jit(solution)/shard_map/ppermute | solution.py:1016
  399.4 30.9 %collective-permute-start.14 = (bf16[768,768]{1,0:T(8,128)(2,1)}, bf16[768,768]{1,0:T(8,128)(2,1)}, u32[]{:S(2)}, u32[]{:S(2)}) collective-permute-start(bf16[768,768]{1,0:T(8,128)(2,1)} %bitcast_select_fusion), channel_id=1, source_target_pairs={{0,8},{8,0},{16,24},{24,16},{1,9},{9,1},{17,25},{25,17},{2,10},{10... | collective-permute-start | bytes 3538952 | tf_op jit(solution)/shard_map/ppermute | solution.py:1016
  401.2 32.7 %all-to-all-start.5 = ((bf16[8,8,8,768]{3,2,1,0:T(8,128)(2,1)}), bf16[8,8,8,768]{3,2,1,0:T(8,128)(2,1)S(1)}, u32[]{:S(2)}, u32[]{:S(2)}) async-start(bf16[8,8,8,768]{3,2,1,0:T(8,128)(2,1)} %copy.100), calls=%async_computation.5 | async-start | bytes 1572864 | tf_op jit(solution)/shard_map/all_to_all | solution.py:1024
  405.1 21.9 %collective-permute-start.13 = (f32[72,128]{1,0:T(8,128)S(1)}, f32[72,128]{1,0:T(8,128)S(1)}, u32[]{:S(2)}, u32[]{:S(2)}) collective-permute-start(f32[72,128]{1,0:T(8,128)S(1)} %copy-done.28), channel_id=1, source_target_pairs={{0,4},{1,5},{2,6},{3,7},{4,0},{5,1},{6,2},{7,3},{8,12},{9,13},{10,... | collective-permute-start | bytes 110600 | tf_op jit(solution)/shard_map/ppermute | solution.py:1016
  408.0 21.4 %collective-permute-start.12 = (bf16[2,192,384]{2,1,0:T(8,128)(2,1)S(1)}, bf16[2,192,384]{2,1,0:T(8,128)(2,1)S(1)}, u32[]{:S(2)}, u32[]{:S(2)}) collective-permute-start(bf16[2,192,384]{2,1,0:T(8,128)(2,1)S(1)} %copy-done.26), channel_id=1, source_target_pairs={{0,2},{1,3},{2,0},{3,1},{4,6},{5,7},{6,4},{7,5},{8,10},{9,11},{10,... | collective-permute-start | bytes 884744 | tf_op jit(solution)/shard_map/ppermute | solution.py:1016
  455.4 22.5 %collective-permute-start.15 = (bf16[768,768]{1,0:T(8,128)(2,1)}, bf16[768,768]{1,0:T(8,128)(2,1)S(1)}, u32[]{:S(2)}, u32[]{:S(2)}) collective-permute-start(bf16[768,768]{1,0:T(8,128)(2,1)} %get-tuple-element.156), channel_id=1, source_target_pairs={{0,8},{8,0},{16,24},{24,16},{1,9},{9,1},{17,25},{25,17},{2,10},{10... | collective-permute-start | bytes 3538952 | tf_op jit(solution)/shard_map/ppermute | solution.py:1016
  455.5 15.8 %collective-permute-start.16 = (bf16[768,384]{1,0:T(8,128)(2,1)S(1)}, bf16[768,384]{1,0:T(8,128)(2,1)}, u32[]{:S(2)}, u32[]{:S(2)}) collective-permute-start(bf16[768,384]{1,0:T(8,128)(2,1)S(1)} %copy-done.25), channel_id=1, source_target_pairs={{0,16},{8,24},{16,0},{24,8},{1,17},{9,25},{17,1},{25,9},{2,18},{10... | collective-permute-start | bytes 1769480 | tf_op jit(solution)/shard_map/ppermute | solution.py:1016
  457.1 44.2 %collective-permute-start.25 = (bf16[96,768]{1,0:T(8,128)(2,1)}, bf16[96,768]{1,0:T(8,128)(2,1)}, u32[]{:S(2)}, u32[]{:S(2)}) collective-permute-start(bf16[96,768]{1,0:T(8,128)(2,1)} %fusion.14.refs_18_), channel_id=1, source_target_pairs={{0,4},{1,5},{2,6},{3,7},{4,0},{5,1},{6,2},{7,3},{8,12},{9,13},{10,... | collective-permute-start | bytes 442376 | tf_op jit(solution)/shard_map/ppermute | solution.py:1016
  457.3 51.6 %collective-permute-start.28 = (bf16[192,384]{1,0:T(8,128)(2,1)}, bf16[192,384]{1,0:T(8,128)(2,1)}, u32[]{:S(2)}, u32[]{:S(2)}) collective-permute-start(bf16[192,384]{1,0:T(8,128)(2,1)} %fusion.15.refs_19_), channel_id=1, source_target_pairs={{0,4},{1,5},{2,6},{3,7},{4,0},{5,1},{6,2},{7,3},{8,12},{9,13},{10,... | collective-permute-start | bytes 442376 | tf_op jit(solution)/shard_map/ppermute | solution.py:1016
  473.6 25.9 %all-to-all-start.7 = ((bf16[8,96,384]{2,1,0:T(8,128)(2,1)}), bf16[8,96,384]{2,1,0:T(8,128)(2,1)}, u32[]{:S(2)}, u32[]{:S(2)}) async-start(bf16[8,96,384]{2,1,0:T(8,128)(2,1)} %bitcast.49.refs_12_), calls=%async_computation.7 | async-start | bytes 1179648 | tf_op jit(solution)/shard_map/all_to_all | solution.py:1024
  479.2 26.0 %collective-permute-start.17 = (bf16[384,768]{1,0:T(8,128)(2,1)}, bf16[384,768]{1,0:T(8,128)(2,1)}, u32[]{:S(2)}, u32[]{:S(2)}) collective-permute-start(bf16[384,768]{1,0:T(8,128)(2,1)} %get-tuple-element.261.refs_11_), channel_id=1, source_target_pairs={{0,16},{8,24},{16,0},{24,8},{1,17},{9,25},{17,1},{25,9},{2,18},{10... | collective-permute-start | bytes 1769480 | tf_op jit(solution)/shard_map/ppermute | solution.py:1016
  505.1 6.9 %collective-permute-start.21 = (bf16[96,768]{1,0:T(8,128)(2,1)S(1)}, bf16[96,768]{1,0:T(8,128)(2,1)S(1)}, u32[]{:S(2)}, u32[]{:S(2)}) collective-permute-start(bf16[96,768]{1,0:T(8,128)(2,1)S(1)} %maximum_select_fusion.3), channel_id=1, source_target_pairs={{0,8},{8,0},{16,24},{24,16},{1,9},{9,1},{17,25},{25,17},{2,10},{10... | collective-permute-start | bytes 442376 | tf_op jit(solution)/shard_map/ppermute | solution.py:1016
  511.4 8.0 %collective-permute-start.24 = (f32[72,128]{1,0:T(8,128)S(1)}, f32[72,128]{1,0:T(8,128)S(1)}, u32[]{:S(2)}, u32[]{:S(2)}) collective-permute-start(f32[72,128]{1,0:T(8,128)S(1)} %add.223), channel_id=1, source_target_pairs={{0,16},{8,24},{16,0},{24,8},{1,17},{9,25},{17,1},{25,9},{2,18},{10... | collective-permute-start | bytes 110600 | tf_op jit(solution)/shard_map/ppermute | solution.py:1016
  512.8 19.7 %all-to-all-start.6 = ((bf16[8,384,96]{1,2,0:T(8,128)(2,1)}), bf16[8,384,96]{1,2,0:T(8,128)(2,1)S(1)}, u32[]{:S(2)}, u32[]{:S(2)}) async-start(bf16[8,384,96]{1,2,0:T(8,128)(2,1)} %bitcast.53), calls=%async_computation.6 | async-start | bytes 1179648 | tf_op jit(solution)/shard_map/all_to_all | solution.py:1024
  518.9 6.2 %collective-permute-start.29 = (bf16[192,384]{1,0:T(8,128)(2,1)S(1)}, bf16[192,384]{1,0:T(8,128)(2,1)S(1)}, u32[]{:S(2)}, u32[]{:S(2)}) collective-permute-start(bf16[192,384]{1,0:T(8,128)(2,1)S(1)} %fusion.12), channel_id=1, source_target_pairs={{0,16},{8,24},{16,0},{24,8},{1,17},{9,25},{17,1},{25,9},{2,18},{10... | collective-permute-start | bytes 442376 | tf_op jit(solution)/shard_map/ppermute | solution.py:1016
  525.2 12.0 %collective-permute-start.30 = (bf16[384,384]{1,0:T(8,128)(2,1)S(1)}, bf16[384,384]{1,0:T(8,128)(2,1)S(1)}, u32[]{:S(2)}, u32[]{:S(2)}) collective-permute-start(bf16[384,384]{1,0:T(8,128)(2,1)S(1)} %maximum_select_fusion.1), channel_id=1, source_target_pairs={{0,8},{8,0},{16,24},{24,16},{1,9},{9,1},{17,25},{25,17},{2,10},{10... | collective-permute-start | bytes 884744 | tf_op jit(solution)/shard_map/ppermute | solution.py:1016
  (48 other events, 255.4 us)

commit v3 on v2

--- a/solution.py
+++ b/solution.py
@@ -123,10 +123,11 @@
     @pl.when(i == 0)
     def _():
         for j, w in enumerate((wq, wk, wv)):
-            w_t[j] = w[...].T
+            w_t[j * D : (j + 1) * D, :] = w[...].T
 
     x = jnp.where(i < n_long, x_l[...], x_s[...])
-    made = [dot(w_t[j], x, 1, 1).astype(bf) for j in range(3)]
+    made = dot(w_t[...], x, 1, 1).astype(bf)
+    made = [made[j * D : (j + 1) * D] for j in range(3)]
 
     @pl.when(i < n_long)
     def _():
@@ -157,7 +158,7 @@
         in_specs=[SMEM_SPEC, row(long_at), row(first)] + [const_spec((D, D))] * 3,
         out_specs=[col(long_at)] * 3 + [col(first)] * 3 + [pl.BlockSpec((LM, D), lambda i: (0, 0))] * 2,
         out_shape=[sds((D, tl), bf)] * 3 + [sds((D, ts), bf)] * 3 + [sds((LM, D), bf)] * 2,
-        scratch_shapes=[pltpu.VMEM((3, D, D), bf)],
+        scratch_shapes=[pltpu.VMEM((3 * D, D), bf)],
         compiler_params=params(),
         cost_estimate=cost(6 * (tl + ts) * D * D, 8 * (tl + ts) * D),
         name="qkv",
@@ -282,6 +283,12 @@
     )(at, lq_l, lk_l, lq_s, lk_s)
 
 
+def put_all(out, marks, parts):
+    for d in range(out.shape[0]):
+        out[d, :LM, :] = marks
+        out[d, LM:, :] = parts
+
+
 def combine_kernel(senders, msg, z, out, bv_out):
     width = z.shape[1]
     most = jnp.concatenate([msg[d, LM : LM + 1, :] for d in range(senders)], axis=0)
@@ -297,8 +304,7 @@
             bv = bv + weight[s, d : d + 1] * msg[d, :LM, s]
         bv_out[:, s] = bv
         w_all.append(mm(z[:, s], bv))
-    out[:LM, :] = jnp.concatenate(w_all, axis=1).astype(bf)
-    out[LM:, :] = three_parts(top + jnp.log(total))
+    put_all(out, jnp.concatenate(w_all, axis=1).astype(bf), three_parts(top + jnp.log(total)))
 
 
 VMEM_SPEC = pl.BlockSpec(memory_space=pltpu.VMEM)
@@ -310,7 +316,7 @@
         functools.partial(combine_kernel, senders),
         in_specs=[VMEM_SPEC] * 2,
         out_specs=[VMEM_SPEC] * 2,
-        out_shape=[sds((LM + 16, width), bf), sds((LM, width), f32)],
+        out_shape=[sds((senders, LM + 16, width), bf), sds((LM, width), f32)],
         compiler_params=params(),
         cost_estimate=cost(1e8, 4e6),
         name="combine",
@@ -531,37 +537,6 @@
     return [copy]
 
 
-def column_jobs(acc, keep, send, core):
-    n = acc.shape[1] // D
-    jobs = []
-    for c in range(n):
-        half, at = c // (n // 2), (c % (n // 2)) * D
-        jobs.append((
-            lambda c=c: acc[:, c * D : (c + 1) * D],
-            lambda src, sem, half=half, at=at: to_side(
-                src, keep.at[:, at : at + D], send.at[:, at : at + D], core == half, sem
-            ),
-        ))
-    return jobs
-
-
-def row_jobs(acc, keep, send, core):
-    half = D // 2
-
-    def copies(src, sem, c):
-        out = []
-        for ref, which in ((keep, core), (send, 1 - core)):
-            start = pl.multiple_of(which * half, half)
-            out.append(pltpu.make_async_copy(src.at[pl.ds(start, half), :], ref.at[:, c * D : (c + 1) * D], sem))
-            out[-1].start()
-        return out
-
-    return [
-        (lambda c=c: acc[:, c * D : (c + 1) * D], lambda src, sem, c=c: copies(src, sem, c))
-        for c in range(acc.shape[1] // D)
-    ]
-
-
 def plain_job(acc, dst):
     def copies(src, sem):
         copy = pltpu.make_async_copy(src, dst, sem)
@@ -571,21 +546,60 @@
     return (lambda: acc[...], copies)
 
 
-def dense_kernel(n_long, chunk, core, x_l, x_s, o_l, o_s, c_l, c_s, w_out, w_up, w_down, g1, b1, bu, bd, g2, b2,
+def dense_kernel(n_long, tile, chunk, core, x_l, x_s, o_l, o_s, c_l, c_s, w_out, w_up, w_down, vecs, bu,
                  out_l, out_s, dr_l, dr_s, do_l, do_s, up_keep, up_send, dn_keep, dn_send, gout, small, small_up,
-                 acc_up, acc_dn, acc_out, act, dact, accs, accu, stage, sem):
+                 acc_up, acc_dn, acc_out, act, dact, accs, accu, x_b, o_b, c_b, out_b, dr_b, do_b,
+                 in_sem, out_sem, end_sem):
     i = pl.program_id(0)
     last = pl.num_programs(0) - 1
-    is_long = i < n_long
+    slot = lax.rem(i, 2)
+    g1, b1, bd, g2, b2 = (vecs.at[k : k + 1] for k in range(5))
+
+    def at(step):
+        return pl.ds(pl.multiple_of(step * tile, tile), tile)
+
+    def in_copies(step, to, refs):
+        x, o, c = refs
+        return [
+            pltpu.make_async_copy(x.at[at(step), :], x_b.at[to], in_sem.at[0, to]),
+            pltpu.make_async_copy(o.at[:, at(step)], o_b.at[to], in_sem.at[1, to]),
+            pltpu.make_async_copy(c.at[at(step), :], c_b.at[to], in_sem.at[2, to]),
+        ]
+
+    def fetch(step, to):
+        @pl.when(step < n_long)
+        def _():
+            for cp in in_copies(step, to, (x_l, o_l, c_l)):
+                cp.start()
+
+        @pl.when(step >= n_long)
+        def _():
+            for cp in in_copies(step - n_long, to, (x_s, o_s, c_s)):
+                cp.start()
+
+    def out_copies(step, refs):
+        out, dr, do = refs
+        return [
+            pltpu.make_async_copy(out_b, out.at[at(step), :], out_sem.at[0]),
+            pltpu.make_async_copy(dr_b, dr.at[at(step), :], out_sem.at[1]),
+            pltpu.make_async_copy(do_b, do.at[:, at(step)], out_sem.at[2]),
+        ]
 
     @pl.when(i == 0)
     def _():
+        fetch(i, slot)
         for ref in (acc_up, acc_dn, acc_out, accs, accu):
             ref[...] = jnp.zeros_like(ref)
 
-    x = jnp.where(is_long, x_l[...], x_s[...]).astype(f32)
-    o_t = jnp.where(is_long, o_l[...], o_s[...])
-    r1 = x + dot(o_t, w_out[...], 0, 0)
+    @pl.when(i < last)
+    def _():
+        fetch(i + 1, 1 - slot)
+
+    for cp in in_copies(0, slot, (x_s, o_s, c_s)):
+        cp.wait()
+
+    o_t = o_b[slot]
+    r1 = x_b[slot].astype(f32) + dot(o_t, w_out[...], 0, 0)
     cen = r1 - jnp.mean(r1, axis=-1, keepdims=True)
     rstd1 = lax.rsqrt(jnp.mean(cen * cen, axis=-1, keepdims=True) + EPSILON)
     xh1 = cen * rstd1
@@ -596,13 +610,19 @@
         a, dg = gelu_parts(dot(h1, w_up[:, cs], 1, 0) + bu[:, cs])
         a = a.astype(bf)
         act[:, cs] = a
-        dact[:, cs] = dg
+        dact[:, cs] = dg.astype(dact.dtype)
         r2 = r2 + dot(a, w_down[cs, :], 1, 0)
     cen2 = r2 - jnp.mean(r2, axis=-1, keepdims=True)
     rstd2 = lax.rsqrt(jnp.mean(cen2 * cen2, axis=-1, keepdims=True) + EPSILON)
     xh2 = cen2 * rstd2
-    out = (xh2 * g2[...] + b2[...]).astype(bf)
-    g = jnp.where(is_long, c_l[...], c_s[...]).astype(f32)
+
+    @pl.when(i > 0)
+    def _():
+        for cp in out_copies(0, (out_s, dr_s, do_s)):
+            cp.wait()
+
+    out_b[...] = (xh2 * g2[...] + b2[...]).astype(bf)
+    g = c_b[slot].astype(f32)
     dxh = g * g2[...]
     dr2 = rstd2 * (
         dxh - jnp.mean(dxh, axis=-1, keepdims=True) - xh2 * jnp.mean(dxh * xh2, axis=-1, keepdims=True)
@@ -616,7 +636,7 @@
     dh1 = dr2
     for c in range(FF // chunk):
         cs = slice(c * chunk, (c + 1) * chunk)
-        dp1 = (dot(dz2, w_down[cs, :], 1, 1) * dact[:, cs]).astype(bf)
+        dp1 = (dot(dz2, w_down[cs, :], 1, 1) * dact[:, cs].astype(f32)).astype(bf)
         accu[:, cs] += fold_rows(dp1.astype(f32))
         dh1 = dh1 + dot(dp1, w_up[:, cs], 1, 1)
         acc_up[:, cs] += dot(h1_t, dp1, 1, 0)
@@ -628,48 +648,81 @@
         dx - jnp.mean(dx, axis=-1, keepdims=True) - xh1 * jnp.mean(dx * xh1, axis=-1, keepdims=True)
     )
     da1 = dr1.astype(bf)
+    dr_b[...] = dr1
     acc_out[...] += dot(o_t, da1, 1, 0)
-    do_t = dot(w_out[...], da1, 1, 1).astype(bf)
-
-    @pl.when(is_long)
-    def _():
-        out_l[...] = out
-        dr_l[...] = dr1
-        do_l[...] = do_t
-
-    @pl.when(jnp.logical_not(is_long))
-    def _():
-        out_s[...] = out
-        dr_s[...] = dr1
-        do_s[...] = do_t
+    do_b[...] = dot(w_out[...], da1, 1, 1).astype(bf)
+
+    @pl.when(i < n_long)
+    def _():
+        for cp in out_copies(i, (out_l, dr_l, do_l)):
+            cp.start()
+
+    @pl.when(i >= n_long)
+    def _():
+        for cp in out_copies(i - n_long, (out_s, dr_s, do_s)):
+            cp.start()
 
     @pl.when(i == last)
     def _():
-        jobs = column_jobs(acc_up, up_keep, up_send, core[0])
-        jobs += row_jobs(acc_dn, dn_keep, dn_send, core[0])
-        put_bf16(jobs + [plain_job(acc_out, gout)], stage, sem)
+        slots = tile // 128
+        half = FF // 2
+        pend = []
+
+        def put(rows, copies):
+            k = len(pend)
+            if k >= slots:
+                for cp in pend[k - slots]:
+                    cp.wait()
+            part = act.at[(k % slots) * 128 : (k % slots + 1) * 128]
+            part[:, : rows.shape[1]] = rows.astype(bf)
+            pend.append(copies(part, end_sem.at[k % slots]))
+
+        def up_copies(part, sem, r):
+            out = []
+            for ref, which in ((up_keep, core[0]), (up_send, 1 - core[0])):
+                start = pl.multiple_of(which * half, half)
+                out.append(pltpu.make_async_copy(part.at[:, pl.ds(start, half)], ref.at[r : r + 128, :], sem))
+                out[-1].start()
+            return out
+
+        for r in range(0, D, 128):
+            put(acc_up[r : r + 128, :], lambda part, sem, r=r: up_copies(part, sem, r))
+        for r in range(0, D, 128):
+            into = r % (D // 2)
+            put(
+                acc_dn[r : r + 128, :],
+                lambda part, sem, r=r, into=into: to_side(
+                    part, dn_keep.at[into : into + 128, :], dn_send.at[into : into + 128, :], core[0] == r // (D // 2), sem
+                ),
+            )
+        for r in range(0, D, 128):
+            put(acc_out[r : r + 128, :], lambda part, sem, r=r: started(part.at[:, :D], gout.at[r : r + 128, :], sem))
         small[...] = jnp.sum(accs[...], axis=1)
         small_up[...] = jnp.sum(accu[...], axis=0, keepdims=True)
-
-
-def dense(core, x_l, x_s, o_l, o_s, c_l, c_s, w_out, w_up, w_down, g1, b1, bu, bd, g2, b2, tile=256, chunk=768):
+        for group in pend[-slots:]:
+            for cp in group:
+                cp.wait()
+        for cp in out_copies(0, (out_s, dr_s, do_s)):
+            cp.wait()
+
+
+def started(src, dst, sem):
+    copy = pltpu.make_async_copy(src, dst, sem)
+    copy.start()
+    return [copy]
+
+
+def dense(core, x_l, x_s, o_l, o_s, c_l, c_s, w_out, w_up, w_down, vecs, bu, tile=512, chunk=1536):
     nl, ns = x_l.shape[0] // tile, x_s.shape[0] // tile
-    long_at = lambda i: jnp.minimum(i, nl - 1)
-    short_at = lambda i: jnp.maximum(i - nl, 0)
-    row = lambda f: pl.BlockSpec((tile, D), lambda i: (f(i), 0))
-    col = lambda f: pl.BlockSpec((D, tile), lambda i: (0, f(i)))
-    anywhere = pl.BlockSpec(memory_space=pl.ANY)
     tl, ts = x_l.shape[0], x_s.shape[0]
-    vec = const_spec((1, D))
-    return pl.pallas_call(
-        functools.partial(dense_kernel, nl, chunk),
+    return pl.pallas_call(
+        functools.partial(dense_kernel, nl, tile, chunk),
         grid=(nl + ns,),
-        in_specs=[SMEM_SPEC, row(long_at), row(short_at), col(long_at), col(short_at), row(long_at), row(short_at)]
+        in_specs=[SMEM_SPEC]
+        + [ANY_SPEC] * 6
         + [const_spec((D, D)), const_spec((D, FF)), const_spec((FF, D))]
-        + [vec, vec, const_spec((1, FF)), vec, vec, vec],
-        out_specs=[row(long_at), row(short_at), row(long_at), row(short_at), col(long_at), col(short_at)]
-        + [anywhere] * 5
-        + [const_spec((6, D)), const_spec((1, FF))],
+        + [const_spec((8, D)), const_spec((1, FF))],
+        out_specs=[ANY_SPEC] * 11 + [const_spec((6, D)), const_spec((1, FF))],
         out_shape=[sds((tl, D), bf), sds((ts, D), bf), sds((tl, D), f32), sds((ts, D), f32)]
         + [sds((D, tl), bf), sds((D, ts), bf), sds((D, FF // 2), bf), sds((D, FF // 2), bf)]
         + [sds((D // 2, FF), bf), sds((D // 2, FF), bf), sds((D, D), bf)]
@@ -682,13 +735,20 @@
             pltpu.VMEM((tile, FF), f32),
             pltpu.VMEM((6, 8, D), f32),
             pltpu.VMEM((8, FF), f32),
-            pltpu.VMEM((2, D, D), bf),
-            pltpu.SemaphoreType.DMA((2,)),
+            pltpu.VMEM((2, tile, D), bf),
+            pltpu.VMEM((2, D, tile), bf),
+            pltpu.VMEM((2, tile, D), bf),
+            pltpu.VMEM((tile, D), bf),
+            pltpu.VMEM((tile, D), f32),
+            pltpu.VMEM((D, tile), bf),
+            pltpu.SemaphoreType.DMA((3, 2)),
+            pltpu.SemaphoreType.DMA((3,)),
+            pltpu.SemaphoreType.DMA((tile // 128,)),
         ],
         compiler_params=params(),
         cost_estimate=cost(2 * (tl + ts) * (3 * D * D + 6 * D * FF), 60e6, (tl + ts) * FF),
         name="dense",
-    )(core, x_l, x_s, o_l, o_s, c_l, c_s, w_out, w_up, w_down, g1, b1, bu, bd, g2, b2)
+    )(core, x_l, x_s, o_l, o_s, c_l, c_s, w_out, w_up, w_down, vecs, bu)
 
 
 def back_f_group(lk_g, w_g, q_g, up_g):
@@ -747,8 +807,7 @@
         dbv = mm(z[:, s], dw[:, s], 0, 0).astype(bf)
         dots.append(jnp.sum(dbv.astype(f32) * bv[:, s], axis=1, keepdims=True))
         dbvs.append(dbv)
-    out[:LM, :] = jnp.concatenate(dbvs, axis=1)
-    out[LM:, :] = three_parts(lanes_of([jnp.concatenate(dots, axis=0)])[:1])
+    put_all(out, jnp.concatenate(dbvs, axis=1), three_parts(lanes_of([jnp.concatenate(dots, axis=0)])[:1]))
 
 
 def back_mix(dw, z, bv, deps=()):
@@ -757,7 +816,7 @@
         after(functools.partial(back_mix_kernel, senders), 3, deps),
         in_specs=[VMEM_SPEC] * 3 + [ANY_SPEC] * len(deps),
         out_specs=[VMEM_SPEC] * 2,
-        out_shape=[sds((LM + 16, width), bf), sds((LM, width), f32)],
+        out_shape=[sds((senders, LM + 16, width), bf), sds((LM, width), f32)],
         compiler_params=params(),
         cost_estimate=cost(1e8, 4e6),
         name="back_mix",
@@ -815,53 +874,72 @@
     )(at, lq_l, lk_l, lq_s, lk_s, dw_l, bv_l, dw_s, bv_s, *deps)
 
 
-def back_b_group(lq_g, k_g, v_g, dbv_g, dots, dconv_g, probs):
-    wide = spread_heads(dbv_g)
+def back_b_group(k_g, v_g, wide, dots, probs):
     dsb = (probs * (dot(wide, v_g, 1, 0) - dots)).astype(bf)
-    dv = (dot(wide, probs.astype(bf), 0, 0) + dconv_g).astype(bf)
-    return dsb, dv, SCALE * pick_heads(dot(dsb, k_g, 1, 1))
-
-
-def back_b_kernel(units, lq, w, dbv, k, v, dconv, x, gv_in, dsb_out, dv_out, dlq_out, gv_out, acc):
-    i = pl.program_id(0)
-
-    @pl.when(i == 0)
-    def _():
-        acc[...] = gv_in[...]
-
+    return dsb, SCALE * pick_heads(dot(dsb, k_g, 1, 1))
+
+
+def back_b_kernel(units, lq, w, dbv, k, v, dsb_out, probs_out, dlq_out):
     level = from_parts(joined(w, units, slice(LM, LM + 16)))
     dots = from_parts(joined(dbv, units, slice(LM, LM + 16)))
     dbv_all = joined(dbv, units, slice(0, LM))
     for gs in group_slices():
         probs = jnp.exp(mark_scores(lq[:, gs], k[gs, :], None) - level[gs])
-        dsb_out[gs, :], dv, dlq_out[:, gs] = back_b_group(
-            lq[:, gs], k[gs, :], v[gs, :], dbv_all[:, gs], dots[gs], dconv[gs, :], probs
+        probs_out[gs, :] = probs.astype(bf)
+        dsb_out[gs, :], dlq_out[:, gs] = back_b_group(
+            k[gs, :], v[gs, :], spread_heads(dbv_all[:, gs]), dots[gs], probs
         )
-        dv_out[gs, :] = dv
-        acc[gs, :] += dot(dv, x[...], 1, 0)
-
-    @pl.when(i == pl.num_programs(0) - 1)
-    def _():
-        gv_out[...] = acc[...].astype(bf)
-
-
-def back_b(lq, w, dbv, k, v, dconv, x, gv, items, units, deps=()):
+
+
+def back_b(lq, w, dbv, k, v, items, units, deps=()):
     rows = k.shape[1] // items
     mark, tok = item_specs(rows)
     unit = unit_spec(units, LM + 16, D // units)
+    return pl.pallas_call(
+        after(functools.partial(back_b_kernel, units), 5, deps),
+        grid=(items,),
+        in_specs=[mark, unit, unit, tok, tok] + [ANY_SPEC] * len(deps),
+        out_specs=[tok, tok, mark],
+        out_shape=[sds(k.shape, bf), sds(k.shape, bf), sds((items * LM, D), f32)],
+        compiler_params=params(),
+        cost_estimate=cost(8 * items * rows * D * GROUP, 10 * items * rows * D, items * rows * D),
+        name="back_b",
+    )(lq, w, dbv, k, v, *deps)
+
+
+def back_v_kernel(units, dbv, probs, dconv, x, gv_in, dv_out, gv_out, acc):
+    i = pl.program_id(0)
+
+    @pl.when(i == 0)
+    def _():
+        acc[...] = gv_in[...]
+
+    dbv_all = joined(dbv, units, slice(0, LM))
+    for gs in group_slices():
+        dv_out[gs, :] = (dot(spread_heads(dbv_all[:, gs]), probs[gs, :], 0, 0) + dconv[gs, :]).astype(bf)
+    acc[...] += dot(dv_out[...], x[...], 1, 0)
+
+    @pl.when(i == pl.num_programs(0) - 1)
+    def _():
+        gv_out[...] = acc[...].T.astype(bf)
+
+
+def back_v(dbv, probs, dconv, x, gv, items, units, deps=()):
+    rows = probs.shape[1] // items
+    _, tok = item_specs(rows)
     square = const_spec((D, D))
     return pl.pallas_call(
-        after(functools.partial(back_b_kernel, units), 8, deps),
+        after(functools.partial(back_v_kernel, units), 5, deps),
         grid=(items,),
-        in_specs=[mark, unit, unit, tok, tok, tok, pl.BlockSpec((rows, D), lambda i: (i, 0)), square]
+        in_specs=[unit_spec(units, LM + 16, D // units), tok, tok, pl.BlockSpec((rows, D), lambda i: (i, 0)), square]
         + [ANY_SPEC] * len(deps),
-        out_specs=[tok, tok, mark, square],
-        out_shape=[sds(k.shape, bf), sds(k.shape, bf), sds((items * LM, D), f32), sds((D, D), bf)],
+        out_specs=[tok, square],
+        out_shape=[sds(probs.shape, bf), sds((D, D), bf)],
         scratch_shapes=[pltpu.VMEM((D, D), f32)],
         compiler_params=params(),
-        cost_estimate=cost(14 * items * rows * D * GROUP, 14 * items * rows * D, items * rows * D),
-        name="back_b",
-    )(lq, w, dbv, k, v, dconv, x, gv, *deps)
+        cost_estimate=cost(6 * items * rows * D * GROUP, 12 * items * rows * D),
+        name="back_v",
+    )(dbv, probs, dconv, x, gv, *deps)
 
 
 def short_back_kernel(length, q, k, v, lq, lk, z, w, bv, up, dconv, x, dsf_out, dsb_out, dv_out, dlq_out, dlk_out, dw_out, gv_out):
@@ -876,11 +954,10 @@
         scores = mark_scores(lq[:, gs], k[gs, :], length[0])
         e = jnp.exp(scores - jnp.max(scores, axis=1, keepdims=True))
         probs = e / jnp.sum(e, axis=1, keepdims=True)
-        dsb_out[gs, :], dv, dlq_out[:, gs] = back_b_group(
-            lq[:, gs], k[gs, :], v[gs, :], jnp.concatenate(dbvs, axis=1), dots, dconv[gs, :], probs
-        )
-        dv_out[gs, :] = dv
-        gv_out[gs, :] = dot(dv, x[...], 1, 0)
+        wide = spread_heads(jnp.concatenate(dbvs, axis=1))
+        dsb_out[gs, :], dlq_out[:, gs] = back_b_group(k[gs, :], v[gs, :], wide, dots, probs)
+        dv_out[gs, :] = (dot(wide, probs.astype(bf), 0, 0) + dconv[gs, :]).astype(bf)
+    gv_out[...] = dot(dv_out[...], x[...], 1, 0)
 
 
 def short_back(length, q, k, v, lq, lk, z, w, bv, up, dconv, x, deps=()):
@@ -904,7 +981,8 @@
         for gs in group_slices():
             part = (dot(spread_heads(marks[:, gs] * SCALE), scores[gs, :], 0, 0) + back[gs]).astype(bf)
             out[gs, :] = part
-            acc[n, gs, :] += dot(part, x[...], 1, 0)
+    both = jnp.concatenate([dq_out[...], dk_out[...]], axis=0)
+    acc[...] += dot(both, x[...], 1, 0)
 
 
 def score_grads_kernel(n_long, length, core, x_l, lq_l, lk_l, dsf_l, dsb_l, sq_l, sk_l,
@@ -929,8 +1007,8 @@
     @pl.when(i == n_long)
     def _():
         jobs = [
-            (lambda: acc[0], lambda src, sem: to_side(src, keep, send, core[0] == 0, sem)),
-            (lambda: acc[1], lambda src, sem: to_side(src, keep, send, core[0] == 1, sem)),
+            (lambda: acc[:D, :], lambda src, sem: to_side(src, keep, send, core[0] == 0, sem)),
+            (lambda: acc[D:, :], lambda src, sem: to_side(src, keep, send, core[0] == 1, sem)),
         ]
         put_bf16(jobs, stage, sem)
 
@@ -963,7 +1041,7 @@
         out_specs=[long_out] * 2 + [short_out] * 2 + [ANY_SPEC] * 2,
         out_shape=[sds((D, tl), bf)] * 2 + [sds((D, ts), bf)] * 2 + [sds((D, D), bf)] * 2,
         scratch_shapes=[
-            pltpu.VMEM((2, D, D), f32),
+            pltpu.VMEM((2 * D, D), f32),
             pltpu.VMEM((2, D, D), bf),
             pltpu.SemaphoreType.DMA((2,)),
         ],
@@ -973,13 +1051,18 @@
     )(length, core, *long_args, *short_args, *deps)
 
 
-def input_grad_kernel(n_long, dr_l, dq_l, dk_l, dv_l, dr_s, dq_s, dk_s, dv_s, wq, wk, wv, out_l, out_s):
+def input_grad_kernel(n_long, dr_l, dq_l, dk_l, dv_l, dr_s, dq_s, dk_s, dv_s, wq, wk, wv, out_l, out_s, w_all):
     i = pl.program_id(0)
     is_long = i < n_long
-    total = jnp.where(is_long, dr_l[...], dr_s[...])
-    for long_ref, short_ref, w in ((dq_l, dq_s, wq), (dk_l, dk_s, wk), (dv_l, dv_s, wv)):
-        grad = jnp.where(is_long, long_ref[...], short_ref[...])
-        total = total + dot(grad, w[...], 0, 1)
+    @pl.when(i == 0)
+    def _():
+        for j, w in enumerate((wq, wk, wv)):
+            w_all[:, j * D : (j + 1) * D] = w[...]
+
+    grad = jnp.concatenate(
+        [jnp.where(is_long, a[...], b[...]) for a, b in ((dq_l, dq_s), (dk_l, dk_s), (dv_l, dv_s))], axis=0
+    )
+    total = jnp.where(is_long, dr_l[...], dr_s[...]) + dot(grad, w_all[...], 0, 1)
     total = total.astype(bf)
 
     @pl.when(is_long)
@@ -1005,6 +1088,7 @@
         + [ANY_SPEC] * len(deps),
         out_specs=[row(at), row(first)],
         out_shape=[sds((tl, D), bf), sds((ts, D), bf)],
+        scratch_shapes=[pltpu.VMEM((D, 3 * D), bf)],
         compiler_params=params(),
         cost_estimate=cost(6 * (tl + ts) * D * D, 12 * (tl + ts) * D),
         name="input_grad",
@@ -1151,7 +1235,7 @@
 class SumStages:
     def __init__(self, values):
         self.values = values
-        self.steps = [("dp", 1), ("seq", 4), ("seq", 2), ("seq", 1), ("dp", 2)]
+        self.steps = [("dp", 1), ("dp", 2), ("seq", 4), ("seq", 2), ("seq", 1)]
 
     def step(self, dep):
         if is_small_mesh():
@@ -1231,14 +1315,14 @@
     got_l = exchange(pad_units(msg_l, n_seq))
     z_own, z_s = inverse(at, lq_l, lk_l, lq_s, lk_s, width)
     w_own, bv_own = combine(got_l, z_own)
-    w_l = gather(w_own)[:owners]
+    w_l = exchange(w_own)[:owners]
     o_s, w_s, bv_s = short_attend(length, q_s, k_s, v_s, lq_s, lk_s, z_s, c_s)
     o_l = mix(lk_l, w_l, q_l, c_l, items, units)
 
-    vec = lambda v: v.reshape(1, -1)
+    vecs = jnp.pad(jnp.stack([ln1_gain, ln1_bias, down_bias, ln2_gain, ln2_bias]), ((0, 3), (0, 0)))
     out_l, out_s, dr_l, dr_s, do_l, do_s, up_keep, up_send, dn_keep, dn_send, g_out, small, small_up = dense(
         core, x_l, x_s, o_l, o_s, cot_long.reshape(items * rows, D), cot_short.reshape(short_rows, D), w_out, w_up,
-        w_down, vec(ln1_gain), vec(ln1_bias), vec(up_bias), vec(down_bias), vec(ln2_gain), vec(ln2_bias),
+        w_down, vecs, up_bias.reshape(1, -1),
     )
 
     dw_l, dlk_part, dsf_l, edges = back_f(lk_l, w_l, q_l, do_l, items, units)
@@ -1257,12 +1341,12 @@
     packed = jnp.concatenate([small.reshape(-1), small_up.reshape(-1), tap_g[:, 0, :].reshape(-1)]).reshape(-1, 128)
     packed = SumStages(packed)
     dbv_own, dw_own = back_mix(got_dw, z_own, bv_own, (dv_s,))
-    dbv_l = gather(dbv_own)[:owners]
+    dbv_l = exchange(dbv_own)[:owners]
     dlq_own, dlk_own, dlq_own_s, dlk_own_s = back_inverse(
         at, lq_l, lk_l, lq_s, lk_s, dw_own, bv_own, dw_s, bv_s, (up.step(), down.step())
     )
-    dsb_l, dv_l, dlq_part, g_v = back_b(
-        lq_l, w_l, dbv_l, k_l, v_l, dc_l, x_l, gv_s, items, units, (up.step(), down.step(), packed.step(dw_own))
+    dsb_l, probs_l, dlq_part = back_b(
+        lq_l, w_l, dbv_l, k_l, v_l, items, units, (up.step(), down.step(), packed.step(dw_own))
     )
 
     owned = (jnp.arange(owners) == me).astype(f32).reshape(items, units, 1, 1)
@@ -1272,13 +1356,10 @@
 
     dl = jnp.stack([with_own(dlq_part, dlq_own), with_own(dlk_part, dlk_own)]).astype(bf)
     dl = dl.reshape(2 * items, n_seq, own_marks, D).transpose(1, 0, 2, 3)
+    dv_l, g_v = back_v(dbv_l, probs_l, dc_l, x_l, gv_s, items, units, (dl,))
     dl = jnp.sum(exchange(dl).astype(f32), axis=0) * (1.0 / seg)
     dl = jnp.pad(dl.reshape(2, items, own_marks, D), ((0, 0), (0, 0), (0, 16 - own_marks), (0, 0)))
     dl = dl.reshape(2, items * 16, D)
-
-    g_v = g_v.T
-    is_first = core[0] == 0
-    value_out = Reduction(jnp.where(is_first, g_v, g_out), jnp.where(is_first, g_out, g_v), 0)
 
     dq_l, dk_l, dq_s, dk_s, qk_keep, qk_send = score_grads(
         length,
@@ -1286,24 +1367,32 @@
         (x_l, lq_l, lk_l, dsf_l, dsb_l, dl[0], dl[1]),
         (x_s, lq_s, lk_s, dsf_s, dsb_s, dlq_s, dlk_s, dlq_own_s, dlk_own_s),
         items,
-        (up.step(), down.step(), packed.step(dlq_part), value_out.theirs),
+        (up.step(), down.step(), g_v, packed.step(dlq_part)),
     )
     query_key = Reduction(qk_keep, qk_send, 1)
+    is_first = core[0] == 0
+    vo_keep = hold(jnp.where(is_first, g_v, g_out), dq_l)
+    value_out = Halving(vo_keep, jnp.where(is_first, g_out, g_v), 0, ("y", "z0", "z1", "x"))
+    up.theirs, down.theirs = tied((up.theirs, down.theirs), dq_l)
     grad_l, grad_s = input_grad(
         (dr_l, dq_l, dk_l, dv_l),
         (dr_s, dq_s, dk_s, dv_s),
         (w_query, w_key, w_value),
-        (query_key.theirs, value_out.over_x()),
+        (query_key.theirs, value_out.theirs),
     )
     query_key.wait_for(grad_l)
     up.last()
     down.last()
     query_key.over_x()
     ready = query_key.value
-    up.own, down.own = hold(up.own, ready), hold(down.own, ready)
-    packed.step(grad_l)
+    up.own, down.own = tied((up.own, down.own), ready)
     packed.step(ready)
-    value_out.over_seq()
+    packed.step(ready)
+    value_out.wait_for(ready)
+    value_out.step()
+    value_out.step()
+    value_out.step()
+    value_out.last()
     query_key.over_seq()
     up_a, up_b = up.both()
     down_a, down_b = down.both()

time: 542 us -> 514 us (0.948)
  Pallas kernels: 317 us -> 298 us
  waiting for transfers between devices: 56.2 us -> 47.5 us
  local copies, waits for them, and re-layouts: 48.3 us -> 40.9 us
    pallas_call x2 -> x3, Pallas kernels: 160 us -> 143 us  [the longest x1 125 us: dense(): pl.pallas_call(functools.partial(dense_kernel, nl, tile, chunk), grid=(nl...]
    all_to_all x8 -> x7, waiting for transfers between devices: 17.6 us -> 10.4 us  [exchange(): return lax.all_to_all(values, 'seq', 0, 0, tiled=True)]
    add x10 -> x13, other arithmetic: 14.4 us -> 16.8 us  [pair_sum(): return keep.astype(f32) + swap(send, axis, bit).astype(f32)]
    ppermute x27 -> x30, starting transfers between devices: 25.3 us -> 27.4 us  [swap(): return lax.ppermute(values, axis, [(i, i ^ bit) for i in range(count)])]
    ppermute x27 -> x30, waiting for transfers between devices: 38.6 us -> 37.1 us  [swap(): return lax.ppermute(values, axis, [(i, i ^ bit) for i in range(count)])]
    all_to_all x8 -> x7, starting transfers between devices: 38.9 us -> 37.6 us  [exchange(): return lax.all_to_all(values, 'seq', 0, 0, tiled=True)]
  transfers between devices with their start and end apart: 39 -> 41, of which waited for: 9 -> 11; matrix products, arithmetic and copies ran while one was open for 14% -> 14% of each run, Pallas kernels for 27% -> 31%
where the time goes in v3:
time: 514 us; the launch traced here: 507 us
  Pallas kernels  298 us (58%)
  starting transfers between devices  75.8 us (15%)
  waiting for transfers between devices  47.5 us (9%)
  local copies, waits for them, and re-layouts  40.9 us (8%)
  other arithmetic  35.3 us (7%)
  matrix products  6.7 us (1%)
    pallas_call x1, Pallas kernels, dense(): pl.pallas_call(functools.partial(dense_kernel, nl, tile, chunk), grid=(nl...  125 us
    all_to_all x7, starting transfers between devices, exchange(): return lax.all_to_all(values, 'seq', 0, 0, tiled=True)  37.6 us
    ppermute x30, waiting for transfers between devices, swap(): return lax.ppermute(values, axis, [(i, i ^ bit) for i in range(count)])  37.1 us
    pallas_call x1, Pallas kernels, back_inverse(): pl.pallas_call(after(back_inverse_kernel, 9, deps), grid_spec=pltpu.Prefe...  28.3 us
    ppermute x30, starting transfers between devices, swap(): return lax.ppermute(values, axis, [(i, i ^ bit) for i in range(count)])  27.4 us
    pallas_call x1, Pallas kernels, qkv(): pl.pallas_call(functools.partial(qkv_kernel, nl), grid=(nl + 1,), in_spec...  17.8 us
    pallas_call x1, Pallas kernels, score_grads(): pl.pallas_call(after(functools.partial(score_grads_kernel, items), 18, de...  17.7 us
    pallas_call x1, Pallas kernels, input_grad(): pl.pallas_call(after(functools.partial(input_grad_kernel, nl), 11, deps),...  17.1 us
  transfers between devices with their start and end apart: 41, of which 11 were waited for; matrix products, arithmetic and copies ran while one was open for 14% of the time, Pallas kernels for 31%

profile of v3, /device:TPU:0, one launch (start us, length us, event | category | flops | bytes accessed | tf_op | source)
XLA Modules:
  0.0 507.1 jit_solution(14111328773724019135)
XLA Ops:
  11.8 3.5 all-to-all-start
  18.6 17.8 %qkv.1 = (bf16[768,2048]{1,0:T(8,128)(2,1)}, bf16[768,2048]{1,0:T(8,128)(2,1)}, bf16[768,2048]{1,0:T(8,128)(2,1)}, bf16[768,512]{1,0:T(8,128)(2,1)}, bf16[768,51...) custom-call(s32[1]{0:T(128)} %bitcast.177.length, ...), custom_call_target="tpu_custom_call" | custom-call | flops 9059696640 | bytes 15728640 | tf_op jit(solution)/shard_map/qkv/pallas_call | solution.py:155
  43.1 7.3 %stats.1 = f32[8,72,384]{2,1,0:T(8,128)} custom-call(bf16[256,768]{1,0:T(8,128)(2,1)} %fusion.1.lq.lq_l.refs_0_.refs_1_.refs_3_, bf16[768,2048]{1,0:T(8,128)(2,1)} %get-tuple-element.96.k.refs_3_, bf16[768,2048]{1,0:T(8,128)(2,1)} %get-tuple-element.97.v.v_l.refs_1_.refs_4_), custom_call_target="tpu_custom_call" | custom-call | flops 1610612736 | bytes 6291456 | tf_op jit(solution)/shard_map/stats/pallas_call | solution.py:205
  50.4 6.4 %all-to-all-start.1 = ((f32[8,72,384]{2,1,0:T(8,128)}), f32[8,72,384]{2,1,0:T(8,128)S(1)}, u32[]{:S(2)}, u32[]{:S(2)}) async-start(f32[8,72,384]{2,1,0:T(8,128)} %stats.1), calls=%async_computation.1 | async-start | bytes 1769472 | tf_op jit(solution)/shard_map/all_to_all | solution.py:1108
  59.2 9.1 %inverse.1 = (f32[64,384]{1,0:T(8,128)}, f32[64,768]{1,0:T(8,128)}) custom-call(s32[2]{0:T(128)} %pad_add_fusion.at.refs_0_, bf16[256,768]{1,0:T(8,128)(2,1)} %fusion.1.lq.lq_l.refs_0_.refs_1_.refs_3_, bf16[256,768]{1,0:T(8,128)(2,1)} %fusion.lk_l.lk.refs_2_.refs_4_, bf16[64,768]{1,0:T(8,128)(2,1)} %get-tuple-element.98.lq_s.lq.refs_4_.refs_3_.refs_10_, ...), custom_call_target="tpu_custom_call" | custom-call | flops 13589544960 | bytes 1000000 | tf_op jit(solution)/shard_map/inverse/pallas_call | solution.py:271
  68.3 10.4 %all-to-all-done.1.msg = f32[8,72,384]{2,1,0:T(8,128)S(1)} async-done(((f32[8,72,384]{2,1,0:T(8,128)}), f32[8,72,384]{2,1,0:T(8,128)S(1)}, u32[]{:S(2)}, u32[]{:S(2)}) %all-to-all-start.1) | async-done | bytes 884768 | tf_op jit(solution)/shard_map/all_to_all | solution.py:1108
  79.6 3.1 combine.1
  82.7 4.3 all-to-all-start.2
  89.3 8.2 %conv.1 = (f32[768,2048]{1,0:T(8,128)}, f32[768,512]{1,0:T(8,128)}) custom-call(s32[1]{0:T(128)} %bitcast.178.length, bf16[768,2048]{1,0:T(8,128)(2,1)} %get-tuple-element.97.v.v_l.refs_1_.refs_4_, bf16[768,512]{1,0:T(8,128)(2,1)} %get-tuple-element.103.v_s.v.refs_2_.refs_3_, bf16[768,128]{1,0:T(8,128)(2,1)} %fusion.4.rim.refs_3_, ...), custom_call_target="tpu_custom_call" | custom-call | flops 3221225472 | bytes 12582912 | tf_op jit(solution)/shard_map/conv/pallas_call | solution.py:454
  97.5 6.5 %short_attend.1 = (bf16[768,512]{1,0:T(8,128)(2,1)}, bf16[64,768]{1,0:T(8,128)(2,1)}, f32[64,768]{1,0:T(8,128)}) custom-call(s32[1]{0:T(128)} %bitcast.179.length, bf16[768,512]{1,0:T(8,128)(2,1)} %get-tuple-element.105.q.refs_1_, bf16[768,512]{1,0:T(8,128)(2,1)} %get-tuple-element.106.k.refs_2_, bf16[768,512]{1,0:T(8,128)(2,1)} %get-tuple-element.103.v_s.v.refs_2_.refs_3_, ...), custom_call_target="tpu_custom_call" | custom-call | flops 805306368 | bytes 3932160 | tf_op jit(solution)/shard_map/short_attend/pallas_call | solution.py:355
  104.8 8.9 %mix.1.o_l = bf16[768,2048]{1,0:T(8,128)(2,1)} custom-call(bf16[256,768]{1,0:T(8,128)(2,1)} %fusion.lk_l.lk.refs_2_.refs_4_, bf16[8,80,384]{2,1,0:T(8,128)(2,1)} %copy-done.18, bf16[768,2048]{1,0:T(8,128)(2,1)} %get-tuple-element.102.q, f32[768,2048]{1,0:T(8,128)} %get-tuple-element.104.conv), custom_call_target="tpu_custom_call" | custom-call | flops 1610612736 | bytes 12582912 | tf_op jit(solution)/shard_map/mix/pallas_call | solution.py:373
  113.8 124.5 %dense.1 = (bf16[2048,768]{1,0:T(8,128)(2,1)}, bf16[512,768]{1,0:T(8,128)(2,1)}, f32[2048,768]{1,0:T(8,128)}, f32[512,768]{1,0:T(8,128)}, bf16[768,2048]{1,0:T(8...) custom-call(s32[1]{0:T(128)} %bitcast.core.refs_1_, ...), custom_call_target="tpu_custom_call" | custom-call | flops 81537269760 | bytes 60000000 | tf_op jit(solution)/shard_map/dense/pallas_call | solution.py:718
  239.6 8.7 %back_f.1 = (f32[8,64,384]{2,1,0:T(8,128)}, f32[256,768]{1,0:T(8,128)}, bf16[768,2048]{1,0:T(8,128)(2,1)}, bf16[4,32,768]{2,1,0:T(8,128)(2,1)}) custom-call(bf16[256,768]{1,0:T(8,128)(2,1)} %fusion.lk_l.lk.refs_2_.refs_4_, bf16[8,80,384]{2,1,0:T(8,128)(2,1)} %copy-done.18, bf16[768,2048]{1,0:T(8,128)(2,1)} %get-tuple-element.102.q, ...), custom_call_target="tpu_custom_call" | custom-call | flops 3221225472 | bytes 9437184 | tf_op jit(solution)/shard_map/back_f/pallas_call | solution.py:782
  248.3 6.1 %all-to-all-start.3 = ((f32[8,64,384]{2,1,0:T(8,128)}), f32[8,64,384]{2,1,0:T(8,128)S(1)}, u32[]{:S(2)}, u32[]{:S(2)}) async-start(f32[8,64,384]{2,1,0:T(8,128)} %get-tuple-element.115), calls=%async_computation.3 | async-start | bytes 1572864 | tf_op jit(solution)/shard_map/all_to_all | solution.py:1108
  254.4 4.8 collective-permute-start.3
  277.4 10.8 %conv_back.1 = (f32[768,2048]{1,0:T(8,128)}, f32[768,512]{1,0:T(8,128)}, f32[12,8,128]{2,1,0:T(8,128)}) custom-call(s32[1]{0:T(128)} %bitcast.180.refs_0_, bf16[768,2048]{1,0:T(8,128)(2,1)} %get-tuple-element.97.v.v_l.refs_1_.refs_4_, bf16[768,512]{1,0:T(8,128)(2,1)} %get-tuple-element.103.v_s.v.refs_2_.refs_3_, bf16[768,128]{1,0:T(8,128)(2,1)} %fusion.4.rim.refs_3_, ...), custom_call_target="tpu_custom_call" | custom-call | flops 4831838208 | bytes 18874368 | tf_op jit(solution)/shard_map/conv_back/pallas_call | solution.py:485
  288.1 9.1 %short_back.1 = (bf16[768,512]{1,0:T(8,128)(2,1)}, bf16[768,512]{1,0:T(8,128)(2,1)}, bf16[768,512]{1,0:T(8,128)(2,1)}, f32[64,768]{1,0:T(8,128)}, f32[64,768]{1,...) custom-call(s32[1]{0:T(128)} %bitcast.181.refs_0_, bf16[768,512]{1,0:T(8,128)(2,1)} %get-tuple-element.105.q.refs_1_, ...), custom_call_target="tpu_custom_call" | custom-call | flops 2415919104 | bytes 7864320 | tf_op jit(solution)/shard_map/short_back/pallas_call | solution.py:965
  302.7 6.5 %all-to-all-start.4 = ((bf16[8,80,384]{2,1,0:T(8,128)(2,1)}), bf16[8,80,384]{2,1,0:T(8,128)(2,1)}, u32[]{:S(2)}, u32[]{:S(2)}) async-start(bf16[8,80,384]{2,1,0:T(8,128)(2,1)} %get-tuple-element.131), calls=%async_computation.4 | async-start | bytes 983040 | tf_op jit(solution)/shard_map/all_to_all | solution.py:1108
  319.7 28.3 %back_inverse.1 = (f32[64,384]{1,0:T(8,128)}, f32[64,384]{1,0:T(8,128)}, f32[64,768]{1,0:T(8,128)}, f32[64,768]{1,0:T(8,128)}) custom-call(s32[2]{0:T(128)} %pad_add_fusion.at.refs_0_, bf16[256,768]{1,0:T(8,128)(2,1)} %fusion.1.lq.lq_l.refs_0_.refs_1_.refs_3_, bf16[256,768]{1,0:T(8,128)(2,1)} %fusion.lk_l.lk.refs_2_.refs_4_, ...), custom_call_target="tpu_custom_call" | custom-call | flops 40768634880 | bytes 2000000 | tf_op jit(solution)/shard_map/back_inverse/pallas_call | solution.py:862
  355.8 8.1 %back_b.1 = (bf16[768,2048]{1,0:T(8,128)(2,1)}, bf16[768,2048]{1,0:T(8,128)(2,1)}, f32[256,768]{1,0:T(8,128)}) custom-call(bf16[256,768]{1,0:T(8,128)(2,1)} %fusion.1.lq.lq_l.refs_0_.refs_1_.refs_3_, bf16[8,80,384]{2,1,0:T(8,128)(2,1)} %copy-done.18, bf16[8,80,384]{2,1,0:T(8,128)(2,1)} %all-to-all-done.4.refs_2_.refs_0_, ...), custom_call_target="tpu_custom_call" | custom-call | flops 3221225472 | bytes 15728640 | tf_op jit(solution)/shard_map/back_b/pallas_call | solution.py:898
  366.2 4.8 all-to-all-start.5
  374.6 10.4 %back_v.1 = (bf16[768,2048]{1,0:T(8,128)(2,1)}, bf16[768,768]{1,0:T(8,128)(2,1)}) custom-call(bf16[8,80,384]{2,1,0:T(8,128)(2,1)} %all-to-all-done.4.refs_2_.refs_0_, bf16[768,2048]{1,0:T(8,128)(2,1)} %get-tuple-element.149.refs_1_, f32[768,2048]{1,0:T(8,128)} %get-tuple-element.150.refs_2_, bf16[2048,768]{1,0:T(8,128)(2,1)} %bitcast.186, ...), custom_call_target="tpu_custom_call" | custom-call | flops 2415919104 | bytes 18874368 | tf_op jit(solution)/shard_map/back_v/pallas_call | solution.py:931
  385.0 3.3 broadcast_select_fusion.1
  388.9 5.0 collective-permute-done.11
  401.9 17.7 %score_grads.1 = (bf16[768,2048]{1,0:T(8,128)(2,1)}, bf16[768,2048]{1,0:T(8,128)(2,1)}, bf16[768,512]{1,0:T(8,128)(2,1)}, bf16[768,512]{1,0:T(8,128)(2,1)}, bf16...) custom-call(s32[1]{0:T(128)} %bitcast.182.refs_0_, s32[1]{0:T(128)} %bitcast.core.refs_1_, bf16[2048,768]{1,0:T(8,128)(2,1)} %bitcast.187, ...), custom_call_target="tpu_custom_call" | custom-call | flops 9059696640 | bytes 39321600 | tf_op jit(solution)/shard_map/score_grads/pallas_call | solution.py:1033
  427.1 5.9 %collective-permute-done.28 = bf16[96,768]{1,0:T(8,128)(2,1)S(1)} collective-permute-done((bf16[96,768]{1,0:T(8,128)(2,1)S(1)}, bf16[96,768]{1,0:T(8,128)(2,1)S(1)}, u32[]{:S(2)}, u32[]{:S(2)}) %collective-permute-start.28) | collective-permute-done | bytes 147488 | tf_op jit(solution)/shard_map/ppermute | solution.py:1100
  436.0 17.1 %input_grad.1 = (bf16[2048,768]{1,0:T(8,128)(2,1)}, bf16[512,768]{1,0:T(8,128)(2,1)}) custom-call(f32[2048,768]{1,0:T(8,128)} %get-tuple-element.112.refs_0_, bf16[768,2048]{1,0:T(8,128)(2,1)} %get-tuple-element.154.refs_1_, bf16[768,2048]{1,0:T(8,128)(2,1)} %get-tuple-element.155.refs_2_, bf16[768,2048]{1,0:T(8,128)(2,1)} %get-tuple-element.156.refs_3_, ...), custom_call_target="tpu_custom_call" | custom-call | flops 9059696640 | bytes 23592960 | tf_op jit(solution)/shard_map/input_grad/pallas_call | solution.py:1084
  456.6 6.0 %all-to-all-start.6 = ((bf16[8,384,96]{1,2,0:T(8,128)(2,1)}), bf16[8,384,96]{1,2,0:T(8,128)(2,1)S(1)}, u32[]{:S(2)}, u32[]{:S(2)}) async-start(bf16[8,384,96]{1,2,0:T(8,128)(2,1)} %bitcast.53), calls=%async_computation.6 | async-start | bytes 1179648 | tf_op jit(solution)/shard_map/all_to_all | solution.py:1108
  468.0 4.2 collective-permute-done.26
  478.4 4.2 collective-permute-done.20
  485.4 5.3 %collective-permute-done.21 = bf16[96,768]{1,0:T(8,128)(2,1)S(1)} collective-permute-done((bf16[96,768]{1,0:T(8,128)(2,1)S(1)}, bf16[96,768]{1,0:T(8,128)(2,1)S(1)}, u32[]{:S(2)}, u32[]{:S(2)}) %collective-permute-start.21) | collective-permute-done | bytes 147488 | tf_op jit(solution)/shard_map/ppermute | solution.py:1100
  495.9 3.8 collective-permute-done.23
  (256 shorter events, 124.7 us)
Async XLA Ops:
  2.3 34.7 %collective-permute-start = (bf16[4,16,768]{2,1,0:T(8,128)(2,1)S(1)}, bf16[4,16,768]{2,1,0:T(8,128)(2,1)S(1)}, u32[]{:S(2)}, u32[]{:S(2)}) collective-permute-start(bf16[4,16,768]{2,1,0:T(8,128)(2,1)S(1)} %get-tuple-element.230), channel_id=1, source_target_pairs={{0,1},{1,2},{2,3},{3,4},{4,5},{5,6},{6,7},{7,0},{8,9},{9,10},{10,1... | collective-permute-start | bytes 294920 | tf_op jit(solution)/shard_map/ppermute | solution.py:1254
  5.2 81.7 %collective-permute-start.1 = (bf16[4,16,768]{2,1,0:T(8,128)(2,1)}, bf16[4,16,768]{2,1,0:T(8,128)(2,1)}, u32[]{:S(2)}, u32[]{:S(2)}) collective-permute-start(bf16[4,16,768]{2,1,0:T(8,128)(2,1)} %get-tuple-element.231), channel_id=1, source_target_pairs={{1,0},{2,1},{3,2},{4,3},{5,4},{6,5},{7,6},{0,7},{9,8},{10,9},{11,1... | collective-permute-start | bytes 294920 | tf_op jit(solution)/shard_map/ppermute | solution.py:1253
  11.8 25.9 %all-to-all-start = ((f32[8,32,768]{2,1,0:T(8,128)}), f32[8,32,768]{2,1,0:T(8,128)S(1)}, u32[]{:S(2)}, u32[]{:S(2)}) async-start(f32[8,32,768]{2,1,0:T(8,128)} %broadcast_in_dim.28), calls=%async_computation | async-start | bytes 1572864 | tf_op jit(solution)/shard_map/all_to_all | solution.py:1108
  50.4 28.3 %all-to-all-start.1 = ((f32[8,72,384]{2,1,0:T(8,128)}), f32[8,72,384]{2,1,0:T(8,128)S(1)}, u32[]{:S(2)}, u32[]{:S(2)}) async-start(f32[8,72,384]{2,1,0:T(8,128)} %stats.1), calls=%async_computation.1 | async-start | bytes 1769472 | tf_op jit(solution)/shard_map/all_to_all | solution.py:1108
  82.7 21.3 %all-to-all-start.2 = ((bf16[8,80,384]{2,1,0:T(8,128)(2,1)}), bf16[8,80,384]{2,1,0:T(8,128)(2,1)S(1)}, u32[]{:S(2)}, u32[]{:S(2)}) async-start(bf16[8,80,384]{2,1,0:T(8,128)(2,1)} %get-tuple-element.101), calls=%async_computation.2 | async-start | bytes 983040 | tf_op jit(solution)/shard_map/all_to_all | solution.py:1108
  238.3 20.9 %collective-permute-start.4 = (bf16[768,1536]{1,0:T(8,128)(2,1)}, bf16[768,1536]{1,0:T(8,128)(2,1)}, u32[]{:S(2)}, u32[]{:S(2)}) collective-permute-start(bf16[768,1536]{1,0:T(8,128)(2,1)} %get-tuple-element.124), channel_id=1, source_target_pairs={{0,8},{8,0},{16,24},{24,16},{1,9},{9,1},{17,25},{25,17},{2,10},{10... | collective-permute-start | bytes 7077896 | tf_op jit(solution)/shard_map/ppermute | solution.py:1100
  238.3 30.2 %collective-permute-start.5 = (bf16[384,3072]{1,0:T(8,128)(2,1)}, bf16[384,3072]{1,0:T(8,128)(2,1)}, u32[]{:S(2)}, u32[]{:S(2)}) collective-permute-start(bf16[384,3072]{1,0:T(8,128)(2,1)} %get-tuple-element.126), channel_id=1, source_target_pairs={{0,8},{8,0},{16,24},{24,16},{1,9},{9,1},{17,25},{25,17},{2,10},{10... | collective-permute-start | bytes 7077896 | tf_op jit(solution)/shard_map/ppermute | solution.py:1100
  248.3 48.9 %all-to-all-start.3 = ((f32[8,64,384]{2,1,0:T(8,128)}), f32[8,64,384]{2,1,0:T(8,128)S(1)}, u32[]{:S(2)}, u32[]{:S(2)}) async-start(f32[8,64,384]{2,1,0:T(8,128)} %get-tuple-element.115), calls=%async_computation.3 | async-start | bytes 1572864 | tf_op jit(solution)/shard_map/all_to_all | solution.py:1108
  254.4 22.0 %collective-permute-start.3 = (bf16[4,16,768]{2,1,0:T(8,128)(2,1)S(1)}, bf16[4,16,768]{2,1,0:T(8,128)(2,1)S(1)}, u32[]{:S(2)}, u32[]{:S(2)}) collective-permute-start(bf16[4,16,768]{2,1,0:T(8,128)(2,1)S(1)} %get-tuple-element.252), channel_id=1, source_target_pairs={{1,0},{2,1},{3,2},{4,3},{5,4},{6,5},{7,6},{0,7},{9,8},{10,9},{11,1... | collective-permute-start | bytes 294920 | tf_op jit(solution)/shard_map/ppermute | solution.py:1253
  259.2 17.3 %collective-permute-start.2 = (bf16[4,16,768]{2,1,0:T(8,128)(2,1)S(1)}, bf16[4,16,768]{2,1,0:T(8,128)(2,1)S(1)}, u32[]{:S(2)}, u32[]{:S(2)}) collective-permute-start(bf16[4,16,768]{2,1,0:T(8,128)(2,1)S(1)} %get-tuple-element.253), channel_id=1, source_target_pairs={{0,1},{1,2},{2,3},{3,4},{4,5},{5,6},{6,7},{7,0},{8,9},{9,10},{10,1... | collective-permute-start | bytes 294920 | tf_op jit(solution)/shard_map/ppermute | solution.py:1254
  267.0 42.8 %collective-permute-start.6 = (bf16[2,2,2,96,768]{4,3,0,1,2:T(8,128)(2,1)}, bf16[2,2,2,96,768]{4,3,0,1,2:T(8,128)(2,1)}, u32[]{:S(2)}, u32[]{:S(2)}) collective-permute-start(bf16[2,2,2,96,768]{4,3,0,1,2:T(8,128)(2,1)} %copy.105), channel_id=1, source_target_pairs={{0,16},{8,24},{16,0},{24,8},{1,17},{9,25},{17,1},{25,9},{2,18},{10... | collective-permute-start | bytes 3538952 | tf_op jit(solution)/shard_map/ppermute | solution.py:1100
  276.2 38.4 %collective-permute-start.8 = (bf16[2,2,384,384]{3,2,0,1:T(8,128)(2,1)}, bf16[2,2,384,384]{3,2,0,1:T(8,128)(2,1)}, u32[]{:S(2)}, u32[]{:S(2)}) collective-permute-start(bf16[2,2,384,384]{3,2,0,1:T(8,128)(2,1)} %bitcast.175), channel_id=1, source_target_pairs={{0,1},{1,0},{2,3},{3,2},{4,5},{5,4},{6,7},{7,6},{8,9},{9,8},{10,11... | collective-permute-start | bytes 3538952 | tf_op jit(solution)/shard_map/ppermute | solution.py:1100
  302.7 53.1 %all-to-all-start.4 = ((bf16[8,80,384]{2,1,0:T(8,128)(2,1)}), bf16[8,80,384]{2,1,0:T(8,128)(2,1)}, u32[]{:S(2)}, u32[]{:S(2)}) async-start(bf16[8,80,384]{2,1,0:T(8,128)(2,1)} %get-tuple-element.131), calls=%async_computation.4 | async-start | bytes 983040 | tf_op jit(solution)/shard_map/all_to_all | solution.py:1108
  312.6 38.3 %collective-permute-start.7 = (bf16[2,2,96,768]{3,2,0,1:T(8,128)(2,1)S(1)}, bf16[2,2,96,768]{3,2,0,1:T(8,128)(2,1)}, u32[]{:S(2)}, u32[]{:S(2)}) collective-permute-start(bf16[2,2,96,768]{3,2,0,1:T(8,128)(2,1)S(1)} %fusion.7), channel_id=1, source_target_pairs={{0,1},{1,0},{2,3},{3,2},{4,5},{5,4},{6,7},{7,6},{8,9},{9,8},{10,11... | collective-permute-start | bytes 1769480 | tf_op jit(solution)/shard_map/ppermute | solution.py:1100
  319.1 33.9 %collective-permute-start.9 = (bf16[2,2,192,384]{3,2,0,1:T(8,128)(2,1)}, bf16[2,2,192,384]{3,2,0,1:T(8,128)(2,1)}, u32[]{:S(2)}, u32[]{:S(2)}) collective-permute-start(bf16[2,2,192,384]{3,2,0,1:T(8,128)(2,1)} %dynamic-slice_convert_fusion.2), channel_id=1, source_target_pairs={{0,16},{8,24},{16,0},{24,8},{1,17},{9,25},{17,1},{25,9},{2,18},{10... | collective-permute-start | bytes 1769480 | tf_op jit(solution)/shard_map/ppermute | solution.py:1100
  366.2 34.8 %all-to-all-start.5 = ((bf16[8,8,8,768]{3,2,1,0:T(8,128)(2,1)}), bf16[8,8,8,768]{3,2,1,0:T(8,128)(2,1)S(1)}, u32[]{:S(2)}, u32[]{:S(2)}) async-start(bf16[8,8,8,768]{3,2,1,0:T(8,128)(2,1)} %bitcast.176.refs_5_), calls=%async_computation.5 | async-start | bytes 1572864 | tf_op jit(solution)/shard_map/all_to_all | solution.py:1108
  371.0 22.9 %collective-permute-start.11 = (bf16[2,96,768]{2,1,0:T(8,128)(2,1)}, bf16[2,96,768]{2,1,0:T(8,128)(2,1)}, u32[]{:S(2)}, u32[]{:S(2)}) collective-permute-start(bf16[2,96,768]{2,1,0:T(8,128)(2,1)} %fusion.10.refs_5_), channel_id=1, source_target_pairs={{0,2},{1,3},{2,0},{3,1},{4,6},{5,7},{6,4},{7,5},{8,10},{9,11},{10,... | collective-permute-start | bytes 884744 | tf_op jit(solution)/shard_map/ppermute | solution.py:1100
  373.1 25.5 %collective-permute-start.12 = (bf16[2,192,384]{2,1,0:T(8,128)(2,1)}, bf16[2,192,384]{2,1,0:T(8,128)(2,1)}, u32[]{:S(2)}, u32[]{:S(2)}) collective-permute-start(bf16[2,192,384]{2,1,0:T(8,128)(2,1)} %fusion.11.refs_6_), channel_id=1, source_target_pairs={{0,2},{1,3},{2,0},{3,1},{4,6},{5,7},{6,4},{7,5},{8,10},{9,11},{10,... | collective-permute-start | bytes 884744 | tf_op jit(solution)/shard_map/ppermute | solution.py:1100
  373.1 15.2 %collective-permute-start.13 = (f32[72,128]{1,0:T(8,128)S(1)}, f32[72,128]{1,0:T(8,128)S(1)}, u32[]{:S(2)}, u32[]{:S(2)}) collective-permute-start(f32[72,128]{1,0:T(8,128)S(1)} %copy-done.27), channel_id=1, source_target_pairs={{0,16},{8,24},{16,0},{24,8},{1,17},{9,25},{17,1},{25,9},{2,18},{10... | collective-permute-start | bytes 110600 | tf_op jit(solution)/shard_map/ppermute | solution.py:1100
  388.3 34.5 %collective-permute-start.15 = (bf16[768,768]{1,0:T(8,128)(2,1)}, bf16[768,768]{1,0:T(8,128)(2,1)}, u32[]{:S(2)}, u32[]{:S(2)}) collective-permute-start(bf16[768,768]{1,0:T(8,128)(2,1)} %get-tuple-element.233), channel_id=1, source_target_pairs={{0,8},{8,0},{16,24},{24,16},{1,9},{9,1},{17,25},{25,17},{2,10},{10... | collective-permute-start | bytes 3538952 | tf_op jit(solution)/shard_map/ppermute | solution.py:1100
  419.7 13.4 %collective-permute-start.14 = (bf16[768,768]{1,0:T(8,128)(2,1)}, bf16[768,768]{1,0:T(8,128)(2,1)S(1)}, u32[]{:S(2)}, u32[]{:S(2)}) collective-permute-start(bf16[768,768]{1,0:T(8,128)(2,1)} %get-tuple-element.161), channel_id=1, source_target_pairs={{0,8},{8,0},{16,24},{24,16},{1,9},{9,1},{17,25},{25,17},{2,10},{10... | collective-permute-start | bytes 3538952 | tf_op jit(solution)/shard_map/ppermute | solution.py:1100
  419.8 13.2 %collective-permute-start.28 = (bf16[96,768]{1,0:T(8,128)(2,1)S(1)}, bf16[96,768]{1,0:T(8,128)(2,1)S(1)}, u32[]{:S(2)}, u32[]{:S(2)}) collective-permute-start(bf16[96,768]{1,0:T(8,128)(2,1)S(1)} %copy-done.30), channel_id=1, source_target_pairs={{0,4},{1,5},{2,6},{3,7},{4,0},{5,1},{6,2},{7,3},{8,12},{9,13},{10,... | collective-permute-start | bytes 442376 | tf_op jit(solution)/shard_map/ppermute | solution.py:1100
  422.4 33.2 %collective-permute-start.29 = (bf16[192,384]{1,0:T(8,128)(2,1)S(1)}, bf16[192,384]{1,0:T(8,128)(2,1)}, u32[]{:S(2)}, u32[]{:S(2)}) collective-permute-start(bf16[192,384]{1,0:T(8,128)(2,1)S(1)} %copy-done.29), channel_id=1, source_target_pairs={{0,4},{1,5},{2,6},{3,7},{4,0},{5,1},{6,2},{7,3},{8,12},{9,13},{10,... | collective-permute-start | bytes 442376 | tf_op jit(solution)/shard_map/ppermute | solution.py:1100
  425.6 41.2 %collective-permute-start.19 = (bf16[2,2,96,768]{3,2,1,0:T(8,128)(2,1)}, bf16[2,2,96,768]{3,2,1,0:T(8,128)(2,1)}, u32[]{:S(2)}, u32[]{:S(2)}) collective-permute-start(bf16[2,2,96,768]{3,2,1,0:T(8,128)(2,1)} %get-tuple-element.239.refs_12_), channel_id=1, source_target_pairs={{0,1},{1,0},{2,3},{3,2},{4,5},{5,4},{6,7},{7,6},{8,9},{9,8},{10,11... | collective-permute-start | bytes 1769480 | tf_op jit(solution)/shard_map/ppermute | solution.py:1100
  434.5 18.6 %collective-permute-start.16 = (bf16[384,768]{1,0:T(8,128)(2,1)}, bf16[384,768]{1,0:T(8,128)(2,1)}, u32[]{:S(2)}, u32[]{:S(2)}) collective-permute-start(bf16[384,768]{1,0:T(8,128)(2,1)} %get-tuple-element.241.refs_11_), channel_id=1, source_target_pairs={{0,16},{8,24},{16,0},{24,8},{1,17},{9,25},{17,1},{25,9},{2,18},{10... | collective-permute-start | bytes 1769480 | tf_op jit(solution)/shard_map/ppermute | solution.py:1100
  455.6 9.1 %collective-permute-start.25 = (f32[72,128]{1,0:T(8,128)S(1)}, f32[72,128]{1,0:T(8,128)S(1)}, u32[]{:S(2)}, u32[]{:S(2)}) collective-permute-start(f32[72,128]{1,0:T(8,128)S(1)} %copy-done.28), channel_id=1, source_target_pairs={{0,4},{1,5},{2,6},{3,7},{4,0},{5,1},{6,2},{7,3},{8,12},{9,13},{10,... | collective-permute-start | bytes 110600 | tf_op jit(solution)/shard_map/ppermute | solution.py:1100
  456.6 43.2 %all-to-all-start.6 = ((bf16[8,384,96]{1,2,0:T(8,128)(2,1)}), bf16[8,384,96]{1,2,0:T(8,128)(2,1)S(1)}, u32[]{:S(2)}, u32[]{:S(2)}) async-start(bf16[8,384,96]{1,2,0:T(8,128)(2,1)} %bitcast.53), calls=%async_computation.6 | async-start | bytes 1179648 | tf_op jit(solution)/shard_map/all_to_all | solution.py:1108
  462.6 22.6 %collective-permute-start.30 = (bf16[96,768]{1,0:T(8,128)(2,1)S(1)}, bf16[96,768]{1,0:T(8,128)(2,1)S(1)}, u32[]{:S(2)}, u32[]{:S(2)}) collective-permute-start(bf16[96,768]{1,0:T(8,128)(2,1)S(1)} %fusion.17), channel_id=1, source_target_pairs={{0,16},{8,24},{16,0},{24,8},{1,17},{9,25},{17,1},{25,9},{2,18},{10... | collective-permute-start | bytes 442376 | tf_op jit(solution)/shard_map/ppermute | solution.py:1100
  463.2 15.0 %collective-permute-start.32 = (bf16[192,384]{1,0:T(8,128)(2,1)S(1)}, bf16[192,384]{1,0:T(8,128)(2,1)S(1)}, u32[]{:S(2)}, u32[]{:S(2)}) collective-permute-start(bf16[192,384]{1,0:T(8,128)(2,1)S(1)} %fusion.16), channel_id=1, source_target_pairs={{0,16},{8,24},{16,0},{24,8},{1,17},{9,25},{17,1},{25,9},{2,18},{10... | collective-permute-start | bytes 442376 | tf_op jit(solution)/shard_map/ppermute | solution.py:1100
  473.9 8.8 %collective-permute-start.20 = (bf16[2,96,768]{2,1,0:T(8,128)(2,1)S(1)}, bf16[2,96,768]{2,1,0:T(8,128)(2,1)S(1)}, u32[]{:S(2)}, u32[]{:S(2)}) collective-permute-start(bf16[2,96,768]{2,1,0:T(8,128)(2,1)S(1)} %fusion.14), channel_id=1, source_target_pairs={{0,2},{1,3},{2,0},{3,1},{4,6},{5,7},{6,4},{7,5},{8,10},{9,11},{10,... | collective-permute-start | bytes 884744 | tf_op jit(solution)/shard_map/ppermute | solution.py:1100
  478.3 17.5 %collective-permute-start.33 = (bf16[384,384]{1,0:T(8,128)(2,1)S(1)}, bf16[384,384]{1,0:T(8,128)(2,1)S(1)}, u32[]{:S(2)}, u32[]{:S(2)}) collective-permute-start(bf16[384,384]{1,0:T(8,128)(2,1)S(1)} %maximum_select_fusion.1), channel_id=1, source_target_pairs={{0,8},{8,0},{16,24},{24,16},{1,9},{9,1},{17,25},{25,17},{2,10},{10... | collective-permute-start | bytes 884744 | tf_op jit(solution)/shard_map/ppermute | solution.py:1100
  482.7 8.0 %collective-permute-start.21 = (bf16[96,768]{1,0:T(8,128)(2,1)S(1)}, bf16[96,768]{1,0:T(8,128)(2,1)S(1)}, u32[]{:S(2)}, u32[]{:S(2)}) collective-permute-start(bf16[96,768]{1,0:T(8,128)(2,1)S(1)} %fusion.21), channel_id=1, source_target_pairs={{0,4},{1,5},{2,6},{3,7},{4,0},{5,1},{6,2},{7,3},{8,12},{9,13},{10,... | collective-permute-start | bytes 442376 | tf_op jit(solution)/shard_map/ppermute | solution.py:1100
  (50 other events, 252.3 us)

commit v4 on v3

--- a/solution.py
+++ b/solution.py
@@ -117,52 +117,54 @@
     return ((pos >= lm * seg) & (pos < (lm + 1) * seg)).astype(f32)
 
 
-def qkv_kernel(n_long, length, x_l, x_s, wq, wk, wv, q_l, k_l, v_l, q_s, k_s, v_s, lq, lk, w_t):
+def project_kernel(n_long, count, length, x_l, x_s, *refs):
+    ws, out_l, out_s = refs[:count], refs[count : 2 * count], refs[2 * count : 3 * count]
+    marks, w_t = refs[3 * count :]
     i = pl.program_id(0)
 
     @pl.when(i == 0)
     def _():
-        for j, w in enumerate((wq, wk, wv)):
+        for j, w in enumerate(ws):
             w_t[j * D : (j + 1) * D, :] = w[...].T
 
     x = jnp.where(i < n_long, x_l[...], x_s[...])
     made = dot(w_t[...], x, 1, 1).astype(bf)
-    made = [made[j * D : (j + 1) * D] for j in range(3)]
+    made = [made[j * D : (j + 1) * D] for j in range(count)]
 
     @pl.when(i < n_long)
     def _():
-        for ref, v in zip((q_l, k_l, v_l), made):
+        for ref, v in zip(out_l, made):
             ref[...] = v
 
     @pl.when(i >= n_long)
     def _():
-        for ref, v in zip((q_s, k_s, v_s), made):
+        for ref, v in zip(out_s, made):
             ref[...] = v
         member = short_member(length[0], made[0].shape[1]).astype(bf)
-        count = (length[0] // LM).astype(f32)
-        lq[...] = (dot(member, made[0], 1, 1) / count).astype(bf)
-        lk[...] = (dot(member, made[1], 1, 1) / count).astype(bf)
-
-
-def qkv(length, x_l, x_s, wq, wk, wv):
+        marks[...] = (dot(member, made[0], 1, 1) / (length[0] // LM).astype(f32)).astype(bf)
+
+
+def project(length, x_l, x_s, ws, deps=()):
     tile = x_s.shape[0]
+    n = len(ws)
     nl = x_l.shape[0] // tile
     long_at = lambda i: jnp.minimum(i, nl - 1)
     row = lambda f: pl.BlockSpec((tile, D), lambda i: (f(i), 0))
     col = lambda f: pl.BlockSpec((D, tile), lambda i: (0, f(i)))
     first = lambda i: 0
     tl, ts = x_l.shape[0], x_s.shape[0]
-    return pl.pallas_call(
-        functools.partial(qkv_kernel, nl),
+    out = pl.pallas_call(
+        after(functools.partial(project_kernel, nl, n), 3 + n, deps),
         grid=(nl + 1,),
-        in_specs=[SMEM_SPEC, row(long_at), row(first)] + [const_spec((D, D))] * 3,
-        out_specs=[col(long_at)] * 3 + [col(first)] * 3 + [pl.BlockSpec((LM, D), lambda i: (0, 0))] * 2,
-        out_shape=[sds((D, tl), bf)] * 3 + [sds((D, ts), bf)] * 3 + [sds((LM, D), bf)] * 2,
-        scratch_shapes=[pltpu.VMEM((3 * D, D), bf)],
-        compiler_params=params(),
-        cost_estimate=cost(6 * (tl + ts) * D * D, 8 * (tl + ts) * D),
-        name="qkv",
-    )(length, x_l, x_s, wq, wk, wv)
+        in_specs=[SMEM_SPEC, row(long_at), row(first)] + [const_spec((D, D))] * n + [ANY_SPEC] * len(deps),
+        out_specs=[col(long_at)] * n + [col(first)] * n + [pl.BlockSpec((LM, D), lambda i: (0, 0))],
+        out_shape=[sds((D, tl), bf)] * n + [sds((D, ts), bf)] * n + [sds((LM, D), bf)],
+        scratch_shapes=[pltpu.VMEM((n * D, D), bf)],
+        compiler_params=params(),
+        cost_estimate=cost(2 * n * (tl + ts) * D * D, 4 * n * (tl + ts) * D),
+        name="project",
+    )(length, x_l, x_s, *ws, *deps)
+    return out[:n], out[n : 2 * n], out[2 * n]
 
 
 def mark_scores(lq_g, k_g, limit):
@@ -537,17 +539,8 @@
     return [copy]
 
 
-def plain_job(acc, dst):
-    def copies(src, sem):
-        copy = pltpu.make_async_copy(src, dst, sem)
-        copy.start()
-        return [copy]
-
-    return (lambda: acc[...], copies)
-
-
 def dense_kernel(n_long, tile, chunk, core, x_l, x_s, o_l, o_s, c_l, c_s, w_out, w_up, w_down, vecs, bu,
-                 out_l, out_s, dr_l, dr_s, do_l, do_s, up_keep, up_send, dn_keep, dn_send, gout, small, small_up,
+                 out_l, out_s, dr_l, dr_s, do_l, do_s, up_keep, up_send, dn_keep, dn_send, vo_keep, vo_send, small, small_up,
                  acc_up, acc_dn, acc_out, act, dact, accs, accu, x_b, o_b, c_b, out_b, dr_b, do_b,
                  in_sem, out_sem, end_sem):
     i = pl.program_id(0)
@@ -696,7 +689,12 @@
                 ),
             )
         for r in range(0, D, 128):
-            put(acc_out[r : r + 128, :], lambda part, sem, r=r: started(part.at[:, :D], gout.at[r : r + 128, :], sem))
+            put(
+                acc_out[r : r + 128, :],
+                lambda part, sem, r=r: to_side(
+                    part.at[:, :D], vo_keep.at[r : r + 128, :], vo_send.at[r : r + 128, :], core[0] == 1, sem
+                ),
+            )
         small[...] = jnp.sum(accs[...], axis=1)
         small_up[...] = jnp.sum(accu[...], axis=0, keepdims=True)
         for group in pend[-slots:]:
@@ -706,12 +704,6 @@
             cp.wait()
 
 
-def started(src, dst, sem):
-    copy = pltpu.make_async_copy(src, dst, sem)
-    copy.start()
-    return [copy]
-
-
 def dense(core, x_l, x_s, o_l, o_s, c_l, c_s, w_out, w_up, w_down, vecs, bu, tile=512, chunk=1536):
     nl, ns = x_l.shape[0] // tile, x_s.shape[0] // tile
     tl, ts = x_l.shape[0], x_s.shape[0]
@@ -722,10 +714,10 @@
         + [ANY_SPEC] * 6
         + [const_spec((D, D)), const_spec((D, FF)), const_spec((FF, D))]
         + [const_spec((8, D)), const_spec((1, FF))],
-        out_specs=[ANY_SPEC] * 11 + [const_spec((6, D)), const_spec((1, FF))],
+        out_specs=[ANY_SPEC] * 12 + [const_spec((6, D)), const_spec((1, FF))],
         out_shape=[sds((tl, D), bf), sds((ts, D), bf), sds((tl, D), f32), sds((ts, D), f32)]
         + [sds((D, tl), bf), sds((D, ts), bf), sds((D, FF // 2), bf), sds((D, FF // 2), bf)]
-        + [sds((D // 2, FF), bf), sds((D // 2, FF), bf), sds((D, D), bf)]
+        + [sds((D // 2, FF), bf), sds((D // 2, FF), bf), sds((D, D), bf), sds((D, D), bf)]
         + [sds((6, D), f32), sds((1, FF), f32)],
         scratch_shapes=[
             pltpu.VMEM((D, FF), f32),
@@ -907,7 +899,7 @@
     )(lq, w, dbv, k, v, *deps)
 
 
-def back_v_kernel(units, dbv, probs, dconv, x, gv_in, dv_out, gv_out, acc):
+def back_v_kernel(units, core, dbv, probs, dconv, x, gv_in, keep_in, send_in, dv_out, keep, send, acc, stage, sem):
     i = pl.program_id(0)
 
     @pl.when(i == 0)
@@ -921,25 +913,29 @@
 
     @pl.when(i == pl.num_programs(0) - 1)
     def _():
-        gv_out[...] = acc[...].T.astype(bf)
-
-
-def back_v(dbv, probs, dconv, x, gv, items, units, deps=()):
+        stage[...] = acc[...].T.astype(bf)
+        for cp in to_side(stage, keep, send, core[0] == 0, sem.at[0]):
+            cp.wait()
+
+
+def back_v(core, dbv, probs, dconv, x, gv, keep, send, items, units, deps=()):
     rows = probs.shape[1] // items
     _, tok = item_specs(rows)
     square = const_spec((D, D))
     return pl.pallas_call(
-        after(functools.partial(back_v_kernel, units), 5, deps),
+        after(functools.partial(back_v_kernel, units), 8, deps),
         grid=(items,),
-        in_specs=[unit_spec(units, LM + 16, D // units), tok, tok, pl.BlockSpec((rows, D), lambda i: (i, 0)), square]
+        in_specs=[SMEM_SPEC, unit_spec(units, LM + 16, D // units), tok, tok]
+        + [pl.BlockSpec((rows, D), lambda i: (i, 0)), square, ANY_SPEC, ANY_SPEC]
         + [ANY_SPEC] * len(deps),
-        out_specs=[tok, square],
-        out_shape=[sds(probs.shape, bf), sds((D, D), bf)],
-        scratch_shapes=[pltpu.VMEM((D, D), f32)],
+        out_specs=[tok, ANY_SPEC, ANY_SPEC],
+        out_shape=[sds(probs.shape, bf), sds((D, D), bf), sds((D, D), bf)],
+        input_output_aliases={6: 1, 7: 2},
+        scratch_shapes=[pltpu.VMEM((D, D), f32), pltpu.VMEM((D, D), bf), pltpu.SemaphoreType.DMA((1,))],
         compiler_params=params(),
         cost_estimate=cost(6 * items * rows * D * GROUP, 12 * items * rows * D),
         name="back_v",
-    )(dbv, probs, dconv, x, gv, *deps)
+    )(core, dbv, probs, dconv, x, gv, keep, send, *deps)
 
 
 def short_back_kernel(length, q, k, v, lq, lk, z, w, bv, up, dconv, x, dsf_out, dsb_out, dv_out, dlq_out, dlk_out, dw_out, gv_out):
@@ -1307,11 +1303,12 @@
     tap_rows = jnp.stack([conv_taps.T, conv_taps[::-1].T], axis=1)
     tap_rows = jnp.pad(tap_rows, ((0, 0), (0, 6), (0, 128 - TAPS)))
 
-    q_l, k_l, v_l, q_s, k_s, v_s, lq_s, lk_s = qkv(length, x_l, x_s, w_query, w_key, w_value)
+    (k_l, v_l), (k_s, v_s), lk_s = project(length, x_l, x_s, (w_key, w_value))
     c_l, c_s = conv(length, v_l, v_s, v_rim, tap_rows, items)
     lq_l, lk_l = marks_of(w_query), marks_of(w_key)
 
     msg_l = stats(lq_l, k_l, v_l, items, units)
+    (q_l,), (q_s,), lq_s = project(length, x_l, x_s, (w_query,), (msg_l,))
     got_l = exchange(pad_units(msg_l, n_seq))
     z_own, z_s = inverse(at, lq_l, lk_l, lq_s, lk_s, width)
     w_own, bv_own = combine(got_l, z_own)
@@ -1320,7 +1317,7 @@
     o_l = mix(lk_l, w_l, q_l, c_l, items, units)
 
     vecs = jnp.pad(jnp.stack([ln1_gain, ln1_bias, down_bias, ln2_gain, ln2_bias]), ((0, 3), (0, 0)))
-    out_l, out_s, dr_l, dr_s, do_l, do_s, up_keep, up_send, dn_keep, dn_send, g_out, small, small_up = dense(
+    out_l, out_s, dr_l, dr_s, do_l, do_s, up_keep, up_send, dn_keep, dn_send, vo_keep, vo_send, small, small_up = dense(
         core, x_l, x_s, o_l, o_s, cot_long.reshape(items * rows, D), cot_short.reshape(short_rows, D), w_out, w_up,
         w_down, vecs, up_bias.reshape(1, -1),
     )
@@ -1356,7 +1353,7 @@
 
     dl = jnp.stack([with_own(dlq_part, dlq_own), with_own(dlk_part, dlk_own)]).astype(bf)
     dl = dl.reshape(2 * items, n_seq, own_marks, D).transpose(1, 0, 2, 3)
-    dv_l, g_v = back_v(dbv_l, probs_l, dc_l, x_l, gv_s, items, units, (dl,))
+    dv_l, vo_keep, vo_send = back_v(core, dbv_l, probs_l, dc_l, x_l, gv_s, vo_keep, vo_send, items, units, (dl,))
     dl = jnp.sum(exchange(dl).astype(f32), axis=0) * (1.0 / seg)
     dl = jnp.pad(dl.reshape(2, items, own_marks, D), ((0, 0), (0, 0), (0, 16 - own_marks), (0, 0)))
     dl = dl.reshape(2, items * 16, D)
@@ -1367,12 +1364,12 @@
         (x_l, lq_l, lk_l, dsf_l, dsb_l, dl[0], dl[1]),
         (x_s, lq_s, lk_s, dsf_s, dsb_s, dlq_s, dlk_s, dlq_own_s, dlk_own_s),
         items,
-        (up.step(), down.step(), g_v, packed.step(dlq_part)),
+        (packed.step(dlq_part), dv_l),
     )
     query_key = Reduction(qk_keep, qk_send, 1)
-    is_first = core[0] == 0
-    vo_keep = hold(jnp.where(is_first, g_v, g_out), dq_l)
-    value_out = Halving(vo_keep, jnp.where(is_first, g_out, g_v), 0, ("y", "z0", "z1", "x"))
+    value_out = Halving(hold(vo_keep, dq_l), vo_send, 0, ("y", "z0", "z1", "x"))
+    up.step()
+    down.step()
     up.theirs, down.theirs = tied((up.theirs, down.theirs), dq_l)
     grad_l, grad_s = input_grad(
         (dr_l, dq_l, dk_l, dv_l),

time: 514 us -> 497 us (0.967)
  local copies, waits for them, and re-layouts: 40.9 us -> 33.7 us
  waiting for transfers between devices: 47.5 us -> 41.6 us
    ppermute x30, waiting for transfers between devices: 37.1 us -> 27.9 us  [swap(): return lax.ppermute(values, axis, [(i, i ^ bit) for i in range(count)])]
    pallas_call x2 -> x3, Pallas kernels: 28.2 us -> 32.8 us  [the longest x2 21.7 us: project(): pl.pallas_call(after(functools.partial(project_kernel, nl, n), 3 + n, dep...]
    unnamed x89 -> x76, local copies, waits for them, and re-layouts: 11.8 us -> 9.72 us
  transfers between devices with their start and end apart: 41 -> 41, of which waited for: 11 -> 12; matrix products, arithmetic and copies ran while one was open for 14% -> 12% of each run, Pallas kernels for 31% -> 33%
where the time goes in v4:
time: 497 us; the launch traced here: 491 us
  Pallas kernels  303 us (61%)
  starting transfers between devices  72.1 us (15%)
  waiting for transfers between devices  41.6 us (8%)
  local copies, waits for them, and re-layouts  33.7 us (7%)
  other arithmetic  32.8 us (7%)
    pallas_call x1, Pallas kernels, dense(): pl.pallas_call(functools.partial(dense_kernel, nl, tile, chunk), grid=(nl...  125 us
    all_to_all x7, starting transfers between devices, exchange(): return lax.all_to_all(values, 'seq', 0, 0, tiled=True)  32.5 us
    ppermute x30, starting transfers between devices, swap(): return lax.ppermute(values, axis, [(i, i ^ bit) for i in range(count)])  28.8 us
    pallas_call x1, Pallas kernels, back_inverse(): pl.pallas_call(after(back_inverse_kernel, 9, deps), grid_spec=pltpu.Prefe...  28.3 us
    ppermute x30, waiting for transfers between devices, swap(): return lax.ppermute(values, axis, [(i, i ^ bit) for i in range(count)])  27.9 us
    pallas_call x2, Pallas kernels, project(): pl.pallas_call(after(functools.partial(project_kernel, nl, n), 3 + n, dep...  21.7 us
    pallas_call x1, Pallas kernels, score_grads(): pl.pallas_call(after(functools.partial(score_grads_kernel, items), 18, de...  17.8 us
    pallas_call x1, Pallas kernels, input_grad(): pl.pallas_call(after(functools.partial(input_grad_kernel, nl), 11, deps),...  17.1 us
  transfers between devices with their start and end apart: 41, of which 12 were waited for; matrix products, arithmetic and copies ran while one was open for 12% of the time, Pallas kernels for 33%

profile of v4, /device:TPU:0, one launch (start us, length us, event | category | flops | bytes accessed | tf_op | source)
XLA Modules:
  0.0 490.6 jit_solution(8539966695821006492)
XLA Ops:
  5.2 3.0 collective-permute-start.1
  11.8 3.5 all-to-all-start
  18.7 12.9 %project.2 = (bf16[768,2048]{1,0:T(8,128)(2,1)}, bf16[768,2048]{1,0:T(8,128)(2,1)}, bf16[768,512]{1,0:T(8,128)(2,1)}, bf16[768,512]{1,0:T(8,128)(2,1)}, bf16[64,768]{1,0:T(8,128)(2,1)}) custom-call(s32[1]{0:T(128)} %bitcast.194.refs_0_, bf16[2048,768]{1,0:T(8,128)(2,1)} %bitcast.202, bf16[512,768]{1,0:T(8,128)(2,1)} %bitcast.233, bf16[768,768]{1,0:T(8,128)(2,1)} %refs_9_.1, ...), custom_call_target="tpu_custom_call" | custom-call | flops 6039797760 | bytes 15728640 | tf_op jit(solution)/shard_map/project/pallas_call | solution.py:156
  41.1 7.3 %stats.1.refs_4_ = f32[8,72,384]{2,1,0:T(8,128)} custom-call(bf16[256,768]{1,0:T(8,128)(2,1)} %fusion.1.lq.lq_l.refs_0_.refs_1_.refs_3_, bf16[768,2048]{1,0:T(8,128)(2,1)} %get-tuple-element.98.k.refs_3_, bf16[768,2048]{1,0:T(8,128)(2,1)} %get-tuple-element.99.v.v_l.refs_1_.refs_4_), custom_call_target="tpu_custom_call" | custom-call | flops 1610612736 | bytes 6291456 | tf_op jit(solution)/shard_map/stats/pallas_call | solution.py:207
  48.4 3.9 all-to-all-start.1
  52.3 8.7 %project.3 = (bf16[768,2048]{1,0:T(8,128)(2,1)}, bf16[768,512]{1,0:T(8,128)(2,1)}, bf16[64,768]{1,0:T(8,128)(2,1)}) custom-call(s32[1]{0:T(128)} %bitcast.195.refs_0_, bf16[2048,768]{1,0:T(8,128)(2,1)} %bitcast.203, bf16[512,768]{1,0:T(8,128)(2,1)} %bitcast.234, bf16[768,768]{1,0:T(8,128)(2,1)} %refs_8_.1, f32[8,72,384]{2,1,0:T(8,128)} %stats.1.refs_4_), custom_call_target="tpu_custom_call" | custom-call | flops 3019898880 | bytes 7864320 | tf_op jit(solution)/shard_map/project/pallas_call | solution.py:156
  61.0 9.1 %inverse.1 = (f32[64,384]{1,0:T(8,128)}, f32[64,768]{1,0:T(8,128)}) custom-call(s32[2]{0:T(128)} %pad_add_fusion.at.refs_0_, bf16[256,768]{1,0:T(8,128)(2,1)} %fusion.1.lq.lq_l.refs_0_.refs_1_.refs_3_, bf16[256,768]{1,0:T(8,128)(2,1)} %fusion.lk_l.lk.refs_2_.refs_4_, bf16[64,768]{1,0:T(8,128)(2,1)} %get-tuple-element.100.lq_s.lq.refs_4_.refs_3_.refs_10_, ...), custom_call_target="tpu_custom_call" | custom-call | flops 13589544960 | bytes 1000000 | tf_op jit(solution)/shard_map/inverse/pallas_call | solution.py:273
  70.1 4.5 all-to-all-done.1.msg
  75.6 3.1 combine.1
  78.7 4.4 all-to-all-start.2
  85.4 8.2 %conv.1 = (f32[768,2048]{1,0:T(8,128)}, f32[768,512]{1,0:T(8,128)}) custom-call(s32[1]{0:T(128)} %bitcast.196.length, bf16[768,2048]{1,0:T(8,128)(2,1)} %get-tuple-element.99.v.v_l.refs_1_.refs_4_, bf16[768,512]{1,0:T(8,128)(2,1)} %get-tuple-element.105.v_s.v.refs_2_.refs_3_, bf16[768,128]{1,0:T(8,128)(2,1)} %fusion.4.rim.refs_3_, ...), custom_call_target="tpu_custom_call" | custom-call | flops 3221225472 | bytes 12582912 | tf_op jit(solution)/shard_map/conv/pallas_call | solution.py:456
  93.6 6.5 %short_attend.1 = (bf16[768,512]{1,0:T(8,128)(2,1)}, bf16[64,768]{1,0:T(8,128)(2,1)}, f32[64,768]{1,0:T(8,128)}) custom-call(s32[1]{0:T(128)} %bitcast.197.length, bf16[768,512]{1,0:T(8,128)(2,1)} %get-tuple-element.107.q.refs_1_, bf16[768,512]{1,0:T(8,128)(2,1)} %get-tuple-element.108.k.refs_2_, bf16[768,512]{1,0:T(8,128)(2,1)} %get-tuple-element.105.v_s.v.refs_2_.refs_3_, ...), custom_call_target="tpu_custom_call" | custom-call | flops 805306368 | bytes 3932160 | tf_op jit(solution)/shard_map/short_attend/pallas_call | solution.py:357
  100.9 8.9 %mix.1.o_l = bf16[768,2048]{1,0:T(8,128)(2,1)} custom-call(bf16[256,768]{1,0:T(8,128)(2,1)} %fusion.lk_l.lk.refs_2_.refs_4_, bf16[8,80,384]{2,1,0:T(8,128)(2,1)} %copy-done.17, bf16[768,2048]{1,0:T(8,128)(2,1)} %get-tuple-element.104.q, f32[768,2048]{1,0:T(8,128)} %get-tuple-element.106.conv), custom_call_target="tpu_custom_call" | custom-call | flops 1610612736 | bytes 12582912 | tf_op jit(solution)/shard_map/mix/pallas_call | solution.py:375
  109.8 124.7 %dense.1 = (bf16[2048,768]{1,0:T(8,128)(2,1)}, bf16[512,768]{1,0:T(8,128)(2,1)}, f32[2048,768]{1,0:T(8,128)}, f32[512,768]{1,0:T(8,128)}, bf16[768,2048]{1,0:T(8...) custom-call(s32[1]{0:T(128)} %bitcast.core.refs_0_.refs_1_, ...), custom_call_target="tpu_custom_call" | custom-call | flops 81537269760 | bytes 60000000 | tf_op jit(solution)/shard_map/dense/pallas_call | solution.py:710
  235.8 8.7 %back_f.1 = (f32[8,64,384]{2,1,0:T(8,128)}, f32[256,768]{1,0:T(8,128)}, bf16[768,2048]{1,0:T(8,128)(2,1)}, bf16[4,32,768]{2,1,0:T(8,128)(2,1)}) custom-call(bf16[256,768]{1,0:T(8,128)(2,1)} %fusion.lk_l.lk.refs_2_.refs_4_, bf16[8,80,384]{2,1,0:T(8,128)(2,1)} %copy-done.17, bf16[768,2048]{1,0:T(8,128)(2,1)} %get-tuple-element.104.q, ...), custom_call_target="tpu_custom_call" | custom-call | flops 3221225472 | bytes 9437184 | tf_op jit(solution)/shard_map/back_f/pallas_call | solution.py:774
  244.4 6.1 %all-to-all-start.3 = ((f32[8,64,384]{2,1,0:T(8,128)}), f32[8,64,384]{2,1,0:T(8,128)S(1)}, u32[]{:S(2)}, u32[]{:S(2)}) async-start(f32[8,64,384]{2,1,0:T(8,128)} %get-tuple-element.117), calls=%async_computation.3 | async-start | bytes 1572864 | tf_op jit(solution)/shard_map/all_to_all | solution.py:1104
  250.6 4.8 collective-permute-start.3
  271.6 10.7 %conv_back.1 = (f32[768,2048]{1,0:T(8,128)}, f32[768,512]{1,0:T(8,128)}, f32[12,8,128]{2,1,0:T(8,128)}) custom-call(s32[1]{0:T(128)} %bitcast.198.refs_0_, bf16[768,2048]{1,0:T(8,128)(2,1)} %get-tuple-element.99.v.v_l.refs_1_.refs_4_, bf16[768,512]{1,0:T(8,128)(2,1)} %get-tuple-element.105.v_s.v.refs_2_.refs_3_, bf16[768,128]{1,0:T(8,128)(2,1)} %fusion.4.rim.refs_3_, ...), custom_call_target="tpu_custom_call" | custom-call | flops 4831838208 | bytes 18874368 | tf_op jit(solution)/shard_map/conv_back/pallas_call | solution.py:487
  282.3 9.2 %short_back.1 = (bf16[768,512]{1,0:T(8,128)(2,1)}, bf16[768,512]{1,0:T(8,128)(2,1)}, bf16[768,512]{1,0:T(8,128)(2,1)}, f32[64,768]{1,0:T(8,128)}, f32[64,768]{1,...) custom-call(s32[1]{0:T(128)} %bitcast.199.refs_0_, bf16[768,512]{1,0:T(8,128)(2,1)} %get-tuple-element.107.q.refs_1_, ...), custom_call_target="tpu_custom_call" | custom-call | flops 2415919104 | bytes 7864320 | tf_op jit(solution)/shard_map/short_back/pallas_call | solution.py:961
  296.4 5.5 %all-to-all-start.4 = ((bf16[8,80,384]{2,1,0:T(8,128)(2,1)}), bf16[8,80,384]{2,1,0:T(8,128)(2,1)S(1)}, u32[]{:S(2)}, u32[]{:S(2)}) async-start(bf16[8,80,384]{2,1,0:T(8,128)(2,1)} %get-tuple-element.133), calls=%async_computation.4 | async-start | bytes 983040 | tf_op jit(solution)/shard_map/all_to_all | solution.py:1104
  311.5 28.3 %back_inverse.1 = (f32[64,384]{1,0:T(8,128)}, f32[64,384]{1,0:T(8,128)}, f32[64,768]{1,0:T(8,128)}, f32[64,768]{1,0:T(8,128)}) custom-call(s32[2]{0:T(128)} %pad_add_fusion.at.refs_0_, bf16[256,768]{1,0:T(8,128)(2,1)} %fusion.1.lq.lq_l.refs_0_.refs_1_.refs_3_, bf16[256,768]{1,0:T(8,128)(2,1)} %fusion.lk_l.lk.refs_2_.refs_4_, ...), custom_call_target="tpu_custom_call" | custom-call | flops 40768634880 | bytes 2000000 | tf_op jit(solution)/shard_map/back_inverse/pallas_call | solution.py:854
  347.7 8.1 %back_b.1 = (bf16[768,2048]{1,0:T(8,128)(2,1)}, bf16[768,2048]{1,0:T(8,128)(2,1)}, f32[256,768]{1,0:T(8,128)}) custom-call(bf16[256,768]{1,0:T(8,128)(2,1)} %fusion.1.lq.lq_l.refs_0_.refs_1_.refs_3_, bf16[8,80,384]{2,1,0:T(8,128)(2,1)} %copy-done.17, bf16[8,80,384]{2,1,0:T(8,128)(2,1)} %copy-done.18, bf16[768,2048]{1,0:T(8,128)(2,1)} %get-tuple-element.98.k.refs_3_, ...), custom_call_target="tpu_custom_call" | custom-call | flops 3221225472 | bytes 15728640 | tf_op jit(solution)/shard_map/back_b/pallas_call | solution.py:890
  358.4 4.7 all-to-all-start.5
  365.7 11.1 %back_v.1 = (bf16[768,2048]{1,0:T(8,128)(2,1)}, bf16[768,768]{1,0:T(8,128)(2,1)}, bf16[768,768]{1,0:T(8,128)(2,1)}) custom-call(s32[1]{0:T(128)} %bitcast.core.refs_0_.refs_1_, bf16[8,80,384]{2,1,0:T(8,128)(2,1)} %copy-done.18, bf16[768,2048]{1,0:T(8,128)(2,1)} %get-tuple-element.152.refs_2_, ...), custom_call_target="tpu_custom_call", output_to_operand_aliasing={{1}: (6, {}), {2}: (7, {})} | custom-call | flops 2415919104 | bytes 18874368 | tf_op jit(solution)/shard_map/back_v/pallas_call | solution.py:925
  377.5 5.4 %all-to-all-done.5 = bf16[8,8,8,768]{3,2,1,0:T(8,128)(2,1)S(1)} async-done(((bf16[8,8,8,768]{3,2,1,0:T(8,128)(2,1)}), bf16[8,8,8,768]{3,2,1,0:T(8,128)(2,1)S(1)}, u32[]{:S(2)}, u32[]{:S(2)}) %all-to-all-start.5) | async-done | bytes 786464 | tf_op jit(solution)/shard_map/all_to_all | solution.py:1104
  383.8 17.8 %score_grads.1 = (bf16[768,2048]{1,0:T(8,128)(2,1)}, bf16[768,2048]{1,0:T(8,128)(2,1)}, bf16[768,512]{1,0:T(8,128)(2,1)}, bf16[768,512]{1,0:T(8,128)(2,1)}, bf16...) custom-call(s32[1]{0:T(128)} %bitcast.200.refs_0_, s32[1]{0:T(128)} %bitcast.core.refs_0_.refs_1_, ...), custom_call_target="tpu_custom_call" | custom-call | flops 9059696640 | bytes 39321600 | tf_op jit(solution)/shard_map/score_grads/pallas_call | solution.py:1029
  411.4 6.3 %collective-permute-done.28 = bf16[96,768]{1,0:T(8,128)(2,1)S(1)} collective-permute-done((bf16[96,768]{1,0:T(8,128)(2,1)S(1)}, bf16[96,768]{1,0:T(8,128)(2,1)S(1)}, u32[]{:S(2)}, u32[]{:S(2)}) %collective-permute-start.28) | collective-permute-done | bytes 147488 | tf_op jit(solution)/shard_map/ppermute | solution.py:1096
  420.3 17.1 %input_grad.1 = (bf16[2048,768]{1,0:T(8,128)(2,1)}, bf16[512,768]{1,0:T(8,128)(2,1)}) custom-call(f32[2048,768]{1,0:T(8,128)} %get-tuple-element.114.refs_0_, bf16[768,2048]{1,0:T(8,128)(2,1)} %get-tuple-element.158.refs_1_, bf16[768,2048]{1,0:T(8,128)(2,1)} %get-tuple-element.159.refs_2_, bf16[768,2048]{1,0:T(8,128)(2,1)} %get-tuple-element.157.refs_19_.refs_3_, ...), custom_call_target="tpu_custom_call" | custom-call | flops 9059696640 | bytes 23592960 | tf_op jit(solution)/shard_map/input_grad/pallas_call | solution.py:1080
  440.8 4.4 all-to-all-start.6
  450.7 4.7 collective-permute-done.24
  461.6 4.7 collective-permute-done.18
  468.7 5.5 %collective-permute-done.19 = bf16[96,768]{1,0:T(8,128)(2,1)S(1)} collective-permute-done((bf16[96,768]{1,0:T(8,128)(2,1)S(1)}, bf16[96,768]{1,0:T(8,128)(2,1)S(1)}, u32[]{:S(2)}, u32[]{:S(2)}) %collective-permute-start.19) | collective-permute-done | bytes 147488 | tf_op jit(solution)/shard_map/ppermute | solution.py:1096
  (240 shorter events, 116.3 us)
Async XLA Ops:
  2.3 29.9 %collective-permute-start = (bf16[4,16,768]{2,1,0:T(8,128)(2,1)S(1)}, bf16[4,16,768]{2,1,0:T(8,128)(2,1)S(1)}, u32[]{:S(2)}, u32[]{:S(2)}) collective-permute-start(bf16[4,16,768]{2,1,0:T(8,128)(2,1)S(1)} %get-tuple-element.234), channel_id=1, source_target_pairs={{0,1},{1,2},{2,3},{3,4},{4,5},{5,6},{6,7},{7,0},{8,9},{9,10},{10,1... | collective-permute-start | bytes 294920 | tf_op jit(solution)/shard_map/ppermute | solution.py:1250
  5.2 77.9 %collective-permute-start.1 = (bf16[4,16,768]{2,1,0:T(8,128)(2,1)}, bf16[4,16,768]{2,1,0:T(8,128)(2,1)}, u32[]{:S(2)}, u32[]{:S(2)}) collective-permute-start(bf16[4,16,768]{2,1,0:T(8,128)(2,1)} %get-tuple-element.235), channel_id=1, source_target_pairs={{1,0},{2,1},{3,2},{4,3},{5,4},{6,5},{7,6},{0,7},{9,8},{10,9},{11,1... | collective-permute-start | bytes 294920 | tf_op jit(solution)/shard_map/ppermute | solution.py:1249
  11.8 23.7 %all-to-all-start = ((f32[8,32,768]{2,1,0:T(8,128)}), f32[8,32,768]{2,1,0:T(8,128)S(1)}, u32[]{:S(2)}, u32[]{:S(2)}) async-start(f32[8,32,768]{2,1,0:T(8,128)} %broadcast_in_dim.28), calls=%async_computation | async-start | bytes 1572864 | tf_op jit(solution)/shard_map/all_to_all | solution.py:1104
  48.4 26.3 %all-to-all-start.1 = ((f32[8,72,384]{2,1,0:T(8,128)}), f32[8,72,384]{2,1,0:T(8,128)S(1)}, u32[]{:S(2)}, u32[]{:S(2)}) async-start(f32[8,72,384]{2,1,0:T(8,128)} %stats.1.refs_4_), calls=%async_computation.1 | async-start | bytes 1769472 | tf_op jit(solution)/shard_map/all_to_all | solution.py:1104
  78.7 21.5 %all-to-all-start.2 = ((bf16[8,80,384]{2,1,0:T(8,128)(2,1)}), bf16[8,80,384]{2,1,0:T(8,128)(2,1)S(1)}, u32[]{:S(2)}, u32[]{:S(2)}) async-start(bf16[8,80,384]{2,1,0:T(8,128)(2,1)} %get-tuple-element.103), calls=%async_computation.2 | async-start | bytes 983040 | tf_op jit(solution)/shard_map/all_to_all | solution.py:1104
  234.5 20.9 %collective-permute-start.4 = (bf16[768,1536]{1,0:T(8,128)(2,1)}, bf16[768,1536]{1,0:T(8,128)(2,1)}, u32[]{:S(2)}, u32[]{:S(2)}) collective-permute-start(bf16[768,1536]{1,0:T(8,128)(2,1)} %get-tuple-element.126), channel_id=1, source_target_pairs={{0,8},{8,0},{16,24},{24,16},{1,9},{9,1},{17,25},{25,17},{2,10},{10... | collective-permute-start | bytes 7077896 | tf_op jit(solution)/shard_map/ppermute | solution.py:1096
  234.5 30.2 %collective-permute-start.5 = (bf16[384,3072]{1,0:T(8,128)(2,1)}, bf16[384,3072]{1,0:T(8,128)(2,1)}, u32[]{:S(2)}, u32[]{:S(2)}) collective-permute-start(bf16[384,3072]{1,0:T(8,128)(2,1)} %get-tuple-element.128), channel_id=1, source_target_pairs={{0,8},{8,0},{16,24},{24,16},{1,9},{9,1},{17,25},{25,17},{2,10},{10... | collective-permute-start | bytes 7077896 | tf_op jit(solution)/shard_map/ppermute | solution.py:1096
  244.4 47.1 %all-to-all-start.3 = ((f32[8,64,384]{2,1,0:T(8,128)}), f32[8,64,384]{2,1,0:T(8,128)S(1)}, u32[]{:S(2)}, u32[]{:S(2)}) async-start(f32[8,64,384]{2,1,0:T(8,128)} %get-tuple-element.117), calls=%async_computation.3 | async-start | bytes 1572864 | tf_op jit(solution)/shard_map/all_to_all | solution.py:1104
  250.6 18.9 %collective-permute-start.3 = (bf16[4,16,768]{2,1,0:T(8,128)(2,1)S(1)}, bf16[4,16,768]{2,1,0:T(8,128)(2,1)S(1)}, u32[]{:S(2)}, u32[]{:S(2)}) collective-permute-start(bf16[4,16,768]{2,1,0:T(8,128)(2,1)S(1)} %get-tuple-element.252), channel_id=1, source_target_pairs={{1,0},{2,1},{3,2},{4,3},{5,4},{6,5},{7,6},{0,7},{9,8},{10,9},{11,1... | collective-permute-start | bytes 294920 | tf_op jit(solution)/shard_map/ppermute | solution.py:1249
  255.4 15.3 %collective-permute-start.2 = (bf16[4,16,768]{2,1,0:T(8,128)(2,1)S(1)}, bf16[4,16,768]{2,1,0:T(8,128)(2,1)S(1)}, u32[]{:S(2)}, u32[]{:S(2)}) collective-permute-start(bf16[4,16,768]{2,1,0:T(8,128)(2,1)S(1)} %get-tuple-element.253), channel_id=1, source_target_pairs={{0,1},{1,2},{2,3},{3,4},{4,5},{5,6},{6,7},{7,0},{8,9},{9,10},{10,1... | collective-permute-start | bytes 294920 | tf_op jit(solution)/shard_map/ppermute | solution.py:1250
  263.2 39.3 %collective-permute-start.6 = (bf16[2,2,2,96,768]{4,3,1,0,2:T(8,128)(2,1)}, bf16[2,2,2,96,768]{4,3,1,0,2:T(8,128)(2,1)}, u32[]{:S(2)}, u32[]{:S(2)}) collective-permute-start(bf16[2,2,2,96,768]{4,3,1,0,2:T(8,128)(2,1)} %copy.98), channel_id=1, source_target_pairs={{0,16},{8,24},{16,0},{24,8},{1,17},{9,25},{17,1},{25,9},{2,18},{10... | collective-permute-start | bytes 3538952 | tf_op jit(solution)/shard_map/ppermute | solution.py:1096
  269.3 37.9 %collective-permute-start.8 = (bf16[2,2,384,384]{3,2,1,0:T(8,128)(2,1)}, bf16[2,2,384,384]{3,2,1,0:T(8,128)(2,1)}, u32[]{:S(2)}, u32[]{:S(2)}) collective-permute-start(bf16[2,2,384,384]{3,2,1,0:T(8,128)(2,1)} %fusion.3.refs_9_), channel_id=1, source_target_pairs={{0,1},{1,0},{2,3},{3,2},{4,5},{5,4},{6,7},{7,6},{8,9},{9,8},{10,11... | collective-permute-start | bytes 3538952 | tf_op jit(solution)/shard_map/ppermute | solution.py:1096
  296.4 50.6 %all-to-all-start.4 = ((bf16[8,80,384]{2,1,0:T(8,128)(2,1)}), bf16[8,80,384]{2,1,0:T(8,128)(2,1)S(1)}, u32[]{:S(2)}, u32[]{:S(2)}) async-start(bf16[8,80,384]{2,1,0:T(8,128)(2,1)} %get-tuple-element.133), calls=%async_computation.4 | async-start | bytes 983040 | tf_op jit(solution)/shard_map/all_to_all | solution.py:1104
  305.1 36.9 %collective-permute-start.7 = (bf16[2,2,96,768]{3,2,1,0:T(8,128)(2,1)}, bf16[2,2,96,768]{3,2,1,0:T(8,128)(2,1)}, u32[]{:S(2)}, u32[]{:S(2)}) collective-permute-start(bf16[2,2,96,768]{3,2,1,0:T(8,128)(2,1)} %fusion.7.refs_9_), channel_id=1, source_target_pairs={{0,1},{1,0},{2,3},{3,2},{4,5},{5,4},{6,7},{7,6},{8,9},{9,8},{10,11... | collective-permute-start | bytes 1769480 | tf_op jit(solution)/shard_map/ppermute | solution.py:1096
  310.0 34.1 %collective-permute-start.9 = (bf16[2,2,192,384]{3,2,1,0:T(8,128)(2,1)}, bf16[2,2,192,384]{3,2,1,0:T(8,128)(2,1)}, u32[]{:S(2)}, u32[]{:S(2)}) collective-permute-start(bf16[2,2,192,384]{3,2,1,0:T(8,128)(2,1)} %dynamic-slice_convert_fusion.2.refs_10_), channel_id=1, source_target_pairs={{0,16},{8,24},{16,0},{24,8},{1,17},{9,25},{17,1},{25,9},{2,18},{10... | collective-permute-start | bytes 1769480 | tf_op jit(solution)/shard_map/ppermute | solution.py:1096
  358.4 24.5 %all-to-all-start.5 = ((bf16[8,8,8,768]{3,2,1,0:T(8,128)(2,1)}), bf16[8,8,8,768]{3,2,1,0:T(8,128)(2,1)S(1)}, u32[]{:S(2)}, u32[]{:S(2)}) async-start(bf16[8,8,8,768]{3,2,1,0:T(8,128)(2,1)} %bitcast.193.refs_8_), calls=%async_computation.5 | async-start | bytes 1572864 | tf_op jit(solution)/shard_map/all_to_all | solution.py:1104
  363.1 38.6 %collective-permute-start.26 = (bf16[2,96,768]{2,1,0:T(8,128)(2,1)}, bf16[2,96,768]{2,1,0:T(8,128)(2,1)}, u32[]{:S(2)}, u32[]{:S(2)}) collective-permute-start(bf16[2,96,768]{2,1,0:T(8,128)(2,1)} %fusion.13.refs_5_), channel_id=1, source_target_pairs={{0,2},{1,3},{2,0},{3,1},{4,6},{5,7},{6,4},{7,5},{8,10},{9,11},{10,... | collective-permute-start | bytes 884744 | tf_op jit(solution)/shard_map/ppermute | solution.py:1096
  365.1 37.8 %collective-permute-start.27 = (bf16[2,192,384]{2,1,0:T(8,128)(2,1)}, bf16[2,192,384]{2,1,0:T(8,128)(2,1)}, u32[]{:S(2)}, u32[]{:S(2)}) collective-permute-start(bf16[2,192,384]{2,1,0:T(8,128)(2,1)} %fusion.14.refs_6_), channel_id=1, source_target_pairs={{0,2},{1,3},{2,0},{3,1},{4,6},{5,7},{6,4},{7,5},{8,10},{9,11},{10,... | collective-permute-start | bytes 884744 | tf_op jit(solution)/shard_map/ppermute | solution.py:1096
  365.1 11.7 %collective-permute-start.11 = (f32[72,128]{1,0:T(8,128)S(1)}, f32[72,128]{1,0:T(8,128)S(1)}, u32[]{:S(2)}, u32[]{:S(2)}) collective-permute-start(f32[72,128]{1,0:T(8,128)S(1)} %copy-done.23), channel_id=1, source_target_pairs={{0,16},{8,24},{16,0},{24,8},{1,17},{9,25},{17,1},{25,9},{2,18},{10... | collective-permute-start | bytes 110600 | tf_op jit(solution)/shard_map/ppermute | solution.py:1096
  376.8 30.8 %collective-permute-start.13 = (bf16[768,768]{1,0:T(8,128)(2,1)}, bf16[768,768]{1,0:T(8,128)(2,1)}, u32[]{:S(2)}, u32[]{:S(2)}) collective-permute-start(bf16[768,768]{1,0:T(8,128)(2,1)} %get-tuple-element.167), channel_id=1, source_target_pairs={{0,8},{8,0},{16,24},{24,16},{1,9},{9,1},{17,25},{25,17},{2,10},{10... | collective-permute-start | bytes 3538952 | tf_op jit(solution)/shard_map/ppermute | solution.py:1096
  401.6 16.7 %collective-permute-start.12 = (bf16[768,768]{1,0:T(8,128)(2,1)}, bf16[768,768]{1,0:T(8,128)(2,1)S(1)}, u32[]{:S(2)}, u32[]{:S(2)}) collective-permute-start(bf16[768,768]{1,0:T(8,128)(2,1)} %get-tuple-element.164), channel_id=1, source_target_pairs={{0,8},{8,0},{16,24},{24,16},{1,9},{9,1},{17,25},{25,17},{2,10},{10... | collective-permute-start | bytes 3538952 | tf_op jit(solution)/shard_map/ppermute | solution.py:1096
  404.6 13.0 %collective-permute-start.28 = (bf16[96,768]{1,0:T(8,128)(2,1)S(1)}, bf16[96,768]{1,0:T(8,128)(2,1)S(1)}, u32[]{:S(2)}, u32[]{:S(2)}) collective-permute-start(bf16[96,768]{1,0:T(8,128)(2,1)S(1)} %fusion.21), channel_id=1, source_target_pairs={{0,4},{1,5},{2,6},{3,7},{4,0},{5,1},{6,2},{7,3},{8,12},{9,13},{10,... | collective-permute-start | bytes 442376 | tf_op jit(solution)/shard_map/ppermute | solution.py:1096
  404.7 35.2 %collective-permute-start.29 = (bf16[192,384]{1,0:T(8,128)(2,1)}, bf16[192,384]{1,0:T(8,128)(2,1)}, u32[]{:S(2)}, u32[]{:S(2)}) collective-permute-start(bf16[192,384]{1,0:T(8,128)(2,1)} %fusion.22), channel_id=1, source_target_pairs={{0,4},{1,5},{2,6},{3,7},{4,0},{5,1},{6,2},{7,3},{8,12},{9,13},{10,... | collective-permute-start | bytes 442376 | tf_op jit(solution)/shard_map/ppermute | solution.py:1096
  410.1 39.3 %collective-permute-start.17 = (bf16[2,2,96,768]{3,2,1,0:T(8,128)(2,1)}, bf16[2,2,96,768]{3,2,1,0:T(8,128)(2,1)}, u32[]{:S(2)}, u32[]{:S(2)}) collective-permute-start(bf16[2,2,96,768]{3,2,1,0:T(8,128)(2,1)} %get-tuple-element.239.refs_12_), channel_id=1, source_target_pairs={{0,1},{1,0},{2,3},{3,2},{4,5},{5,4},{6,7},{7,6},{8,9},{9,8},{10,11... | collective-permute-start | bytes 1769480 | tf_op jit(solution)/shard_map/ppermute | solution.py:1096
  419.7 17.6 %collective-permute-start.14 = (bf16[384,768]{1,0:T(8,128)(2,1)}, bf16[384,768]{1,0:T(8,128)(2,1)}, u32[]{:S(2)}, u32[]{:S(2)}) collective-permute-start(bf16[384,768]{1,0:T(8,128)(2,1)} %get-tuple-element.241.refs_11_), channel_id=1, source_target_pairs={{0,16},{8,24},{16,0},{24,8},{1,17},{9,25},{17,1},{25,9},{2,18},{10... | collective-permute-start | bytes 1769480 | tf_op jit(solution)/shard_map/ppermute | solution.py:1096
  440.8 42.5 %all-to-all-start.6 = ((bf16[8,384,96]{1,2,0:T(8,128)(2,1)}), bf16[8,384,96]{1,2,0:T(8,128)(2,1)S(1)}, u32[]{:S(2)}, u32[]{:S(2)}) async-start(bf16[8,384,96]{1,2,0:T(8,128)(2,1)} %bitcast.49), calls=%async_computation.6 | async-start | bytes 1179648 | tf_op jit(solution)/shard_map/all_to_all | solution.py:1104
  445.3 23.2 %collective-permute-start.30 = (bf16[96,768]{1,0:T(8,128)(2,1)S(1)}, bf16[96,768]{1,0:T(8,128)(2,1)S(1)}, u32[]{:S(2)}, u32[]{:S(2)}) collective-permute-start(bf16[96,768]{1,0:T(8,128)(2,1)S(1)} %copy-done.21), channel_id=1, source_target_pairs={{0,16},{8,24},{16,0},{24,8},{1,17},{9,25},{17,1},{25,9},{2,18},{10... | collective-permute-start | bytes 442376 | tf_op jit(solution)/shard_map/ppermute | solution.py:1096
  446.8 14.7 %collective-permute-start.32 = (bf16[192,384]{1,0:T(8,128)(2,1)S(1)}, bf16[192,384]{1,0:T(8,128)(2,1)S(1)}, u32[]{:S(2)}, u32[]{:S(2)}) collective-permute-start(bf16[192,384]{1,0:T(8,128)(2,1)S(1)} %fusion.16), channel_id=1, source_target_pairs={{0,16},{8,24},{16,0},{24,8},{1,17},{9,25},{17,1},{25,9},{2,18},{10... | collective-permute-start | bytes 442376 | tf_op jit(solution)/shard_map/ppermute | solution.py:1096
  447.4 8.0 %collective-permute-start.24 = (f32[72,128]{1,0:T(8,128)S(1)}, f32[72,128]{1,0:T(8,128)S(1)}, u32[]{:S(2)}, u32[]{:S(2)}) collective-permute-start(f32[72,128]{1,0:T(8,128)S(1)} %add.244), channel_id=1, source_target_pairs={{0,2},{1,3},{2,0},{3,1},{4,6},{5,7},{6,4},{7,5},{8,10},{9,11},{10,... | collective-permute-start | bytes 110600 | tf_op jit(solution)/shard_map/ppermute | solution.py:1096
  457.1 9.3 %collective-permute-start.18 = (bf16[2,96,768]{2,1,0:T(8,128)(2,1)S(1)}, bf16[2,96,768]{2,1,0:T(8,128)(2,1)S(1)}, u32[]{:S(2)}, u32[]{:S(2)}) collective-permute-start(bf16[2,96,768]{2,1,0:T(8,128)(2,1)S(1)} %fusion.10), channel_id=1, source_target_pairs={{0,2},{1,3},{2,0},{3,1},{4,6},{5,7},{6,4},{7,5},{8,10},{9,11},{10,... | collective-permute-start | bytes 884744 | tf_op jit(solution)/shard_map/ppermute | solution.py:1096
  461.5 18.7 %collective-permute-start.33 = (bf16[384,384]{1,0:T(8,128)(2,1)S(1)}, bf16[384,384]{1,0:T(8,128)(2,1)S(1)}, u32[]{:S(2)}, u32[]{:S(2)}) collective-permute-start(bf16[384,384]{1,0:T(8,128)(2,1)S(1)} %maximum_select_fusion.1), channel_id=1, source_target_pairs={{0,8},{8,0},{16,24},{24,16},{1,9},{9,1},{17,25},{25,17},{2,10},{10... | collective-permute-start | bytes 884744 | tf_op jit(solution)/shard_map/ppermute | solution.py:1096
  466.4 7.8 %collective-permute-start.19 = (bf16[96,768]{1,0:T(8,128)(2,1)S(1)}, bf16[96,768]{1,0:T(8,128)(2,1)S(1)}, u32[]{:S(2)}, u32[]{:S(2)}) collective-permute-start(bf16[96,768]{1,0:T(8,128)(2,1)S(1)} %fusion.19), channel_id=1, source_target_pairs={{0,4},{1,5},{2,6},{3,7},{4,0},{5,1},{6,2},{7,3},{8,12},{9,13},{10,... | collective-permute-start | bytes 442376 | tf_op jit(solution)/shard_map/ppermute | solution.py:1096
  (44 other events, 195.2 us)

commit v5 on v4

--- a/solution.py
+++ b/solution.py
@@ -1383,12 +1383,10 @@
     query_key.over_x()
     ready = query_key.value
     up.own, down.own = tied((up.own, down.own), ready)
-    packed.step(ready)
-    packed.step(ready)
     value_out.wait_for(ready)
-    value_out.step()
-    value_out.step()
-    value_out.step()
+    for _ in range(3):
+        value_out.step()
+        packed.step(value_out.theirs)
     value_out.last()
     query_key.over_seq()
     up_a, up_b = up.both()
@@ -1396,7 +1394,7 @@
     v_a, v_b = value_out.both()
     q_g, k_g = query_key.both()
 
-    packed = packed.step(ready).reshape(-1)
+    packed = packed.values.reshape(-1)
     small = packed[: 6 * D].reshape(6, D)
     small_up = packed[6 * D : 6 * D + FF]
     taps_g = packed[6 * D + FF :].reshape(H, 128)[:, :TAPS].T

time: 497 us -> 495 us (level)
  transfers between devices with their start and end apart: 41 -> 41, of which waited for: 12 -> 11; matrix products, arithmetic and copies ran while one was open for 12% -> 12% of each run, Pallas kernels for 33% -> 33%
where the time goes in v5:
time: 495 us; the launch traced here: 488 us
  Pallas kernels  303 us (61%)
  starting transfers between devices  69.4 us (14%)
  waiting for transfers between devices  41.5 us (8%)
  local copies, waits for them, and re-layouts  33.7 us (7%)
  other arithmetic  32.9 us (7%)
    pallas_call x1, Pallas kernels, dense(): pl.pallas_call(functools.partial(dense_kernel, nl, tile, chunk), grid=(nl...  125 us
    all_to_all x7, starting transfers between devices, exchange(): return lax.all_to_all(values, 'seq', 0, 0, tiled=True)  31.5 us
    pallas_call x1, Pallas kernels, back_inverse(): pl.pallas_call(after(back_inverse_kernel, 9, deps), grid_spec=pltpu.Prefe...  28.3 us
    ppermute x30, waiting for transfers between devices, swap(): return lax.ppermute(values, axis, [(i, i ^ bit) for i in range(count)])  27.8 us
    ppermute x30, starting transfers between devices, swap(): return lax.ppermute(values, axis, [(i, i ^ bit) for i in range(count)])  27.1 us
    pallas_call x2, Pallas kernels, project(): pl.pallas_call(after(functools.partial(project_kernel, nl, n), 3 + n, dep...  21.6 us
    pallas_call x1, Pallas kernels, score_grads(): pl.pallas_call(after(functools.partial(score_grads_kernel, items), 18, de...  17.8 us
    pallas_call x1, Pallas kernels, input_grad(): pl.pallas_call(after(functools.partial(input_grad_kernel, nl), 11, deps),...  17.1 us
  transfers between devices with their start and end apart: 41, of which 11 were waited for; matrix products, arithmetic and copies ran while one was open for 12% of the time, Pallas kernels for 33%

profile of v5, /device:TPU:0, one launch (start us, length us, event | category | flops | bytes accessed | tf_op | source)
XLA Modules:
  0.0 487.8 jit_solution(14209059328332588633)
XLA Ops:
  5.2 3.0 collective-permute-start.1
  11.8 3.5 all-to-all-start
  18.7 12.9 %project.2 = (bf16[768,2048]{1,0:T(8,128)(2,1)}, bf16[768,2048]{1,0:T(8,128)(2,1)}, bf16[768,512]{1,0:T(8,128)(2,1)}, bf16[768,512]{1,0:T(8,128)(2,1)}, bf16[64,768]{1,0:T(8,128)(2,1)}) custom-call(s32[1]{0:T(128)} %bitcast.194.refs_0_, bf16[2048,768]{1,0:T(8,128)(2,1)} %bitcast.202, bf16[512,768]{1,0:T(8,128)(2,1)} %bitcast.233, bf16[768,768]{1,0:T(8,128)(2,1)} %refs_9_.1, ...), custom_call_target="tpu_custom_call" | custom-call | flops 6039797760 | bytes 15728640 | tf_op jit(solution)/shard_map/project/pallas_call | solution.py:156
  41.1 7.3 %stats.1.refs_4_ = f32[8,72,384]{2,1,0:T(8,128)} custom-call(bf16[256,768]{1,0:T(8,128)(2,1)} %fusion.1.lq.lq_l.refs_0_.refs_1_.refs_3_, bf16[768,2048]{1,0:T(8,128)(2,1)} %get-tuple-element.98.k.refs_3_, bf16[768,2048]{1,0:T(8,128)(2,1)} %get-tuple-element.99.v.v_l.refs_1_.refs_4_), custom_call_target="tpu_custom_call" | custom-call | flops 1610612736 | bytes 6291456 | tf_op jit(solution)/shard_map/stats/pallas_call | solution.py:207
  48.4 3.8 all-to-all-start.1
  52.2 8.7 %project.3 = (bf16[768,2048]{1,0:T(8,128)(2,1)}, bf16[768,512]{1,0:T(8,128)(2,1)}, bf16[64,768]{1,0:T(8,128)(2,1)}) custom-call(s32[1]{0:T(128)} %bitcast.195.refs_0_, bf16[2048,768]{1,0:T(8,128)(2,1)} %bitcast.203, bf16[512,768]{1,0:T(8,128)(2,1)} %bitcast.234, bf16[768,768]{1,0:T(8,128)(2,1)} %refs_8_.1, f32[8,72,384]{2,1,0:T(8,128)} %stats.1.refs_4_), custom_call_target="tpu_custom_call" | custom-call | flops 3019898880 | bytes 7864320 | tf_op jit(solution)/shard_map/project/pallas_call | solution.py:156
  60.9 9.1 %inverse.1 = (f32[64,384]{1,0:T(8,128)}, f32[64,768]{1,0:T(8,128)}) custom-call(s32[2]{0:T(128)} %pad_add_fusion.at.refs_0_, bf16[256,768]{1,0:T(8,128)(2,1)} %fusion.1.lq.lq_l.refs_0_.refs_1_.refs_3_, bf16[256,768]{1,0:T(8,128)(2,1)} %fusion.lk_l.lk.refs_2_.refs_4_, bf16[64,768]{1,0:T(8,128)(2,1)} %get-tuple-element.100.lq_s.lq.refs_4_.refs_3_.refs_10_, ...), custom_call_target="tpu_custom_call" | custom-call | flops 13589544960 | bytes 1000000 | tf_op jit(solution)/shard_map/inverse/pallas_call | solution.py:273
  70.1 4.5 all-to-all-done.1.msg
  75.5 3.1 combine.1
  78.6 4.3 all-to-all-start.2
  85.3 8.2 %conv.1 = (f32[768,2048]{1,0:T(8,128)}, f32[768,512]{1,0:T(8,128)}) custom-call(s32[1]{0:T(128)} %bitcast.196.length, bf16[768,2048]{1,0:T(8,128)(2,1)} %get-tuple-element.99.v.v_l.refs_1_.refs_4_, bf16[768,512]{1,0:T(8,128)(2,1)} %get-tuple-element.105.v_s.v.refs_2_.refs_3_, bf16[768,128]{1,0:T(8,128)(2,1)} %fusion.4.rim.refs_3_, ...), custom_call_target="tpu_custom_call" | custom-call | flops 3221225472 | bytes 12582912 | tf_op jit(solution)/shard_map/conv/pallas_call | solution.py:456
  93.5 6.5 %short_attend.1 = (bf16[768,512]{1,0:T(8,128)(2,1)}, bf16[64,768]{1,0:T(8,128)(2,1)}, f32[64,768]{1,0:T(8,128)}) custom-call(s32[1]{0:T(128)} %bitcast.197.length, bf16[768,512]{1,0:T(8,128)(2,1)} %get-tuple-element.107.q.refs_1_, bf16[768,512]{1,0:T(8,128)(2,1)} %get-tuple-element.108.k.refs_2_, bf16[768,512]{1,0:T(8,128)(2,1)} %get-tuple-element.105.v_s.v.refs_2_.refs_3_, ...), custom_call_target="tpu_custom_call" | custom-call | flops 805306368 | bytes 3932160 | tf_op jit(solution)/shard_map/short_attend/pallas_call | solution.py:357
  100.8 8.9 %mix.1.o_l = bf16[768,2048]{1,0:T(8,128)(2,1)} custom-call(bf16[256,768]{1,0:T(8,128)(2,1)} %fusion.lk_l.lk.refs_2_.refs_4_, bf16[8,80,384]{2,1,0:T(8,128)(2,1)} %copy-done.17, bf16[768,2048]{1,0:T(8,128)(2,1)} %get-tuple-element.104.q, f32[768,2048]{1,0:T(8,128)} %get-tuple-element.106.conv), custom_call_target="tpu_custom_call" | custom-call | flops 1610612736 | bytes 12582912 | tf_op jit(solution)/shard_map/mix/pallas_call | solution.py:375
  109.7 124.7 %dense.1 = (bf16[2048,768]{1,0:T(8,128)(2,1)}, bf16[512,768]{1,0:T(8,128)(2,1)}, f32[2048,768]{1,0:T(8,128)}, f32[512,768]{1,0:T(8,128)}, bf16[768,2048]{1,0:T(8...) custom-call(s32[1]{0:T(128)} %bitcast.core.refs_0_.refs_1_, ...), custom_call_target="tpu_custom_call" | custom-call | flops 81537269760 | bytes 60000000 | tf_op jit(solution)/shard_map/dense/pallas_call | solution.py:710
  235.7 8.7 %back_f.1 = (f32[8,64,384]{2,1,0:T(8,128)}, f32[256,768]{1,0:T(8,128)}, bf16[768,2048]{1,0:T(8,128)(2,1)}, bf16[4,32,768]{2,1,0:T(8,128)(2,1)}) custom-call(bf16[256,768]{1,0:T(8,128)(2,1)} %fusion.lk_l.lk.refs_2_.refs_4_, bf16[8,80,384]{2,1,0:T(8,128)(2,1)} %copy-done.17, bf16[768,2048]{1,0:T(8,128)(2,1)} %get-tuple-element.104.q, ...), custom_call_target="tpu_custom_call" | custom-call | flops 3221225472 | bytes 9437184 | tf_op jit(solution)/shard_map/back_f/pallas_call | solution.py:774
  244.3 6.1 %all-to-all-start.3 = ((f32[8,64,384]{2,1,0:T(8,128)}), f32[8,64,384]{2,1,0:T(8,128)S(1)}, u32[]{:S(2)}, u32[]{:S(2)}) async-start(f32[8,64,384]{2,1,0:T(8,128)} %get-tuple-element.117), calls=%async_computation.3 | async-start | bytes 1572864 | tf_op jit(solution)/shard_map/all_to_all | solution.py:1104
  250.5 4.8 collective-permute-start.3
  255.3 3.0 convert_add_fusion.1
  271.5 10.7 %conv_back.1 = (f32[768,2048]{1,0:T(8,128)}, f32[768,512]{1,0:T(8,128)}, f32[12,8,128]{2,1,0:T(8,128)}) custom-call(s32[1]{0:T(128)} %bitcast.198.refs_0_, bf16[768,2048]{1,0:T(8,128)(2,1)} %get-tuple-element.99.v.v_l.refs_1_.refs_4_, bf16[768,512]{1,0:T(8,128)(2,1)} %get-tuple-element.105.v_s.v.refs_2_.refs_3_, bf16[768,128]{1,0:T(8,128)(2,1)} %fusion.4.rim.refs_3_, ...), custom_call_target="tpu_custom_call" | custom-call | flops 4831838208 | bytes 18874368 | tf_op jit(solution)/shard_map/conv_back/pallas_call | solution.py:487
  282.2 9.2 %short_back.1 = (bf16[768,512]{1,0:T(8,128)(2,1)}, bf16[768,512]{1,0:T(8,128)(2,1)}, bf16[768,512]{1,0:T(8,128)(2,1)}, f32[64,768]{1,0:T(8,128)}, f32[64,768]{1,...) custom-call(s32[1]{0:T(128)} %bitcast.199.refs_0_, bf16[768,512]{1,0:T(8,128)(2,1)} %get-tuple-element.107.q.refs_1_, ...), custom_call_target="tpu_custom_call" | custom-call | flops 2415919104 | bytes 7864320 | tf_op jit(solution)/shard_map/short_back/pallas_call | solution.py:961
  296.3 5.5 %all-to-all-start.4 = ((bf16[8,80,384]{2,1,0:T(8,128)(2,1)}), bf16[8,80,384]{2,1,0:T(8,128)(2,1)S(1)}, u32[]{:S(2)}, u32[]{:S(2)}) async-start(bf16[8,80,384]{2,1,0:T(8,128)(2,1)} %get-tuple-element.133), calls=%async_computation.4 | async-start | bytes 983040 | tf_op jit(solution)/shard_map/all_to_all | solution.py:1104
  311.4 28.3 %back_inverse.1 = (f32[64,384]{1,0:T(8,128)}, f32[64,384]{1,0:T(8,128)}, f32[64,768]{1,0:T(8,128)}, f32[64,768]{1,0:T(8,128)}) custom-call(s32[2]{0:T(128)} %pad_add_fusion.at.refs_0_, bf16[256,768]{1,0:T(8,128)(2,1)} %fusion.1.lq.lq_l.refs_0_.refs_1_.refs_3_, bf16[256,768]{1,0:T(8,128)(2,1)} %fusion.lk_l.lk.refs_2_.refs_4_, ...), custom_call_target="tpu_custom_call" | custom-call | flops 40768634880 | bytes 2000000 | tf_op jit(solution)/shard_map/back_inverse/pallas_call | solution.py:854
  347.6 8.1 %back_b.1 = (bf16[768,2048]{1,0:T(8,128)(2,1)}, bf16[768,2048]{1,0:T(8,128)(2,1)}, f32[256,768]{1,0:T(8,128)}) custom-call(bf16[256,768]{1,0:T(8,128)(2,1)} %fusion.1.lq.lq_l.refs_0_.refs_1_.refs_3_, bf16[8,80,384]{2,1,0:T(8,128)(2,1)} %copy-done.17, bf16[8,80,384]{2,1,0:T(8,128)(2,1)} %copy-done.18, bf16[768,2048]{1,0:T(8,128)(2,1)} %get-tuple-element.98.k.refs_3_, ...), custom_call_target="tpu_custom_call" | custom-call | flops 3221225472 | bytes 15728640 | tf_op jit(solution)/shard_map/back_b/pallas_call | solution.py:890
  358.3 4.7 all-to-all-start.5
  365.6 11.1 %back_v.1 = (bf16[768,2048]{1,0:T(8,128)(2,1)}, bf16[768,768]{1,0:T(8,128)(2,1)}, bf16[768,768]{1,0:T(8,128)(2,1)}) custom-call(s32[1]{0:T(128)} %bitcast.core.refs_0_.refs_1_, bf16[8,80,384]{2,1,0:T(8,128)(2,1)} %copy-done.18, bf16[768,2048]{1,0:T(8,128)(2,1)} %get-tuple-element.152.refs_2_, ...), custom_call_target="tpu_custom_call", output_to_operand_aliasing={{1}: (6, {}), {2}: (7, {})} | custom-call | flops 2415919104 | bytes 18874368 | tf_op jit(solution)/shard_map/back_v/pallas_call | solution.py:925
  377.4 5.4 %all-to-all-done.5 = bf16[8,8,8,768]{3,2,1,0:T(8,128)(2,1)S(1)} async-done(((bf16[8,8,8,768]{3,2,1,0:T(8,128)(2,1)}), bf16[8,8,8,768]{3,2,1,0:T(8,128)(2,1)S(1)}, u32[]{:S(2)}, u32[]{:S(2)}) %all-to-all-start.5) | async-done | bytes 786464 | tf_op jit(solution)/shard_map/all_to_all | solution.py:1104
  383.7 17.8 %score_grads.1 = (bf16[768,2048]{1,0:T(8,128)(2,1)}, bf16[768,2048]{1,0:T(8,128)(2,1)}, bf16[768,512]{1,0:T(8,128)(2,1)}, bf16[768,512]{1,0:T(8,128)(2,1)}, bf16...) custom-call(s32[1]{0:T(128)} %bitcast.200.refs_0_, s32[1]{0:T(128)} %bitcast.core.refs_0_.refs_1_, ...), custom_call_target="tpu_custom_call" | custom-call | flops 9059696640 | bytes 39321600 | tf_op jit(solution)/shard_map/score_grads/pallas_call | solution.py:1029
  411.3 6.3 %collective-permute-done.28 = bf16[96,768]{1,0:T(8,128)(2,1)S(1)} collective-permute-done((bf16[96,768]{1,0:T(8,128)(2,1)S(1)}, bf16[96,768]{1,0:T(8,128)(2,1)S(1)}, u32[]{:S(2)}, u32[]{:S(2)}) %collective-permute-start.28) | collective-permute-done | bytes 147488 | tf_op jit(solution)/shard_map/ppermute | solution.py:1096
  420.2 17.1 %input_grad.1 = (bf16[2048,768]{1,0:T(8,128)(2,1)}, bf16[512,768]{1,0:T(8,128)(2,1)}) custom-call(f32[2048,768]{1,0:T(8,128)} %get-tuple-element.114.refs_0_, bf16[768,2048]{1,0:T(8,128)(2,1)} %get-tuple-element.158.refs_1_, bf16[768,2048]{1,0:T(8,128)(2,1)} %get-tuple-element.159.refs_2_, bf16[768,2048]{1,0:T(8,128)(2,1)} %get-tuple-element.157.refs_19_.refs_3_, ...), custom_call_target="tpu_custom_call" | custom-call | flops 9059696640 | bytes 23592960 | tf_op jit(solution)/shard_map/input_grad/pallas_call | solution.py:1080
  445.7 3.5 all-to-all-start.6
  454.7 7.2 %collective-permute-done.24 = f32[72,128]{1,0:T(8,128)S(1)} collective-permute-done((f32[72,128]{1,0:T(8,128)S(1)}, f32[72,128]{1,0:T(8,128)S(1)}, u32[]{:S(2)}, u32[]{:S(2)}) %collective-permute-start.24) | collective-permute-done | bytes 36896 | tf_op jit(solution)/shard_map/ppermute | solution.py:1096
  461.9 8.6 %collective-permute-done.19 = bf16[96,768]{1,0:T(8,128)(2,1)S(1)} collective-permute-done((bf16[96,768]{1,0:T(8,128)(2,1)S(1)}, bf16[96,768]{1,0:T(8,128)(2,1)S(1)}, u32[]{:S(2)}, u32[]{:S(2)}) %collective-permute-start.19) | collective-permute-done | bytes 147488 | tf_op jit(solution)/shard_map/ppermute | solution.py:1096
  (240 shorter events, 110.7 us)
Async XLA Ops:
  2.3 29.9 %collective-permute-start = (bf16[4,16,768]{2,1,0:T(8,128)(2,1)S(1)}, bf16[4,16,768]{2,1,0:T(8,128)(2,1)S(1)}, u32[]{:S(2)}, u32[]{:S(2)}) collective-permute-start(bf16[4,16,768]{2,1,0:T(8,128)(2,1)S(1)} %get-tuple-element.234), channel_id=1, source_target_pairs={{0,1},{1,2},{2,3},{3,4},{4,5},{5,6},{6,7},{7,0},{8,9},{9,10},{10,1... | collective-permute-start | bytes 294920 | tf_op jit(solution)/shard_map/ppermute | solution.py:1250
  5.2 77.8 %collective-permute-start.1 = (bf16[4,16,768]{2,1,0:T(8,128)(2,1)}, bf16[4,16,768]{2,1,0:T(8,128)(2,1)}, u32[]{:S(2)}, u32[]{:S(2)}) collective-permute-start(bf16[4,16,768]{2,1,0:T(8,128)(2,1)} %get-tuple-element.235), channel_id=1, source_target_pairs={{1,0},{2,1},{3,2},{4,3},{5,4},{6,5},{7,6},{0,7},{9,8},{10,9},{11,1... | collective-permute-start | bytes 294920 | tf_op jit(solution)/shard_map/ppermute | solution.py:1249
  11.8 23.7 %all-to-all-start = ((f32[8,32,768]{2,1,0:T(8,128)}), f32[8,32,768]{2,1,0:T(8,128)S(1)}, u32[]{:S(2)}, u32[]{:S(2)}) async-start(f32[8,32,768]{2,1,0:T(8,128)} %broadcast_in_dim.28), calls=%async_computation | async-start | bytes 1572864 | tf_op jit(solution)/shard_map/all_to_all | solution.py:1104
  48.4 26.2 %all-to-all-start.1 = ((f32[8,72,384]{2,1,0:T(8,128)}), f32[8,72,384]{2,1,0:T(8,128)S(1)}, u32[]{:S(2)}, u32[]{:S(2)}) async-start(f32[8,72,384]{2,1,0:T(8,128)} %stats.1.refs_4_), calls=%async_computation.1 | async-start | bytes 1769472 | tf_op jit(solution)/shard_map/all_to_all | solution.py:1104
  78.6 21.4 %all-to-all-start.2 = ((bf16[8,80,384]{2,1,0:T(8,128)(2,1)}), bf16[8,80,384]{2,1,0:T(8,128)(2,1)S(1)}, u32[]{:S(2)}, u32[]{:S(2)}) async-start(bf16[8,80,384]{2,1,0:T(8,128)(2,1)} %get-tuple-element.103), calls=%async_computation.2 | async-start | bytes 983040 | tf_op jit(solution)/shard_map/all_to_all | solution.py:1104
  234.4 20.9 %collective-permute-start.4 = (bf16[768,1536]{1,0:T(8,128)(2,1)}, bf16[768,1536]{1,0:T(8,128)(2,1)}, u32[]{:S(2)}, u32[]{:S(2)}) collective-permute-start(bf16[768,1536]{1,0:T(8,128)(2,1)} %get-tuple-element.126), channel_id=1, source_target_pairs={{0,8},{8,0},{16,24},{24,16},{1,9},{9,1},{17,25},{25,17},{2,10},{10... | collective-permute-start | bytes 7077896 | tf_op jit(solution)/shard_map/ppermute | solution.py:1096
  234.4 30.2 %collective-permute-start.5 = (bf16[384,3072]{1,0:T(8,128)(2,1)}, bf16[384,3072]{1,0:T(8,128)(2,1)}, u32[]{:S(2)}, u32[]{:S(2)}) collective-permute-start(bf16[384,3072]{1,0:T(8,128)(2,1)} %get-tuple-element.128), channel_id=1, source_target_pairs={{0,8},{8,0},{16,24},{24,16},{1,9},{9,1},{17,25},{25,17},{2,10},{10... | collective-permute-start | bytes 7077896 | tf_op jit(solution)/shard_map/ppermute | solution.py:1096
  244.3 47.1 %all-to-all-start.3 = ((f32[8,64,384]{2,1,0:T(8,128)}), f32[8,64,384]{2,1,0:T(8,128)S(1)}, u32[]{:S(2)}, u32[]{:S(2)}) async-start(f32[8,64,384]{2,1,0:T(8,128)} %get-tuple-element.117), calls=%async_computation.3 | async-start | bytes 1572864 | tf_op jit(solution)/shard_map/all_to_all | solution.py:1104
  250.5 18.9 %collective-permute-start.3 = (bf16[4,16,768]{2,1,0:T(8,128)(2,1)S(1)}, bf16[4,16,768]{2,1,0:T(8,128)(2,1)S(1)}, u32[]{:S(2)}, u32[]{:S(2)}) collective-permute-start(bf16[4,16,768]{2,1,0:T(8,128)(2,1)S(1)} %get-tuple-element.252), channel_id=1, source_target_pairs={{1,0},{2,1},{3,2},{4,3},{5,4},{6,5},{7,6},{0,7},{9,8},{10,9},{11,1... | collective-permute-start | bytes 294920 | tf_op jit(solution)/shard_map/ppermute | solution.py:1249
  255.3 15.3 %collective-permute-start.2 = (bf16[4,16,768]{2,1,0:T(8,128)(2,1)S(1)}, bf16[4,16,768]{2,1,0:T(8,128)(2,1)S(1)}, u32[]{:S(2)}, u32[]{:S(2)}) collective-permute-start(bf16[4,16,768]{2,1,0:T(8,128)(2,1)S(1)} %get-tuple-element.253), channel_id=1, source_target_pairs={{0,1},{1,2},{2,3},{3,4},{4,5},{5,6},{6,7},{7,0},{8,9},{9,10},{10,1... | collective-permute-start | bytes 294920 | tf_op jit(solution)/shard_map/ppermute | solution.py:1250
  263.1 39.3 %collective-permute-start.6 = (bf16[2,2,2,96,768]{4,3,1,0,2:T(8,128)(2,1)}, bf16[2,2,2,96,768]{4,3,1,0,2:T(8,128)(2,1)}, u32[]{:S(2)}, u32[]{:S(2)}) collective-permute-start(bf16[2,2,2,96,768]{4,3,1,0,2:T(8,128)(2,1)} %copy.98), channel_id=1, source_target_pairs={{0,16},{8,24},{16,0},{24,8},{1,17},{9,25},{17,1},{25,9},{2,18},{10... | collective-permute-start | bytes 3538952 | tf_op jit(solution)/shard_map/ppermute | solution.py:1096
  269.2 37.9 %collective-permute-start.8 = (bf16[2,2,384,384]{3,2,1,0:T(8,128)(2,1)}, bf16[2,2,384,384]{3,2,1,0:T(8,128)(2,1)}, u32[]{:S(2)}, u32[]{:S(2)}) collective-permute-start(bf16[2,2,384,384]{3,2,1,0:T(8,128)(2,1)} %fusion.3.refs_9_), channel_id=1, source_target_pairs={{0,1},{1,0},{2,3},{3,2},{4,5},{5,4},{6,7},{7,6},{8,9},{9,8},{10,11... | collective-permute-start | bytes 3538952 | tf_op jit(solution)/shard_map/ppermute | solution.py:1096
  296.3 50.6 %all-to-all-start.4 = ((bf16[8,80,384]{2,1,0:T(8,128)(2,1)}), bf16[8,80,384]{2,1,0:T(8,128)(2,1)S(1)}, u32[]{:S(2)}, u32[]{:S(2)}) async-start(bf16[8,80,384]{2,1,0:T(8,128)(2,1)} %get-tuple-element.133), calls=%async_computation.4 | async-start | bytes 983040 | tf_op jit(solution)/shard_map/all_to_all | solution.py:1104
  305.1 36.9 %collective-permute-start.7 = (bf16[2,2,96,768]{3,2,1,0:T(8,128)(2,1)}, bf16[2,2,96,768]{3,2,1,0:T(8,128)(2,1)}, u32[]{:S(2)}, u32[]{:S(2)}) collective-permute-start(bf16[2,2,96,768]{3,2,1,0:T(8,128)(2,1)} %fusion.7.refs_9_), channel_id=1, source_target_pairs={{0,1},{1,0},{2,3},{3,2},{4,5},{5,4},{6,7},{7,6},{8,9},{9,8},{10,11... | collective-permute-start | bytes 1769480 | tf_op jit(solution)/shard_map/ppermute | solution.py:1096
  309.9 34.1 %collective-permute-start.9 = (bf16[2,2,192,384]{3,2,1,0:T(8,128)(2,1)}, bf16[2,2,192,384]{3,2,1,0:T(8,128)(2,1)}, u32[]{:S(2)}, u32[]{:S(2)}) collective-permute-start(bf16[2,2,192,384]{3,2,1,0:T(8,128)(2,1)} %dynamic-slice_convert_fusion.2.refs_10_), channel_id=1, source_target_pairs={{0,16},{8,24},{16,0},{24,8},{1,17},{9,25},{17,1},{25,9},{2,18},{10... | collective-permute-start | bytes 1769480 | tf_op jit(solution)/shard_map/ppermute | solution.py:1096
  358.3 24.5 %all-to-all-start.5 = ((bf16[8,8,8,768]{3,2,1,0:T(8,128)(2,1)}), bf16[8,8,8,768]{3,2,1,0:T(8,128)(2,1)S(1)}, u32[]{:S(2)}, u32[]{:S(2)}) async-start(bf16[8,8,8,768]{3,2,1,0:T(8,128)(2,1)} %bitcast.193.refs_8_), calls=%async_computation.5 | async-start | bytes 1572864 | tf_op jit(solution)/shard_map/all_to_all | solution.py:1104
  363.0 38.6 %collective-permute-start.26 = (bf16[2,96,768]{2,1,0:T(8,128)(2,1)}, bf16[2,96,768]{2,1,0:T(8,128)(2,1)}, u32[]{:S(2)}, u32[]{:S(2)}) collective-permute-start(bf16[2,96,768]{2,1,0:T(8,128)(2,1)} %fusion.13.refs_5_), channel_id=1, source_target_pairs={{0,2},{1,3},{2,0},{3,1},{4,6},{5,7},{6,4},{7,5},{8,10},{9,11},{10,... | collective-permute-start | bytes 884744 | tf_op jit(solution)/shard_map/ppermute | solution.py:1096
  365.0 37.8 %collective-permute-start.27 = (bf16[2,192,384]{2,1,0:T(8,128)(2,1)}, bf16[2,192,384]{2,1,0:T(8,128)(2,1)}, u32[]{:S(2)}, u32[]{:S(2)}) collective-permute-start(bf16[2,192,384]{2,1,0:T(8,128)(2,1)} %fusion.14.refs_6_), channel_id=1, source_target_pairs={{0,2},{1,3},{2,0},{3,1},{4,6},{5,7},{6,4},{7,5},{8,10},{9,11},{10,... | collective-permute-start | bytes 884744 | tf_op jit(solution)/shard_map/ppermute | solution.py:1096
  365.0 11.7 %collective-permute-start.11 = (f32[72,128]{1,0:T(8,128)S(1)}, f32[72,128]{1,0:T(8,128)S(1)}, u32[]{:S(2)}, u32[]{:S(2)}) collective-permute-start(f32[72,128]{1,0:T(8,128)S(1)} %copy-done.23), channel_id=1, source_target_pairs={{0,16},{8,24},{16,0},{24,8},{1,17},{9,25},{17,1},{25,9},{2,18},{10... | collective-permute-start | bytes 110600 | tf_op jit(solution)/shard_map/ppermute | solution.py:1096
  376.7 30.8 %collective-permute-start.13 = (bf16[768,768]{1,0:T(8,128)(2,1)}, bf16[768,768]{1,0:T(8,128)(2,1)}, u32[]{:S(2)}, u32[]{:S(2)}) collective-permute-start(bf16[768,768]{1,0:T(8,128)(2,1)} %get-tuple-element.167), channel_id=1, source_target_pairs={{0,8},{8,0},{16,24},{24,16},{1,9},{9,1},{17,25},{25,17},{2,10},{10... | collective-permute-start | bytes 3538952 | tf_op jit(solution)/shard_map/ppermute | solution.py:1096
  401.5 16.7 %collective-permute-start.12 = (bf16[768,768]{1,0:T(8,128)(2,1)}, bf16[768,768]{1,0:T(8,128)(2,1)S(1)}, u32[]{:S(2)}, u32[]{:S(2)}) collective-permute-start(bf16[768,768]{1,0:T(8,128)(2,1)} %get-tuple-element.164), channel_id=1, source_target_pairs={{0,8},{8,0},{16,24},{24,16},{1,9},{9,1},{17,25},{25,17},{2,10},{10... | collective-permute-start | bytes 3538952 | tf_op jit(solution)/shard_map/ppermute | solution.py:1096
  404.6 13.0 %collective-permute-start.28 = (bf16[96,768]{1,0:T(8,128)(2,1)S(1)}, bf16[96,768]{1,0:T(8,128)(2,1)S(1)}, u32[]{:S(2)}, u32[]{:S(2)}) collective-permute-start(bf16[96,768]{1,0:T(8,128)(2,1)S(1)} %fusion.21), channel_id=1, source_target_pairs={{0,4},{1,5},{2,6},{3,7},{4,0},{5,1},{6,2},{7,3},{8,12},{9,13},{10,... | collective-permute-start | bytes 442376 | tf_op jit(solution)/shard_map/ppermute | solution.py:1096
  404.6 36.5 %collective-permute-start.29 = (bf16[192,384]{1,0:T(8,128)(2,1)}, bf16[192,384]{1,0:T(8,128)(2,1)}, u32[]{:S(2)}, u32[]{:S(2)}) collective-permute-start(bf16[192,384]{1,0:T(8,128)(2,1)} %fusion.22), channel_id=1, source_target_pairs={{0,4},{1,5},{2,6},{3,7},{4,0},{5,1},{6,2},{7,3},{8,12},{9,13},{10,... | collective-permute-start | bytes 442376 | tf_op jit(solution)/shard_map/ppermute | solution.py:1096
  410.0 29.7 %collective-permute-start.17 = (bf16[2,2,96,768]{3,2,1,0:T(8,128)(2,1)}, bf16[2,2,96,768]{3,2,1,0:T(8,128)(2,1)}, u32[]{:S(2)}, u32[]{:S(2)}) collective-permute-start(bf16[2,2,96,768]{3,2,1,0:T(8,128)(2,1)} %get-tuple-element.239.refs_12_), channel_id=1, source_target_pairs={{0,1},{1,0},{2,3},{3,2},{4,5},{5,4},{6,7},{7,6},{8,9},{9,8},{10,11... | collective-permute-start | bytes 1769480 | tf_op jit(solution)/shard_map/ppermute | solution.py:1096
  419.6 17.6 %collective-permute-start.14 = (bf16[384,768]{1,0:T(8,128)(2,1)}, bf16[384,768]{1,0:T(8,128)(2,1)}, u32[]{:S(2)}, u32[]{:S(2)}) collective-permute-start(bf16[384,768]{1,0:T(8,128)(2,1)} %get-tuple-element.241.refs_11_), channel_id=1, source_target_pairs={{0,16},{8,24},{16,0},{24,8},{1,17},{9,25},{17,1},{25,9},{2,18},{10... | collective-permute-start | bytes 1769480 | tf_op jit(solution)/shard_map/ppermute | solution.py:1096
  441.0 9.5 %collective-permute-start.18 = (bf16[2,96,768]{2,1,0:T(8,128)(2,1)S(1)}, bf16[2,96,768]{2,1,0:T(8,128)(2,1)S(1)}, u32[]{:S(2)}, u32[]{:S(2)}) collective-permute-start(bf16[2,96,768]{2,1,0:T(8,128)(2,1)S(1)} %fusion.10), channel_id=1, source_target_pairs={{0,2},{1,3},{2,0},{3,1},{4,6},{5,7},{6,4},{7,5},{8,10},{9,11},{10,... | collective-permute-start | bytes 884744 | tf_op jit(solution)/shard_map/ppermute | solution.py:1096
  442.0 7.9 %collective-permute-start.32 = (bf16[192,384]{1,0:T(8,128)(2,1)S(1)}, bf16[192,384]{1,0:T(8,128)(2,1)S(1)}, u32[]{:S(2)}, u32[]{:S(2)}) collective-permute-start(bf16[192,384]{1,0:T(8,128)(2,1)S(1)} %fusion.16), channel_id=1, source_target_pairs={{0,16},{8,24},{16,0},{24,8},{1,17},{9,25},{17,1},{25,9},{2,18},{10... | collective-permute-start | bytes 442376 | tf_op jit(solution)/shard_map/ppermute | solution.py:1096
  445.7 34.8 %all-to-all-start.6 = ((bf16[8,384,96]{1,2,0:T(8,128)(2,1)}), bf16[8,384,96]{1,2,0:T(8,128)(2,1)S(1)}, u32[]{:S(2)}, u32[]{:S(2)}) async-start(bf16[8,384,96]{1,2,0:T(8,128)(2,1)} %bitcast.49), calls=%async_computation.6 | async-start | bytes 1179648 | tf_op jit(solution)/shard_map/all_to_all | solution.py:1104
  450.0 23.8 %collective-permute-start.33 = (bf16[384,384]{1,0:T(8,128)(2,1)S(1)}, bf16[384,384]{1,0:T(8,128)(2,1)S(1)}, u32[]{:S(2)}, u32[]{:S(2)}) collective-permute-start(bf16[384,384]{1,0:T(8,128)(2,1)S(1)} %maximum_select_fusion.1), channel_id=1, source_target_pairs={{0,8},{8,0},{16,24},{24,16},{1,9},{9,1},{17,25},{25,17},{2,10},{10... | collective-permute-start | bytes 884744 | tf_op jit(solution)/shard_map/ppermute | solution.py:1096
  450.6 19.9 %collective-permute-start.19 = (bf16[96,768]{1,0:T(8,128)(2,1)S(1)}, bf16[96,768]{1,0:T(8,128)(2,1)S(1)}, u32[]{:S(2)}, u32[]{:S(2)}) collective-permute-start(bf16[96,768]{1,0:T(8,128)(2,1)S(1)} %fusion.19), channel_id=1, source_target_pairs={{0,4},{1,5},{2,6},{3,7},{4,0},{5,1},{6,2},{7,3},{8,12},{9,13},{10,... | collective-permute-start | bytes 442376 | tf_op jit(solution)/shard_map/ppermute | solution.py:1096
  453.1 8.8 %collective-permute-start.24 = (f32[72,128]{1,0:T(8,128)S(1)}, f32[72,128]{1,0:T(8,128)S(1)}, u32[]{:S(2)}, u32[]{:S(2)}) collective-permute-start(f32[72,128]{1,0:T(8,128)S(1)} %add.244), channel_id=1, source_target_pairs={{0,2},{1,3},{2,0},{3,1},{4,6},{5,7},{6,4},{7,5},{8,10},{9,11},{10,... | collective-permute-start | bytes 110600 | tf_op jit(solution)/shard_map/ppermute | solution.py:1096
  454.6 18.0 %collective-permute-start.31 = (bf16[96,1536]{1,0:T(8,128)(2,1)S(1)}, bf16[96,1536]{1,0:T(8,128)(2,1)S(1)}, u32[]{:S(2)}, u32[]{:S(2)}) collective-permute-start(bf16[96,1536]{1,0:T(8,128)(2,1)S(1)} %maximum_select_fusion), channel_id=1, source_target_pairs={{0,8},{8,0},{16,24},{24,16},{1,9},{9,1},{17,25},{25,17},{2,10},{10... | collective-permute-start | bytes 884744 | tf_op jit(solution)/shard_map/ppermute | solution.py:1096
  (44 other events, 195.9 us)
